TPU v7x, 128 devices: a whole 4x4x4 slice. The times are simulated.
128 devices in a mesh: dp: 8 (over y, x_lo), tensor: 16 (over z, x_hi, core).
Axes of the slice: x: 4 (x_hi: 2, x_lo: 2; x = x_hi * 2 + x_lo), y: 4, z: 4, core: 2. Of those that a mesh axis runs over, the one named last changes fastest.
Arguments:
- context: bfloat16 [4096, 8192], P('dp', 'tensor'), may hold values from -6 to 6
- residual: bfloat16 [4096, 5120], P(('dp', 'tensor')), may hold values from -6 to 6
- out_proj: bfloat16 [8192, 5120], P('tensor'), may hold values from -0.0625 to 0.0625
- final_gain: bfloat16 [5120], replicated, may hold values from 0.099609375 to 1.8984375
- next_ids: int32 [2, 4096], P(None, ('dp', 'tensor')), may hold values from 0 to 76031, as said below
- embed_table: bfloat16 [76032, 5120], P('tensor', 'dp'), may hold values from -6 to 6
- head_weight: bfloat16 [2, 5120, 5120], P(None, None, 'tensor'), may hold values from -0.078125 to 0.078125
- state_grad: float32 [2, 4096, 5120], P(None, ('dp', 'tensor')), may hold values from -0.25 to 0.25
Outputs:
- states: bfloat16 [2, 4096, 5120], P(None, ('dp', 'tensor'))
- head_grad: float32 [2, 5120, 5120], P(None, 'dp', 'tensor')
Inputs may be any that keep to these rules, and one draw needn't show every extreme that they name: `next_ids`: among the ids held by all devices that share one index of tensor, each block of 4752 consecutive ids is named at most 64 times, and one such block exactly 64 times.
All inputs are finite; a program needn't handle non-finite values.
Results may differ from a plain program's by a relative error of at most 0.025.
Values may be sent and summed in bfloat16 or wider, within the bound.
No kernel may reach another device: no remote copies, remote signals or barrier semaphores. Data moves between devices by JAX's collectives and lax.ppermute only.
A program may use at most 128 MiB of HBM per device.

v0:
```python
import jax
import jax.numpy as jnp
from jax import lax
from jax.sharding import PartitionSpec as P

norm_eps = 1e-06


def rms_scale(values):
    return lax.rsqrt(jnp.mean(values * values, axis=-1, keepdims=True) + norm_eps)


def silu_slope(pre_act):
    sigmoid = jax.nn.sigmoid(pre_act)
    return sigmoid * (1.0 + pre_act * (1.0 - sigmoid))


def on_device(
    context, residual, out_proj, final_gain, next_ids, embed_table, head_weight, state_grad
):
    tensor_count = lax.axis_size("tensor")
    dp_count = lax.axis_size("dp")
    tok_rows = residual.shape[0]
    model_width = residual.shape[1]
    head_count = head_weight.shape[0]
    vocab_rows = embed_table.shape[0]
    table_cols = embed_table.shape[1]
    all_ids = lax.all_gather(next_ids, "dp", axis=1, tiled=True)
    flat_ids = all_ids.reshape(-1)
    owners = flat_ids // vocab_rows
    local_rows = flat_ids - owners * vocab_rows
    capacity = 2 * flat_ids.shape[0] // tensor_count
    onehot = (owners[:, None] == jnp.arange(tensor_count, dtype=jnp.int32)[None, :]).astype(
        jnp.int32
    )
    slot_ids = jnp.sum((jnp.cumsum(onehot, axis=0) - onehot) * onehot, axis=1)
    requests = jnp.zeros((tensor_count, capacity), jnp.int32).at[owners, slot_ids].set(local_rows)
    found_rows = jnp.take(
        embed_table,
        lax.all_to_all(requests, "tensor", split_axis=0, concat_axis=0, tiled=True),
        axis=0,
    )
    answers = lax.all_to_all(found_rows, "tensor", split_axis=0, concat_axis=0, tiled=True)
    my_rows = answers[owners, slot_ids].reshape(head_count, dp_count, tok_rows, table_cols)
    spread = lax.all_to_all(my_rows, "dp", split_axis=1, concat_axis=3, tiled=True)
    embeds = spread.reshape(head_count, tok_rows, dp_count * table_cols)
    projected = lax.psum_scatter(
        jnp.dot(context, out_proj, preferred_element_type=jnp.float32).astype(jnp.bfloat16),
        "tensor",
        scatter_dimension=0,
        tiled=True,
    ).astype(jnp.float32)
    hidden = residual.astype(jnp.float32) + projected
    current = hidden * rms_scale(hidden) * final_gain.astype(jnp.float32)
    saved_states = []
    saved_inputs = []
    saved_gathered = []
    saved_acts = []
    outputs = []
    for head_index in range(head_count):
        inputs = (current * rms_scale(current) + embeds[head_index].astype(jnp.float32)).astype(
            jnp.bfloat16
        )
        gathered = lax.all_gather(inputs, "tensor", axis=0, tiled=True)
        pre_act = jnp.dot(gathered, head_weight[head_index], preferred_element_type=jnp.float32)
        update = jax.nn.silu(pre_act).astype(jnp.bfloat16)
        returned = lax.all_to_all(update, "tensor", split_axis=0, concat_axis=1, tiled=True)
        saved_states.append(current)
        saved_inputs.append(inputs)
        saved_gathered.append(gathered)
        saved_acts.append(pre_act)
        current = current + returned.astype(jnp.float32)
        outputs.append(current.astype(jnp.bfloat16))
    gradient = jnp.zeros((tok_rows, model_width), jnp.float32)
    head_grads = [None] * head_count
    for head_index in reversed(range(head_count)):
        gradient = gradient + state_grad[head_index]
        down_cols = lax.all_to_all(
            gradient.astype(jnp.bfloat16), "tensor", split_axis=1, concat_axis=0, tiled=True
        )
        d_act = (down_cols.astype(jnp.float32) * silu_slope(saved_acts[head_index])).astype(
            jnp.bfloat16
        )
        rows_used = saved_gathered[head_index]

        def grad_rows(row_start, row_count, inputs_used=rows_used, slope_act=d_act):
            return lax.dot_general(
                inputs_used, slope_act, (((0,), (0,)), ((), ())), preferred_element_type=jnp.float32
            )

        head_grads[head_index] = lax.psum_scatter(
            grad_rows(jnp.int32(0), lax.axis_size("dp") * (model_width // dp_count)).astype(
                jnp.bfloat16
            ),
            "dp",
            scatter_dimension=0,
            tiled=True,
        ).astype(jnp.float32)
        if head_index > 0:

            def input_rows(
                row_start, row_count, slope_act=d_act, weight_cols=head_weight[head_index]
            ):
                return lax.dot_general(
                    slope_act,
                    weight_cols,
                    (((1,), (1,)), ((), ())),
                    preferred_element_type=jnp.float32,
                )

            d_input = lax.psum_scatter(
                input_rows(jnp.int32(0), lax.axis_size("tensor") * tok_rows).astype(jnp.bfloat16),
                "tensor",
                scatter_dimension=0,
                tiled=True,
            ).astype(jnp.float32)
            previous = saved_states[head_index]
            scale_prev = rms_scale(previous)
            gradient = (
                gradient
                + scale_prev * d_input
                - previous * scale_prev**3 * jnp.mean(d_input * previous, axis=-1, keepdims=True)
            )
    weight_out = jnp.stack(head_grads)
    return (jnp.stack(outputs), weight_out)


def solution(mesh):
    in_specs = (
        P("dp", "tensor"),
        P(("dp", "tensor"), None),
        P("tensor", None),
        P(),
        P(None, ("dp", "tensor")),
        P("tensor", "dp"),
        P(None, None, "tensor"),
        P(None, ("dp", "tensor"), None),
    )
    out_specs = (P(None, ("dp", "tensor"), None), P(None, "dp", "tensor"))
    return jax.shard_map(
        on_device, mesh=mesh, in_specs=in_specs, out_specs=out_specs, check_vma=False
    )
```

profile of v0, /device:TPU:4, one launch (start us, length us, event | category | flops | bytes accessed | tf_op | source)
XLA Modules:
  0.0 558.7 jit_solution(12604801721044250412)
XLA Ops:
  8.2 7.1 %convolution_convert_fusion.1 = bf16[512,5120]{1,0:T(8,128)(2,1)} fusion(bf16[512,512]{1,0:T(8,128)(2,1)S(1)} %copy-done, bf16[512,5120]{1,0:T(8,128)(2,1)} %param.10), kind=kOutput, calls=%fused_computation.4 | convolution fusion | flops 2686976000 | bytes 11010048 | tf_op jit(solution)/shard_map/dot_general | solution.py:48
  16.0 18.7 %all-gather = s32[8,32,2]{1,2,0:T(2,128)S(1)} all-gather(s32[1,32,2]{1,2,0:T(2,128)S(1)} %bitcast.138), channel_id=1, replica_groups=mesh['dp'=8,'tensor'=16] {'dp'}, dimensions={0}, use_global_device_ids=true | all-gather | bytes 2304 | tf_op jit(solution)/shard_map/all_gather | solution.py:28
  36.5 25.3 %scatter_fusion = s32[16,64]{1,0:T(8,128)S(1)} fusion(s32[16,64]{1,0:T(8,128)S(1)} %broadcast_in_dim.14, s32[512]{0:T(512)S(1)} %bitcast.118, s32[512]{0:T(512)S(1)} %get-tuple-element.12), kind=kCustom, calls=%fused_computation.2 | custom fusion | bytes 10240 | tf_op jit(solution)/shard_map/scatter | solution.py:37
  61.8 13.0 %all_to_all.84 = s32[16,1,64]{2,1,0:T(1,128)S(1)} all-to-all(s32[16,1,64]{2,1,0:T(1,128)S(1)} %bitcast.116), channel_id=1, replica_groups=mesh['dp'=8,'tensor'=16] {'tensor'}, dimensions={0} | all-to-all | bytes 8192 | tf_op jit(solution)/shard_map/all_to_all | solution.py:40
  74.9 7.8 %gather_fusion = bf16[1024,640]{1,0:T(8,128)(2,1)S(1)} fusion(bf16[4752,640]{1,0:T(8,128)(2,1)} %param.13, s32[1024]{0:T(1024)S(1)} %broadcast_clamp_fusion), kind=kCustom, calls=%fused_computation | custom fusion | bytes 2625536 | tf_op jit(solution)/shard_map/jit(_take)/gather | solution.py:38
  83.0 26.6 %all_to_all.85 = bf16[16,64,640]{2,1,0:T(8,128)(2,1)S(1)} all-to-all(bf16[16,64,640]{2,1,0:T(8,128)(2,1)S(1)} %broadcast_select_fusion), channel_id=1, replica_groups=mesh['dp'=8,'tensor'=16] {'tensor'}, dimensions={0} | all-to-all | bytes 2621440 | tf_op jit(solution)/shard_map/all_to_all | solution.py:43
  118.4 12.0 %all-to-all-done.2 = bf16[2,8,32,640]{3,2,0,1:T(8,128)(2,1)S(1)} async-done(((bf16[2,8,32,640]{3,2,0,1:T(8,128)(2,1)}), bf16[2,8,32,640]{3,2,0,1:T(8,128)(2,1)S(1)}, u32[]{:S(2)}, u32[]{:S(2)}) %all-to-all-start.2) | async-done | bytes 655392 | tf_op jit(solution)/shard_map/all_to_all | solution.py:45
  135.0 54.8 %all-gather.4.cloned.1.call-done = bf16[512,5120]{1,0:T(8,128)(2,1)} async-done(((bf16[32,5120]{1,0:T(8,128)(2,1)}), bf16[512,5120]{1,0:T(8,128)(2,1)}) %all-gather.4.cloned.1.call-update) | async-done | bytes 5242896 | tf_op jit(solution)/shard_map/all_gather | solution.py:64
  189.8 6.2 %multiply_convert_fusion.3 = (bf16[512,320]{0,1:T(8,128)(2,1)S(1)}, f32[512,320]{0,1:T(8,128)}) fusion(bf16[512,5120]{1,0:T(8,128)(2,1)} %all-gather.4.cloned.1.call-done, bf16[2,5120,320]{1,2,0:T(8,128)(2,1)} %param.14), kind=kOutput, calls=%fused_computation.34 | convolution fusion | flops 1678540800 | bytes 9502720 | tf_op jit(solution)/shard_map/dot_general | solution.py:65
  197.0 6.3 %all-to-all-start.3 = ((bf16[16,32,320]{2,1,0:T(8,128)(2,1)}), bf16[16,32,320]{2,1,0:T(8,128)(2,1)S(1)}, u32[]{:S(2)}, u32[]{:S(2)}) async-start(bf16[16,32,320]{2,1,0:T(8,128)(2,1)} %bitcast.16), calls=%async_computation.4 | async-start | bytes 786432 | tf_op jit(solution)/shard_map/all_to_all | solution.py:67
  204.2 7.4 %all-to-all-done.3 = bf16[16,32,320]{2,1,0:T(8,128)(2,1)S(1)} async-done(((bf16[16,32,320]{2,1,0:T(8,128)(2,1)}), bf16[16,32,320]{2,1,0:T(8,128)(2,1)S(1)}, u32[]{:S(2)}, u32[]{:S(2)}) %all-to-all-start.3) | async-done | bytes 327712 | tf_op jit(solution)/shard_map/all_to_all | solution.py:67
  216.4 14.4 %all_to_all.86 = bf16[32,16,320]{2,0,1:T(8,128)(2,1)S(1)} all-to-all(bf16[32,16,320]{2,0,1:T(8,128)(2,1)S(1)} %copy.36), channel_id=1, replica_groups=mesh['dp'=8,'tensor'=16] {'tensor'}, dimensions={1} | all-to-all | bytes 655360 | tf_op jit(solution)/shard_map/all_to_all | solution.py:78
  231.2 41.4 %all-gather.6.cloned.1.call-done = bf16[512,5120]{1,0:T(8,128)(2,1)} async-done(((bf16[32,5120]{1,0:T(8,128)(2,1)}), bf16[512,5120]{1,0:T(8,128)(2,1)}) %all-gather.6.cloned.1.call-update) | async-done | bytes 5242896 | tf_op jit(solution)/shard_map/all_gather | solution.py:64
  272.6 5.6 %multiply_convert_fusion.1 = (bf16[512,320]{0,1:T(8,128)(2,1)S(1)}, bf16[512,320]{0,1:T(8,128)(2,1)S(1)}) fusion(f32[512,320]{0,1:T(8,128)S(1)} %copy.37, bf16[512,5120]{1,0:T(8,128)(2,1)} %all-gather.6.cloned.1.call-done, bf16[2,5120,320]{1,2,0:T(8,128)(2,1)} %param.14), kind=kOutput, calls=%fused_computation.28 | convolution fusion | flops 1679523840 | bytes 9830400 | tf_op jit(solution)/shard_map/dot_general | solution.py:65
  278.2 6.6 %convolution_convert_fusion = bf16[512,5120]{1,0:T(8,128)(2,1)} fusion(bf16[512,320]{0,1:T(8,128)(2,1)S(1)} %get-tuple-element.8, bf16[2,5120,320]{1,2,0:T(8,128)(2,1)} %param.14), kind=kOutput, calls=%fused_computation.3 | convolution fusion | flops 1680343040 | bytes 8847360 | tf_op jit(solution)/shard_map/dot_general | solution.py:104
  284.9 6.1 %convolution_convert_fusion.2 = bf16[5120,320]{0,1:T(8,128)(2,1)} fusion(bf16[512,320]{0,1:T(8,128)(2,1)S(1)} %get-tuple-element.8, bf16[512,5120]{1,0:T(8,128)(2,1)} %all-gather.6.cloned.1.call-done), kind=kOutput, calls=%fused_computation.5 | convolution fusion | flops 1679360000 | bytes 8847360 | tf_op jit(solution)/shard_map/dot_general | solution.py:87
  290.9 6.0 %copy.42 = bf16[5120,320]{1,0:T(8,128)(2,1)} copy(bf16[5120,320]{0,1:T(8,128)(2,1)} %convolution_convert_fusion.2) | data formatting | bytes 6553600
  297.3 13.9 %all_to_all.87 = bf16[16,32,320]{2,1,0:T(8,128)(2,1)S(1)} all-to-all(bf16[16,32,320]{2,1,0:T(8,128)(2,1)S(1)} %bitcast.130), channel_id=1, replica_groups=mesh['dp'=8,'tensor'=16] {'tensor'}, dimensions={0} | all-to-all | bytes 655360 | tf_op jit(solution)/shard_map/all_to_all | solution.py:67
  311.9 56.7 %reduce-scatter.11.cloned.1.call-done = bf16[32,5120]{1,0:T(8,128)(2,1)} async-done(((bf16[512,5120]{1,0:T(8,128)(2,1)}), bf16[32,5120]{1,0:T(8,128)(2,1)}) %reduce-scatter.11.cloned.1.call-update) | async-done | bytes 327696 | tf_op jit(solution)/shard_map/reduce_scatter | solution.py:111
  371.8 14.3 %all_to_all.88 = bf16[32,16,320]{2,0,1:T(8,128)(2,1)S(1)} all-to-all(bf16[32,16,320]{2,0,1:T(8,128)(2,1)S(1)} %copy.38), channel_id=1, replica_groups=mesh['dp'=8,'tensor'=16] {'tensor'}, dimensions={1} | all-to-all | bytes 655360 | tf_op jit(solution)/shard_map/all_to_all | solution.py:78
  386.4 6.5 %convolution_convert_fusion.3 = bf16[5120,320]{0,1:T(8,128)(2,1)} fusion(bf16[512,5120]{1,0:T(8,128)(2,1)} %all-gather.4.cloned.1.call-done, f32[512,320]{0,1:T(8,128)S(1)} %copy.39, f32[512,320]{0,1:T(8,128)} %get-tuple-element.17), kind=kOutput, calls=%fused_computation.6 | convolution fusion | flops 1680834560 | bytes 9830400 | tf_op jit(solution)/shard_map/dot_general | solution.py:87
  392.9 6.0 %copy.40 = bf16[5120,320]{1,0:T(8,128)(2,1)} copy(bf16[5120,320]{0,1:T(8,128)(2,1)} %convolution_convert_fusion.3) | data formatting | bytes 6553600
  398.9 61.8 %reduce-scatter.15.cloned.1.call-done = bf16[640,320]{1,0:T(8,128)(2,1)} async-done(((bf16[5120,320]{1,0:T(8,128)(2,1)}), bf16[640,320]{1,0:T(8,128)(2,1)}) %reduce-scatter.15.cloned.1.call-update) | async-done | bytes 409616
  462.8 86.4 %reduce-scatter.13.cloned.1.call-done = bf16[640,320]{1,0:T(8,128)(2,1)} async-done(((bf16[5120,320]{1,0:T(8,128)(2,1)}), bf16[640,320]{1,0:T(8,128)(2,1)}) %reduce-scatter.13.cloned.1.call-update) | async-done | bytes 409616
  (91 shorter events, 33.2 us)
Async XLA Ops:
  7.2 1.1 copy-start
  7.2 123.4 %reduce-scatter.9.cloned.1.call-start = ((), (), s32[]{:S(2)}) async-start(), calls=%async_computation.11 | async-start | bytes 5570560 | tf_op jit(solution)/shard_map/reduce_scatter | solution.py:47
  15.3 0.7 copy-start.5
  83.0 35.4 %copy-start.4 = (bf16[5120]{0:T(1024)(128)(2,1)S(1)}, bf16[5120]{0:T(1024)(128)(2,1)}, u32[]{:S(2)}) copy-start(bf16[5120]{0:T(1024)(128)(2,1)} %param.11) | copy-start | bytes 30724
  109.6 21.0 %copy-start.2 = (bf16[32,5120]{1,0:T(8,128)(2,1)S(1)}, bf16[32,5120]{1,0:T(8,128)(2,1)}, u32[]{:S(2)}) copy-start(bf16[32,5120]{1,0:T(8,128)(2,1)} %param.9) | copy-start | bytes 983044
  114.8 15.6 %all-to-all-start.2 = ((bf16[2,8,32,640]{3,2,0,1:T(8,128)(2,1)}), bf16[2,8,32,640]{3,2,0,1:T(8,128)(2,1)S(1)}, u32[]{:S(2)}, u32[]{:S(2)}) async-start(bf16[2,8,32,640]{3,2,0,1:T(8,128)(2,1)} %copy.29), calls=%async_computation.3 | async-start | bytes 1310720 | tf_op jit(solution)/shard_map/all_to_all | solution.py:45
  118.3 71.5 %all-gather.4.cloned.1.call-start = ((), (), s32[]{:S(2)}) async-start(), calls=%async_computation.12 | async-start | bytes 5570560 | tf_op jit(solution)/shard_map/all_gather | solution.py:64
  196.0 16.4 %copy-start.3 = (bf16[32,5120]{1,0:T(8,128)(2,1)S(1)}, bf16[32,5120]{1,0:T(8,128)(2,1)}, u32[]{:S(2)}) copy-start(bf16[32,5120]{1,0:T(8,128)(2,1)} %reduce-scatter.9.cloned.1.call-done) | copy-start | bytes 983044
  197.0 14.7 %all-to-all-start.3 = ((bf16[16,32,320]{2,1,0:T(8,128)(2,1)}), bf16[16,32,320]{2,1,0:T(8,128)(2,1)S(1)}, u32[]{:S(2)}, u32[]{:S(2)}) async-start(bf16[16,32,320]{2,1,0:T(8,128)(2,1)} %bitcast.16), calls=%async_computation.4 | async-start | bytes 786432 | tf_op jit(solution)/shard_map/all_to_all | solution.py:67
  203.3 69.3 %all-gather.6.cloned.1.call-start = ((), (), s32[]{:S(2)}) async-start(), calls=%async_computation.13 | async-start | bytes 5570560 | tf_op jit(solution)/shard_map/all_gather | solution.py:64
  214.8 153.8 %reduce-scatter.11.cloned.1.call-start = ((), (), s32[]{:S(2)}) async-start(), calls=%async_computation.14 | async-start | bytes 5570560 | tf_op jit(solution)/shard_map/reduce_scatter | solution.py:111
  284.8 175.9 %reduce-scatter.15.cloned.1.call-start = ((), (), s32[]{:S(2)}) async-start(), calls=%async_computation.16 | async-start | bytes 4423680
  297.0 252.3 %reduce-scatter.13.cloned.1.call-start = ((), (), s32[]{:S(2)}) async-start(), calls=%async_computation.15 | async-start | bytes 4423680
  392.9 158.9 %copy-start.1 = (bf16[512,512]{1,0:T(8,128)(2,1)S(1)}, bf16[512,512]{1,0:T(8,128)(2,1)}, u32[]{:S(2)}) copy-start(bf16[512,512]{1,0:T(8,128)(2,1)} %param.8) | copy-start | bytes 1572868
Sparse Core Ops, SparseCore 0:
  15.5 94.6 reduce-scatter.8
  135.1 54.6 all-gather.3
  214.9 57.6 all-gather.5
  284.9 83.6 reduce-scatter.10
  370.9 89.7 reduce-scatter.14
  463.0 86.2 reduce-scatter.12
where the time goes:
time: 561 us; the launch traced here: 559 us
  waiting for transfers between devices  321 us (57%)
  blocking collectives  101 us (18%)
  local copies, waits for them, and re-layouts  60.7 us (11%)
  matrix products  38.1 us (7%)
  between operations  14.4 us (3%)
  other arithmetic  13.7 us (2%)
  starting transfers between devices  10.1 us (2%)
    unnamed x8, waiting for transfers between devices  148 us
    all_gather x2, waiting for transfers between devices, on_device(): gathered = lax.all_gather(inputs, 'tensor', axis=0, tiled=True)  96.2 us
    reduce_scatter x1, waiting for transfers between devices, on_device(): lax.psum_scatter(input_rows(jnp.int32(0), lax.axis_size('tensor') * tok_r...  56.7 us
    all_to_all x2, blocking collectives, on_device(): lax.all_to_all(gradient.astype(jnp.bfloat16), 'tensor', split_axis=1, con...  28.7 us
    all_to_all x1, blocking collectives, on_device(): lax.all_to_all(found_rows, 'tensor', split_axis=0, concat_axis=0, tiled=T...  26.6 us
    scatter x1, local copies, waits for them, and re-layouts, on_device(): jnp.zeros((tensor_count, capacity), jnp.int32).at[owners, slot_ids]  25.3 us
    all_gather x1, blocking collectives, on_device(): all_ids = lax.all_gather(next_ids, 'dp', axis=1, tiled=True)  18.7 us
    unnamed x22, local copies, waits for them, and re-layouts  17.2 us
  transfers between devices with their start and end apart: 8, of which 7 were waited for; matrix products, arithmetic and copies ran while one was open for 13% of the time, Pallas kernels for 0%

commit v1 on v0

v1 whole, which is shorter than its diff:
```python
import jax
import jax.numpy as jnp
from jax import lax
from jax.sharding import PartitionSpec as P

norm_eps = 1e-06
bf16 = jnp.bfloat16
f32 = jnp.float32


def rms_scale(values):
    return lax.rsqrt(jnp.mean(values * values, axis=-1, keepdims=True) + norm_eps)


def silu_slope(pre_act):
    sigmoid = jax.nn.sigmoid(pre_act)
    return sigmoid * (1.0 + pre_act * (1.0 - sigmoid))


def matmul(left, right, left_dim=1, right_dim=0):
    return lax.dot_general(
        left, right, (((left_dim,), (right_dim,)), ((), ())), preferred_element_type=f32
    )


core_swap = [(index, index ^ 1) for index in range(16)]
same_core = [[2 * chip + core for chip in range(8)] for core in range(2)]
x_lo_swap = [(index, index ^ 1) for index in range(8)]


def to_sibling(values):
    return lax.ppermute(values, "tensor", core_swap)


def exchange(values, split_axis=0, concat_axis=0):
    return lax.all_to_all(
        values,
        "tensor",
        split_axis=split_axis,
        concat_axis=concat_axis,
        tiled=True,
        axis_index_groups=same_core,
    )


def y_send(values, step):
    moves = [(index, (index + 2 * step) % 8) for index in range(8)]
    return lax.ppermute(values, "dp", moves)


def gather_rows(block):
    rows, width = block.shape
    copies = jnp.broadcast_to(block[None], (8, rows, width))
    return exchange(copies).reshape(8 * rows, width)


def scatter_sum(products):
    rows, width = products.shape
    return jnp.sum(exchange(products.reshape(8, rows // 8, width)).astype(f32), axis=0)


def after(values, *earlier):
    return lax.optimization_barrier((values,) + earlier)[0]


def on_device(
    context, residual, out_proj, final_gain, next_ids, embed_table, head_weight, state_grad
):
    tensor_count = lax.axis_size("tensor")
    dp_count = lax.axis_size("dp")
    my_core = lax.axis_index("tensor") % 2
    my_dp = lax.axis_index("dp")
    my_y, my_x = my_dp // 2, my_dp % 2
    first_core = my_core == 0
    tok_rows = residual.shape[0]
    model_width = residual.shape[1]
    head_count, _, head_cols = head_weight.shape
    vocab_rows = embed_table.shape[0]
    table_cols = embed_table.shape[1]
    chip_count = tensor_count // 2

    ids_here = next_ids.reshape(1, -1)
    id_count = ids_here.shape[1]
    group_ids = dp_count * id_count
    capacity = 2 * group_ids // tensor_count
    places_all = tensor_count * capacity
    group = lax.all_to_all(
        jnp.broadcast_to(ids_here, (dp_count, id_count)), "dp", split_axis=0, concat_axis=0, tiled=True
    ).reshape(group_ids)
    owners = group // vocab_rows
    rows_in = group - owners * vocab_rows
    before = jnp.triu(jnp.ones((group_ids, group_ids), bf16), 1)
    is_owner = owners[None, :] == jnp.arange(tensor_count, dtype=jnp.int32)[:, None]
    earlier = matmul(is_owner.astype(bf16), before)
    slots = jnp.sum(jnp.where(is_owner, earlier, 0.0), axis=0).astype(jnp.int32)
    places = owners * capacity + slots
    pick = (places[:, None] == jnp.arange(places_all, dtype=jnp.int32)[None, :]).astype(bf16)
    digits = jnp.stack([rows_in // 64, rows_in % 64]).astype(bf16)
    asked = matmul(digits, pick)
    requests = (asked[0] * 64.0 + asked[1]).astype(jnp.int32).reshape(tensor_count, capacity)
    wanted = lax.all_to_all(requests, "tensor", split_axis=0, concat_axis=0, tiled=True)
    found_rows = jnp.take(embed_table, wanted, axis=0, mode="clip")
    answers = lax.all_to_all(found_rows, "tensor", split_axis=0, concat_axis=0, tiled=True)
    my_rows = matmul(pick, answers.reshape(places_all, table_cols)).astype(bf16)
    my_rows = my_rows.reshape(dp_count, head_count, tok_rows, table_cols)
    spread = lax.all_to_all(my_rows, "dp", split_axis=0, concat_axis=3, tiled=True)
    embeds = spread.reshape(head_count, tok_rows, dp_count * table_cols)

    sibling_weight = to_sibling(head_weight)
    chip_weight = jnp.where(
        first_core,
        jnp.concatenate([head_weight, sibling_weight], axis=2),
        jnp.concatenate([sibling_weight, head_weight], axis=2),
    )

    by_core = context.reshape(chip_count, 2, tok_rows, context.shape[1])
    near_rows = jnp.where(first_core, by_core[:, 0], by_core[:, 1]).reshape(chip_count * tok_rows, -1)
    far_rows = jnp.where(first_core, by_core[:, 1], by_core[:, 0]).reshape(chip_count * tok_rows, -1)
    far = to_sibling(matmul(far_rows, out_proj).astype(bf16))
    near = matmul(near_rows, out_proj).astype(bf16)
    projected = scatter_sum((near.astype(f32) + far.astype(f32)).astype(bf16))
    hidden = residual.astype(f32) + projected
    current = hidden * rms_scale(hidden) * final_gain.astype(f32)
    saved_states = []
    saved_gathered = []
    saved_acts = []
    outputs = []
    for head_index in range(head_count):
        inputs = (current * rms_scale(current) + embeds[head_index].astype(f32)).astype(bf16)
        gathered = gather_rows(inputs)
        pre_act = matmul(gathered, chip_weight[head_index])
        update = jax.nn.silu(pre_act).astype(bf16)
        returned = exchange(update, 0, 1)
        saved_states.append(current)
        saved_gathered.append(gathered)
        saved_acts.append(pre_act)
        current = current + returned.astype(f32)
        outputs.append(current.astype(bf16))

    def chip_rows(head_index, d_act):
        mine = jnp.where(first_core, d_act[:, :head_cols], d_act[:, head_cols:])
        theirs = jnp.where(first_core, d_act[:, head_cols:], d_act[:, :head_cols])
        all_d_act = jnp.concatenate([mine, to_sibling(theirs)], axis=0)
        gathered = saved_gathered[head_index]
        all_inputs = jnp.concatenate([gathered, to_sibling(gathered)], axis=0)
        return all_inputs, all_d_act

    cols = model_width // dp_count
    gradient = jnp.zeros((tok_rows, model_width), f32)
    head_grads = [None] * head_count
    for head_index in reversed(range(head_count)):
        gradient = gradient + state_grad[head_index]
        down_cols = exchange(gradient.astype(bf16), 1, 0)
        d_act = (down_cols.astype(f32) * silu_slope(saved_acts[head_index])).astype(bf16)
        all_inputs, all_d_act = chip_rows(head_index, d_act)
        if head_index > 0:
            d_input = scatter_sum(matmul(d_act, chip_weight[head_index], 1, 1).astype(bf16))
            arrived = []
            for step in range(4):
                target = (my_y + step) % 4
                piece = lax.dynamic_slice_in_dim(all_inputs, target * 2 * cols, 2 * cols, 1)
                product = matmul(piece, all_d_act, 0, 0).astype(bf16)
                arrived.append(y_send(product, step) if step else product)
            total = sum(part.astype(f32) for part in arrived)
            keep = jnp.where(my_x == 0, total[:cols], total[cols:])
            give = jnp.where(my_x == 0, total[cols:], total[:cols]).astype(bf16)
            head_grads[head_index] = keep + lax.ppermute(give, "dp", x_lo_swap).astype(f32)
            previous = saved_states[head_index]
            scale_prev = rms_scale(previous)
            gradient = (
                gradient
                + scale_prev * d_input
                - previous * scale_prev**3 * jnp.mean(d_input * previous, axis=-1, keepdims=True)
            )
        else:
            product = matmul(all_inputs, all_d_act, 0, 0).astype(bf16)
            parts = lax.all_to_all(
                product.reshape(dp_count, cols, head_cols), "dp", split_axis=0, concat_axis=0, tiled=True
            )
            head_grads[head_index] = jnp.sum(parts.astype(f32), axis=0)
    weight_out = jnp.stack(head_grads)
    return (jnp.stack(outputs), weight_out)


def solution(mesh):
    in_specs = (
        P("dp", "tensor"),
        P(("dp", "tensor"), None),
        P("tensor", None),
        P(),
        P(None, ("dp", "tensor")),
        P("tensor", "dp"),
        P(None, None, "tensor"),
        P(None, ("dp", "tensor"), None),
    )
    out_specs = (P(None, ("dp", "tensor"), None), P(None, "dp", "tensor"))
    return jax.shard_map(
        on_device, mesh=mesh, in_specs=in_specs, out_specs=out_specs, check_vma=False
    )
```

time: 561 us -> 407 us (0.73)
  waiting for transfers between devices: 321 us -> 173 us
  starting transfers between devices: 10.1 us -> 69.3 us
  blocking collectives: 101 us -> 58.5 us
  local copies, waits for them, and re-layouts: 60.7 us -> 19.1 us
  other arithmetic: 13.7 us -> 33 us
  between operations: 14.4 us -> 0.94 us
  matrix products: 38.1 us -> 49 us
    unnamed x8 -> x0, waiting for transfers between devices: 148 us -> none
    all_gather x2 -> x0, waiting for transfers between devices: 96.2 us -> none  [on_device(): gathered = lax.all_gather(inputs, 'tensor', axis=0, tiled=True)]
    all_to_all x2 -> x10, waiting for transfers between devices: 19.4 us -> 103 us  [the longest x6 78.5 us: exchange(): lax.all_to_all(values, 'tensor', split_axis=split_axis, concat_axis=conca...]
    ppermute x0 -> x10, waiting for transfers between devices: none -> 70 us  [the longest x3 59 us: y_send(): return lax.ppermute(values, 'dp', moves)]
    reduce_scatter x2 -> x0, waiting for transfers between devices: 56.7 us -> none  [the longest x1 56.7 us: on_device(): lax.psum_scatter(input_rows(jnp.int32(0), lax.axis_size('tensor') * tok_r...]
    all_to_all x2 -> x10, starting transfers between devices: 9.87 us -> 60.7 us  [the longest x6 38.3 us: exchange(): lax.all_to_all(values, 'tensor', split_axis=split_axis, concat_axis=conca...]
    scatter x1 -> x0, local copies, waits for them, and re-layouts: 25.3 us -> none  [on_device(): jnp.zeros((tensor_count, capacity), jnp.int32).at[owners, slot_ids]]
    all_to_all x4 -> x2, blocking collectives: 69.2 us -> 45.6 us  [exchange(): lax.all_to_all(values, 'tensor', split_axis=split_axis, concat_axis=conca...]
  transfers between devices with their start and end apart: 8 -> 20, of which waited for: 7 -> 12; matrix products, arithmetic and copies ran while one was open for 13% -> 21% of each run, Pallas kernels for 0% -> 0%
where the time goes in v1:
time: 407 us; the launch traced here: 403 us
  waiting for transfers between devices  173 us (43%)
  starting transfers between devices  69.3 us (17%)
  blocking collectives  58.5 us (14%)
  matrix products  49 us (12%)
  other arithmetic  33 us (8%)
  local copies, waits for them, and re-layouts  19.1 us (5%)
    all_to_all x6, waiting for transfers between devices, exchange(): lax.all_to_all(values, 'tensor', split_axis=split_axis, concat_axis=conca...  78.5 us
    ppermute x3, waiting for transfers between devices, y_send(): return lax.ppermute(values, 'dp', moves)  59 us
    dot_general x13, matrix products, matmul(): lax.dot_general(left, right, (((left_dim,), (right_dim,)), ((), ())), pre...  49 us
    all_to_all x2, blocking collectives, exchange(): lax.all_to_all(values, 'tensor', split_axis=split_axis, concat_axis=conca...  45.6 us
    all_to_all x6, starting transfers between devices, exchange(): lax.all_to_all(values, 'tensor', split_axis=split_axis, concat_axis=conca...  38.3 us
    all_to_all x1, waiting for transfers between devices, on_device(): lax.all_to_all(found_rows, 'tensor', split_axis=0, concat_axis=0, tiled=T...  18.2 us
    select_n x1, other arithmetic, on_device(): jnp.where(first_core, jnp.concatenate([head_weight, sibling_weight], axis...  15.4 us
    all_to_all x1, blocking collectives, on_device(): lax.all_to_all(requests, 'tensor', split_axis=0, concat_axis=0, tiled=True)  12.9 us
  transfers between devices with their start and end apart: 20, of which 12 were waited for; matrix products, arithmetic and copies ran while one was open for 21% of the time, Pallas kernels for 0%

profile of v1, /device:TPU:4, one launch (start us, length us, event | category | flops | bytes accessed | tf_op | source)
XLA Modules:
  0.0 402.8 jit_solution(7694095445221420520)
XLA Ops:
  8.2 5.6 %convolution_convert_fusion.2 = bf16[256,5120]{1,0:T(8,128)(2,1)} fusion(bf16[256,512]{1,0:T(8,128)(2,1)S(1)} %bitcast.128, bf16[512,5120]{1,0:T(8,128)(2,1)} %param.10), kind=kOutput, calls=%fused_computation.16 | convolution fusion | flops 1343488000 | bytes 8126464 | tf_op jit(solution)/shard_map/dot_general | solution.py:21
  16.1 12.9 %all_to_all.106 = s32[16,1,64]{2,1,0:T(1,128)S(1)} all-to-all(s32[16,1,64]{2,1,0:T(1,128)S(1)} %bitcast.131), channel_id=1, replica_groups=mesh['dp'=8,'tensor'=16] {'tensor'}, dimensions={0} | all-to-all | bytes 8192 | tf_op jit(solution)/shard_map/all_to_all | solution.py:101
  29.7 8.8 %gather_fusion = bf16[1024,640]{1,0:T(8,128)(2,1)} fusion(bf16[4752,640]{1,0:T(8,128)(2,1)} %param.13, s32[1024]{0:T(1024)S(1)} %broadcast_clamp_fusion), kind=kCustom, calls=%fused_computation | custom fusion | bytes 2625536 | tf_op jit(solution)/shard_map/jit(_take)/gather | solution.py:102
  38.5 7.1 %all-to-all-start.3 = ((bf16[16,64,640]{2,1,0:T(8,128)(2,1)}), bf16[16,64,640]{2,1,0:T(8,128)(2,1)}, u32[]{:S(2)}, u32[]{:S(2)}) async-start(bf16[16,64,640]{2,1,0:T(8,128)(2,1)} %bitcast.8), calls=%async_computation.3 | async-start | bytes 2621440 | tf_op jit(solution)/shard_map/all_to_all | solution.py:103
  45.8 18.2 %all-to-all-done.3 = bf16[16,64,640]{2,1,0:T(8,128)(2,1)} async-done(((bf16[16,64,640]{2,1,0:T(8,128)(2,1)}), bf16[16,64,640]{2,1,0:T(8,128)(2,1)}, u32[]{:S(2)}, u32[]{:S(2)}) %all-to-all-start.3) | async-done | bytes 1310752 | tf_op jit(solution)/shard_map/all_to_all | solution.py:103
  67.2 5.7 %all-to-all-start.4 = ((bf16[8,2,32,640]{3,2,1,0:T(8,128)(2,1)}), bf16[8,2,32,640]{3,2,1,0:T(8,128)(2,1)S(1)}, u32[]{:S(2)}, u32[]{:S(2)}) async-start(bf16[8,2,32,640]{3,2,1,0:T(8,128)(2,1)} %bitcast.124), calls=%async_computation.4 | async-start | bytes 1310720 | tf_op jit(solution)/shard_map/all_to_all | solution.py:106
  78.4 6.2 %all-to-all-done.4 = bf16[8,2,32,640]{3,2,1,0:T(8,128)(2,1)S(1)} async-done(((bf16[8,2,32,640]{3,2,1,0:T(8,128)(2,1)}), bf16[8,2,32,640]{3,2,1,0:T(8,128)(2,1)S(1)}, u32[]{:S(2)}, u32[]{:S(2)}) %all-to-all-start.4) | async-done | bytes 655392 | tf_op jit(solution)/shard_map/all_to_all | solution.py:106
  91.9 28.6 %all-to-all-done = bf16[8,32,5120]{2,1,0:T(8,128)(2,1)S(1)} async-done(((bf16[8,32,5120]{2,1,0:T(8,128)(2,1)}), bf16[8,32,5120]{2,1,0:T(8,128)(2,1)S(1)}, u32[]{:S(2)}, u32[]{:S(2)}) %all-to-all-start) | async-done | bytes 2621472 | tf_op jit(solution)/shard_map/all_to_all | solution.py:36
  125.3 6.2 %all-to-all-start.5 = ((bf16[8,32,5120]{2,1,0:T(8,128)(2,1)}), bf16[8,32,5120]{2,1,0:T(8,128)(2,1)S(1)}, u32[]{:S(2)}, u32[]{:S(2)}) async-start(bf16[8,32,5120]{2,1,0:T(8,128)(2,1)} %broadcast_in_dim.50), calls=%async_computation.5 | async-start | bytes 5242880 | tf_op jit(solution)/shard_map/all_to_all | solution.py:36
  131.6 15.4 %maximum_select_fusion = bf16[2,5120,640]{1,2,0:T(8,128)(2,1)} fusion(bf16[2,5120,320]{1,2,0:T(8,128)(2,1)} %collective-permute-done.1, bf16[2,5120,320]{1,2,0:T(8,128)(2,1)} %param.14, pred[]{:T(512)S(6)} %eq.42), kind=kLoop, calls=%fused_computation.1 | loop fusion | flops 58982400 | bytes 26214400 | tf_op jit(solution)/shard_map/jit(_where)/select_n | solution.py:110
  147.0 15.3 %all-to-all-done.5 = bf16[8,32,5120]{2,1,0:T(8,128)(2,1)S(1)} async-done(((bf16[8,32,5120]{2,1,0:T(8,128)(2,1)}), bf16[8,32,5120]{2,1,0:T(8,128)(2,1)S(1)}, u32[]{:S(2)}, u32[]{:S(2)}) %all-to-all-start.5) | async-done | bytes 2621472 | tf_op jit(solution)/shard_map/all_to_all | solution.py:36
  162.3 7.0 %multiply_convert_fusion.1 = (bf16[256,640]{1,0:T(8,128)(2,1)}, f32[256,640]{1,0:T(8,128)}) fusion(bf16[256,5120]{1,0:T(8,128)(2,1)S(1)} %bitcast.109, bf16[2,5120,640]{1,2,0:T(8,128)(2,1)} %maximum_select_fusion), kind=kOutput, calls=%fused_computation.69 | convolution fusion | flops 1678540800 | bytes 10158080 | tf_op jit(solution)/shard_map/dot_general | solution.py:21
  169.3 6.2 %all-to-all-start.6 = ((bf16[8,32,640]{2,1,0:T(8,128)(2,1)}), bf16[8,32,640]{2,1,0:T(8,128)(2,1)S(1)}, u32[]{:S(2)}, u32[]{:S(2)}) async-start(bf16[8,32,640]{2,1,0:T(8,128)(2,1)} %bitcast.126), calls=%async_computation.6 | async-start | bytes 655360 | tf_op jit(solution)/shard_map/all_to_all | solution.py:36
  181.9 6.6 %all-to-all-start.9 = ((bf16[32,8,640]{2,0,1:T(8,128)(2,1)}), bf16[32,8,640]{2,0,1:T(8,128)(2,1)}, u32[]{:S(2)}, u32[]{:S(2)}) async-start(bf16[32,8,640]{2,0,1:T(8,128)(2,1)} %copy.38), calls=%async_computation.9 | async-start | bytes 655360 | tf_op jit(solution)/shard_map/all_to_all | solution.py:36
  195.5 33.8 %all_to_all.107 = bf16[8,32,5120]{2,1,0:T(8,128)(2,1)S(1)} all-to-all(bf16[8,32,5120]{2,1,0:T(8,128)(2,1)S(1)} %broadcast_in_dim.51), channel_id=1, replica_groups={{0,2,4,6,8,10,12,14},{1,3,5,7,9,11,13,15},{16,18,20,22,24,26,28,30},{17..., dimensions={0} | all-to-all | bytes 5242880 | tf_op jit(solution)/shard_map/all_to_all | solution.py:36
  229.2 6.1 %fusion.26 = (bf16[256,640]{1,0:T(8,128)(2,1)}, bf16[256,640]{1,0:T(8,128)(2,1)}) fusion(bf16[32,8,640]{2,0,1:T(8,128)(2,1)} %all-to-all-done.9, bf16[256,5120]{1,0:T(8,128)(2,1)S(1)} %bitcast.98, bf16[2,5120,640]{1,2,0:T(8,128)(2,1)} %maximum_select_fusion), kind=kOutput, calls=%fused_computation.56 | convolution fusion | flops 1679687680 | bytes 10158080 | tf_op jit(solution)/shard_map/dot_general | solution.py:21
  235.3 6.6 %all-to-all-start.8 = ((bf16[8,32,640]{2,1,0:T(8,128)(2,1)}), bf16[8,32,640]{2,1,0:T(8,128)(2,1)}, u32[]{:S(2)}, u32[]{:S(2)}) async-start(bf16[8,32,640]{2,1,0:T(8,128)(2,1)} %bitcast.127), calls=%async_computation.8 | async-start | bytes 655360 | tf_op jit(solution)/shard_map/all_to_all | solution.py:36
  242.0 6.7 %convolution_convert_fusion.1 = bf16[256,5120]{1,0:T(8,128)(2,1)} fusion(bf16[256,640]{1,0:T(8,128)(2,1)} %get-tuple-element.8, bf16[2,5120,640]{1,2,0:T(8,128)(2,1)} %maximum_select_fusion), kind=kOutput, calls=%fused_computation.15 | convolution fusion | flops 1679032320 | bytes 9502720 | tf_op jit(solution)/shard_map/dot_general | solution.py:21
  248.7 7.2 %all-to-all-start.10 = ((bf16[8,32,5120]{2,1,0:T(8,128)(2,1)}), bf16[8,32,5120]{2,1,0:T(8,128)(2,1)}, u32[]{:S(2)}, u32[]{:S(2)}) async-start(bf16[8,32,5120]{2,1,0:T(8,128)(2,1)} %bitcast.112), calls=%async_computation.10 | async-start | bytes 5242880 | tf_op jit(solution)/shard_map/all_to_all | solution.py:36
  258.3 24.8 %all-to-all-done.10 = bf16[8,32,5120]{2,1,0:T(8,128)(2,1)} async-done(((bf16[8,32,5120]{2,1,0:T(8,128)(2,1)}), bf16[8,32,5120]{2,1,0:T(8,128)(2,1)}, u32[]{:S(2)}, u32[]{:S(2)}) %all-to-all-start.10) | async-done | bytes 2621472 | tf_op jit(solution)/shard_map/all_to_all | solution.py:36
  286.7 11.8 %all_to_all.108 = bf16[32,8,640]{2,0,1:T(8,128)(2,1)S(1)} all-to-all(bf16[32,8,640]{2,0,1:T(8,128)(2,1)S(1)} %bitcast.121), channel_id=1, replica_groups={{0,2,4,6,8,10,12,14},{1,3,5,7,9,11,13,15},{16,18,20,22,24,26,28,30},{17..., dimensions={1} | all-to-all | bytes 655360 | tf_op jit(solution)/shard_map/all_to_all | solution.py:36
  326.4 41.7 %collective-permute-done.6 = bf16[1280,320]{0,1:T(8,128)(2,1)} collective-permute-done((bf16[1280,320]{0,1:T(8,128)(2,1)}, bf16[1280,320]{0,1:T(8,128)(2,1)}, u32[]{:S(2)}, u32[]{:S(2)}) %collective-permute-start.6) | collective-permute-done | bytes 819232 | tf_op jit(solution)/shard_map/ppermute | solution.py:48
  368.1 17.3 %collective-permute-done.7 = bf16[1280,320]{0,1:T(8,128)(2,1)} collective-permute-done((bf16[1280,320]{0,1:T(8,128)(2,1)}, bf16[1280,320]{0,1:T(8,128)(2,1)}, u32[]{:S(2)}, u32[]{:S(2)}) %collective-permute-start.7) | collective-permute-done | bytes 819232 | tf_op jit(solution)/shard_map/ppermute | solution.py:48
  390.6 8.3 %collective-permute-done.9 = bf16[640,320]{0,1:T(8,128)(2,1)S(1)} collective-permute-done((bf16[640,320]{0,1:T(8,128)(2,1)S(1)}, bf16[640,320]{0,1:T(8,128)(2,1)S(1)}, u32[]{:S(2)}, u32[]{:S(2)}) %collective-permute-start.9) | collective-permute-done | bytes 409632 | tf_op jit(solution)/shard_map/ppermute | solution.py:167
  (116 shorter events, 87.7 us)
Async XLA Ops:
  2.0 11.8 %all-to-all-start.1 = ((s32[8,1,64]{2,1,0:T(1,128)}), s32[8,1,64]{2,1,0:T(1,128)S(1)}, u32[]{:S(2)}, u32[]{:S(2)}) async-start(s32[8,1,64]{2,1,0:T(1,128)} %broadcast_in_dim.23), calls=%async_computation.1 | async-start | bytes 8192 | tf_op jit(solution)/shard_map/all_to_all | solution.py:87
  13.8 59.1 %collective-permute-start = (bf16[256,5120]{1,0:T(8,128)(2,1)}, bf16[256,5120]{1,0:T(8,128)(2,1)S(1)}, u32[]{:S(2)}, u32[]{:S(2)}) collective-permute-start(bf16[256,5120]{1,0:T(8,128)(2,1)} %convolution_convert_fusion.2), channel_id=1, source_target_pairs={{0,1},{1,0},{2,3},{3,2},{4,5},{5,4},{6,7},{7,6},{8,9},{9,8},{10,11... | collective-permute-start | bytes 7864328 | tf_op jit(solution)/shard_map/ppermute | solution.py:32
  38.5 25.4 %all-to-all-start.3 = ((bf16[16,64,640]{2,1,0:T(8,128)(2,1)}), bf16[16,64,640]{2,1,0:T(8,128)(2,1)}, u32[]{:S(2)}, u32[]{:S(2)}) async-start(bf16[16,64,640]{2,1,0:T(8,128)(2,1)} %bitcast.8), calls=%async_computation.3 | async-start | bytes 2621440 | tf_op jit(solution)/shard_map/all_to_all | solution.py:103
  45.6 85.9 %collective-permute-start.1 = (bf16[2,5120,320]{1,2,0:T(8,128)(2,1)}, bf16[2,5120,320]{1,2,0:T(8,128)(2,1)}, u32[]{:S(2)}, u32[]{:S(2)}) collective-permute-start(bf16[2,5120,320]{1,2,0:T(8,128)(2,1)} %param.14), channel_id=1, source_target_pairs={{0,1},{1,0},{2,3},{3,2},{4,5},{5,4},{6,7},{7,6},{8,9},{9,8},{10,11... | collective-permute-start | bytes 19660808 | tf_op jit(solution)/shard_map/ppermute | solution.py:32
  67.2 17.5 %all-to-all-start.4 = ((bf16[8,2,32,640]{3,2,1,0:T(8,128)(2,1)}), bf16[8,2,32,640]{3,2,1,0:T(8,128)(2,1)S(1)}, u32[]{:S(2)}, u32[]{:S(2)}) async-start(bf16[8,2,32,640]{3,2,1,0:T(8,128)(2,1)} %bitcast.124), calls=%async_computation.4 | async-start | bytes 1310720 | tf_op jit(solution)/shard_map/all_to_all | solution.py:106
  84.7 35.8 %all-to-all-start = ((bf16[8,32,5120]{2,1,0:T(8,128)(2,1)}), bf16[8,32,5120]{2,1,0:T(8,128)(2,1)S(1)}, u32[]{:S(2)}, u32[]{:S(2)}) async-start(bf16[8,32,5120]{2,1,0:T(8,128)(2,1)} %bitcast.105), calls=%async_computation | async-start | bytes 5242880 | tf_op jit(solution)/shard_map/all_to_all | solution.py:36
  125.3 37.0 %all-to-all-start.5 = ((bf16[8,32,5120]{2,1,0:T(8,128)(2,1)}), bf16[8,32,5120]{2,1,0:T(8,128)(2,1)S(1)}, u32[]{:S(2)}, u32[]{:S(2)}) async-start(bf16[8,32,5120]{2,1,0:T(8,128)(2,1)} %broadcast_in_dim.50), calls=%async_computation.5 | async-start | bytes 5242880 | tf_op jit(solution)/shard_map/all_to_all | solution.py:36
  169.3 12.7 %all-to-all-start.6 = ((bf16[8,32,640]{2,1,0:T(8,128)(2,1)}), bf16[8,32,640]{2,1,0:T(8,128)(2,1)S(1)}, u32[]{:S(2)}, u32[]{:S(2)}) async-start(bf16[8,32,640]{2,1,0:T(8,128)(2,1)} %bitcast.126), calls=%async_computation.6 | async-start | bytes 655360 | tf_op jit(solution)/shard_map/all_to_all | solution.py:36
  181.9 13.2 %all-to-all-start.9 = ((bf16[32,8,640]{2,0,1:T(8,128)(2,1)}), bf16[32,8,640]{2,0,1:T(8,128)(2,1)}, u32[]{:S(2)}, u32[]{:S(2)}) async-start(bf16[32,8,640]{2,0,1:T(8,128)(2,1)} %copy.38), calls=%async_computation.9 | async-start | bytes 655360 | tf_op jit(solution)/shard_map/all_to_all | solution.py:36
  235.3 13.3 %all-to-all-start.8 = ((bf16[8,32,640]{2,1,0:T(8,128)(2,1)}), bf16[8,32,640]{2,1,0:T(8,128)(2,1)}, u32[]{:S(2)}, u32[]{:S(2)}) async-start(bf16[8,32,640]{2,1,0:T(8,128)(2,1)} %bitcast.127), calls=%async_computation.8 | async-start | bytes 655360 | tf_op jit(solution)/shard_map/all_to_all | solution.py:36
  248.7 34.4 %all-to-all-start.10 = ((bf16[8,32,5120]{2,1,0:T(8,128)(2,1)}), bf16[8,32,5120]{2,1,0:T(8,128)(2,1)}, u32[]{:S(2)}, u32[]{:S(2)}) async-start(bf16[8,32,5120]{2,1,0:T(8,128)(2,1)} %bitcast.112), calls=%async_computation.10 | async-start | bytes 5242880 | tf_op jit(solution)/shard_map/all_to_all | solution.py:36
  255.9 43.1 %collective-permute-start.2 = (bf16[256,5120]{1,0:T(8,128)(2,1)}, bf16[256,5120]{1,0:T(8,128)(2,1)}, u32[]{:S(2)}, u32[]{:S(2)}) collective-permute-start(bf16[256,5120]{1,0:T(8,128)(2,1)} %bitcast.110), channel_id=1, source_target_pairs={{0,1},{1,0},{2,3},{3,2},{4,5},{5,4},{6,7},{7,6},{8,9},{9,8},{10,11... | collective-permute-start | bytes 7864328 | tf_op jit(solution)/shard_map/ppermute | solution.py:32
  255.9 56.5 %collective-permute-start.4 = (bf16[256,5120]{1,0:T(8,128)(2,1)S(1)}, bf16[256,5120]{1,0:T(8,128)(2,1)}, u32[]{:S(2)}, u32[]{:S(2)}) collective-permute-start(bf16[256,5120]{1,0:T(8,128)(2,1)S(1)} %bitcast.99), channel_id=1, source_target_pairs={{0,1},{1,0},{2,3},{3,2},{4,5},{5,4},{6,7},{7,6},{8,9},{9,8},{10,11... | collective-permute-start | bytes 7864328 | tf_op jit(solution)/shard_map/ppermute | solution.py:32
  285.7 12.8 %copy-start.10 = (f32[256,640]{1,0:T(8,128)S(1)}, f32[256,640]{1,0:T(8,128)}, u32[]{:S(2)}) copy-start(f32[256,640]{1,0:T(8,128)} %get-tuple-element.21) | copy-start | bytes 1966084
  286.7 13.8 %copy-start.4 = (bf16[8,32,5120]{2,1,0:T(8,128)(2,1)S(1)}, bf16[8,32,5120]{2,1,0:T(8,128)(2,1)}, u32[]{:S(2)}) copy-start(bf16[8,32,5120]{2,1,0:T(8,128)(2,1)} %copy-done.3) | copy-start | bytes 7864324
  298.9 1.5 collective-permute-start.3
  306.1 92.9 %all-to-all-start.12 = ((bf16[8,640,320]{1,2,0:T(8,128)(2,1)}), bf16[8,640,320]{1,2,0:T(8,128)(2,1)}, u32[]{:S(2)}, u32[]{:S(2)}) async-start(bf16[8,640,320]{1,2,0:T(8,128)(2,1)} %bitcast.104), calls=%async_computation.12 | async-start | bytes 6553600 | tf_op jit(solution)/shard_map/all_to_all | solution.py:177
  310.9 1.5 collective-permute-start.5
  315.1 53.0 %collective-permute-start.6 = (bf16[1280,320]{0,1:T(8,128)(2,1)}, bf16[1280,320]{0,1:T(8,128)(2,1)}, u32[]{:S(2)}, u32[]{:S(2)}) collective-permute-start(bf16[1280,320]{0,1:T(8,128)(2,1)} %convolution_convert_fusion.6), channel_id=1, source_target_pairs={{0,32},{16,48},{32,64},{48,80},{64,96},{80,112},{96,0},{112,16},{1... | collective-permute-start | bytes 2457608 | tf_op jit(solution)/shard_map/ppermute | solution.py:48
  319.7 65.8 %collective-permute-start.7 = (bf16[1280,320]{0,1:T(8,128)(2,1)}, bf16[1280,320]{0,1:T(8,128)(2,1)}, u32[]{:S(2)}, u32[]{:S(2)}) collective-permute-start(bf16[1280,320]{0,1:T(8,128)(2,1)} %convolution_convert_fusion.5), channel_id=1, source_target_pairs={{0,64},{16,80},{32,96},{48,112},{64,0},{80,16},{96,32},{112,48},{1... | collective-permute-start | bytes 2457608 | tf_op jit(solution)/shard_map/ppermute | solution.py:48
  324.9 60.5 %collective-permute-start.8 = (bf16[1280,320]{0,1:T(8,128)(2,1)}, bf16[1280,320]{0,1:T(8,128)(2,1)}, u32[]{:S(2)}, u32[]{:S(2)}) collective-permute-start(bf16[1280,320]{0,1:T(8,128)(2,1)} %convolution_convert_fusion.4), channel_id=1, source_target_pairs={{0,96},{16,112},{32,0},{48,16},{64,32},{80,48},{96,64},{112,80},{1... | collective-permute-start | bytes 2457608 | tf_op jit(solution)/shard_map/ppermute | solution.py:48
  326.4 63.2 %copy-start.8 = (bf16[1,32,5120]{2,1,0:T(8,128)(2,1)S(1)}, bf16[1,32,5120]{2,1,0:T(8,128)(2,1)}, u32[]{:S(2)}) copy-start(bf16[1,32,5120]{2,1,0:T(8,128)(2,1)} %get-tuple-element.7) | copy-start | bytes 983044
  326.4 63.2 %copy-start.9 = (bf16[1,32,5120]{2,1,0:T(8,128)(2,1)S(1)}, bf16[1,32,5120]{2,1,0:T(8,128)(2,1)}, u32[]{:S(2)}) copy-start(bf16[1,32,5120]{2,1,0:T(8,128)(2,1)} %get-tuple-element.2) | copy-start | bytes 983044
  388.1 10.8 %collective-permute-start.9 = (bf16[640,320]{0,1:T(8,128)(2,1)S(1)}, bf16[640,320]{0,1:T(8,128)(2,1)S(1)}, u32[]{:S(2)}, u32[]{:S(2)}) collective-permute-start(bf16[640,320]{0,1:T(8,128)(2,1)S(1)} %select_convert_fusion), channel_id=1, source_target_pairs={{0,16},{16,0},{32,48},{48,32},{64,80},{80,64},{96,112},{112,96},{1... | collective-permute-start | bytes 1228808 | tf_op jit(solution)/shard_map/ppermute | solution.py:167
  (9 other events, 47.9 us)

commit v2 on v1

v2 whole, which is shorter than its diff:
```python
import jax
import jax.numpy as jnp
from jax import lax
from jax.experimental import pallas as pl
from jax.experimental.pallas import tpu as pltpu
from jax.sharding import PartitionSpec as P

norm_eps = 1e-06
bf16 = jnp.bfloat16
f32 = jnp.float32
chips = 8
vmem_limit = 16 * 1024 * 1024

steps = [(dz, dx) for dz in range(4) for dx in range(2)]
core_swap = [(index, index ^ 1) for index in range(16)]
same_core = [[2 * chip + core for chip in range(chips)] for core in range(2)]


def chip_moves(axis, dz, dx):
    moves = []
    cores = 2 if axis == "tensor" else 1
    for chip in range(chips):
        target = ((chip // 2 + dz) % 4) * 2 + ((chip % 2) ^ dx)
        for core in range(cores):
            moves.append((chip * cores + core, target * cores + core))
    return moves


def send(values, axis, dz, dx):
    return lax.ppermute(values, axis, chip_moves(axis, dz, dx))


def to_sibling(values):
    return lax.ppermute(values, "tensor", core_swap)


def exchange(values):
    return lax.all_to_all(
        values, "tensor", split_axis=0, concat_axis=0, tiled=True, axis_index_groups=same_core
    )


def gather_chips(block):
    parts = {(0, 0): block}
    parts[(0, 1)] = send(block, "tensor", 0, 1)
    parts[(2, 0)] = send(block, "tensor", 2, 0)
    parts[(1, 0)] = send(block, "tensor", 3, 0)
    parts[(3, 0)] = send(block, "tensor", 1, 0)
    parts[(1, 1)] = send(parts[(0, 1)], "tensor", 3, 0)
    parts[(3, 1)] = send(parts[(0, 1)], "tensor", 1, 0)
    parts[(2, 1)] = send(parts[(2, 0)], "tensor", 0, 1)
    return [parts[step] for step in steps]


def add(*parts):
    total = parts[0].astype(f32)
    for part in parts[1:]:
        total = total + part.astype(f32)
    return total


def scatter_chips(blocks, axis):
    parts = dict(zip(steps, blocks))
    across = send(parts[(2, 1)], axis, 0, 1)
    up = send(parts[(1, 1)], axis, 1, 0)
    down = send(parts[(3, 1)], axis, 3, 0)
    near_up = send(parts[(1, 0)], axis, 1, 0)
    near_down = send(parts[(3, 0)], axis, 3, 0)
    far = send(add(parts[(2, 0)], across).astype(bf16), axis, 2, 0)
    side = send(add(parts[(0, 1)], up, down).astype(bf16), axis, 0, 1)
    return [parts[(0, 0)], near_up, near_down, far, side]


def matmul(left, right, left_dim=1, right_dim=0):
    return lax.dot_general(
        left, right, (((left_dim,), (right_dim,)), ((), ())), preferred_element_type=f32
    )


def call(body, grid, in_specs, out_specs, out_shape, scratch=(), flops=0, moved=0):
    return pl.pallas_call(
        body,
        grid_spec=pltpu.PrefetchScalarGridSpec(
            num_scalar_prefetch=1,
            grid=grid,
            in_specs=in_specs,
            out_specs=out_specs,
            scratch_shapes=list(scratch),
        ),
        out_shape=out_shape,
        compiler_params=pltpu.CompilerParams(vmem_limit_bytes=vmem_limit),
        cost_estimate=pl.CostEstimate(flops=flops, bytes_accessed=moved, transcendentals=0),
    )


def whole():
    return pl.BlockSpec(memory_space=pltpu.VMEM)


def struct(shape, dtype):
    return jax.ShapeDtypeStruct(shape, dtype)


def block_rows(index, rows):
    return pl.ds(pl.multiple_of(index * rows, rows), rows)


def project(place, context, out_proj, rows, far_side, arrived=None):
    depth, width = out_proj.shape
    tile = 1024
    half = chips * rows

    def left(place_ref, context_ref):
        core = place_ref[chips]
        core = 1 - core if far_side else core
        return jnp.concatenate(
            [context_ref[block_rows(place_ref[i] * 2 + core, rows), :] for i in range(chips)], axis=0
        )

    def far_body(place_ref, context_ref, weight_ref, out_ref):
        part = block_rows(pl.program_id(0), tile)
        out_ref[:, part] = matmul(left(place_ref, context_ref), weight_ref[...]).astype(bf16)

    def near_body(place_ref, context_ref, weight_ref, arrived_ref, *out_refs):
        part = block_rows(pl.program_id(0), tile)
        total = matmul(left(place_ref, context_ref), weight_ref[...])
        total = (total + arrived_ref[:, part].astype(f32)).astype(bf16)
        for i in range(chips):
            out_refs[i][:, part] = total[i * rows : (i + 1) * rows]

    in_specs = [whole(), pl.BlockSpec((depth, tile), lambda i, place: (0, i))]
    costs = dict(flops=2 * half * depth * width, moved=2 * depth * width + 4 * half * width)
    if far_side:
        return call(
            far_body, (width // tile,), in_specs, whole(), struct((half, width), bf16), **costs
        )(place, context, out_proj)
    return call(
        near_body,
        (width // tile,),
        in_specs + [whole()],
        [whole()] * chips,
        [struct((rows, width), bf16)] * chips,
        **costs,
    )(place, context, out_proj, arrived)


def forward(place, pieces, weight, sibling, head):
    rows, width = pieces[0].shape
    cols = weight.shape[1]
    tile = 1024
    half = chips * rows
    count = width // tile

    def body(place_ref, *refs):
        piece_refs, (mine_ref, sibling_ref), (update_ref, slope_ref, gathered_ref) = (
            refs[:chips],
            refs[chips : chips + 2],
            refs[chips + 2 : chips + 5],
        )
        mine_acc, sibling_acc = refs[chips + 5 :]
        step = pl.program_id(0)
        part = block_rows(step, tile)
        for i in range(chips):
            gathered_ref[block_rows(place_ref[i], rows), part] = piece_refs[i][:, part]
        left = gathered_ref[:, part]
        mine = matmul(left, mine_ref[0], 1, 1)
        theirs = matmul(left, sibling_ref[0], 1, 1)

        @pl.when(step == 0)
        def _():
            mine_acc[...] = mine
            sibling_acc[...] = theirs

        @pl.when(step > 0)
        def _():
            mine_acc[...] += mine
            sibling_acc[...] += theirs

        @pl.when(step == count - 1)
        def _():
            def results(pre_act):
                sigmoid = 1.0 / (1.0 + jnp.exp(-pre_act))
                return pre_act * sigmoid, sigmoid * (1.0 + pre_act * (1.0 - sigmoid))

            first = place_ref[chips] == 0
            update_a, slope_a = results(mine_acc[...])
            update_b, slope_b = results(sibling_acc[...])
            update_ref[...] = jnp.concatenate(
                [jnp.where(first, update_a, update_b), jnp.where(first, update_b, update_a)], axis=1
            ).astype(bf16)
            slope_ref[...] = jnp.concatenate(
                [jnp.where(first, slope_a, slope_b), jnp.where(first, slope_b, slope_a)], axis=1
            )

    weight_spec = pl.BlockSpec((1, cols, tile), lambda i, place: (head, 0, i))
    return call(
        body,
        (count,),
        [whole()] * chips + [weight_spec] * 2,
        [whole()] * 3,
        [
            struct((half, 2 * cols), bf16),
            struct((half, 2 * cols), f32),
            struct((half, width), bf16),
        ],
        [pltpu.VMEM((half, cols), f32)] * 2,
        flops=4 * half * width * cols,
        moved=4 * width * cols + 4 * half * width,
    )(place, *pieces, weight, sibling)


def slope_product(place, down, slope):
    half, both = slope.shape
    cols = both // 2

    def body(place_ref, down_ref, slope_ref, mine_ref, theirs_ref):
        d_act = down_ref[...].astype(f32) * slope_ref[...]
        first = place_ref[chips] == 0
        low, high = d_act[:, :cols], d_act[:, cols:]
        mine_ref[...] = jnp.where(first, low, high).astype(bf16)
        theirs_ref[...] = jnp.where(first, high, low).astype(bf16)

    return call(
        body,
        (1,),
        [whole()] * 2,
        [whole()] * 2,
        [struct((half, cols), bf16)] * 2,
        moved=half * both * 8,
    )(place, down.reshape(half, both), slope)


def backward(place, mine, theirs, weight, sibling, head):
    half, cols = mine.shape
    width = weight.shape[2]
    rows = half // chips
    tile = 1024

    def body(place_ref, mine_ref, theirs_ref, weight_ref, sibling_ref, *out_refs):
        def ordered(ref):
            return jnp.concatenate([ref[block_rows(place_ref[i], rows), :] for i in range(chips)], axis=0)

        part = block_rows(pl.program_id(0), tile)
        total = matmul(ordered(mine_ref), weight_ref[0])
        total = total + matmul(ordered(theirs_ref), sibling_ref[0])
        total = total.astype(bf16)
        for i in range(chips):
            out_refs[i][:, part] = total[i * rows : (i + 1) * rows]

    weight_spec = pl.BlockSpec((1, cols, tile), lambda i, place: (head, 0, i))
    return call(
        body,
        (width // tile,),
        [whole()] * 2 + [weight_spec] * 2,
        [whole()] * chips,
        [struct((rows, width), bf16)] * chips,
        flops=4 * half * width * cols,
        moved=4 * width * cols + 2 * half * width,
    )(place, mine, theirs, weight, sibling)


def grad_block(target, inputs, sibling_inputs, mine, sibling_mine, cols, dtype):
    half = inputs.shape[0]
    out_rows = mine.shape[1]

    def body(place_ref, inputs_ref, sibling_ref, mine_ref, sibling_mine_ref, out_ref):
        part = block_rows(place_ref[0], cols)
        total = matmul(mine_ref[...], inputs_ref[:, part], 0, 0)
        total = total + matmul(sibling_mine_ref[...], sibling_ref[:, part], 0, 0)
        out_ref[...] = total.astype(dtype)

    return call(
        body,
        (1,),
        [whole()] * 4,
        whole(),
        struct((out_rows, cols), dtype),
        flops=4 * half * cols * out_rows,
        moved=4 * half * (cols + out_rows) + 4 * cols * out_rows,
    )(target.reshape(1), inputs, sibling_inputs, mine, sibling_mine)


def mean_last(values):
    return jnp.mean(values, axis=-1, keepdims=True)


def first_state(place, residual, terms, gain, embeds):
    rows, width = residual.shape
    cols = width // chips

    def body(place_ref, residual_ref, *refs):
        term_refs, gain_ref, embeds_ref, state_ref, inputs_ref = refs[:-4], *refs[-4:]
        hidden = residual_ref[...].astype(f32) + add(*[ref[...] for ref in term_refs])
        state = hidden * lax.rsqrt(mean_last(hidden * hidden) + norm_eps) * gain_ref[...].astype(f32)
        state_ref[...] = state
        scale = lax.rsqrt(mean_last(state * state) + norm_eps)
        for i in range(chips):
            part = slice(i * cols, (i + 1) * cols)
            inputs_ref[:, part] = (state[:, part] * scale + embeds_ref[i].astype(f32)).astype(bf16)

    return call(
        body,
        (1,),
        [whole()] * (3 + len(terms)),
        [whole()] * 2,
        [struct((rows, width), f32), struct((rows, width), bf16)],
        moved=rows * width * 20,
    )(place, residual, *terms, gain.reshape(1, width), embeds)


def next_state(place, state, returned, embeds):
    rows, width = state.shape
    cols = width // chips

    def body(place_ref, state_ref, returned_ref, embeds_ref, state_out, inputs_ref, rounded_ref):
        returned_all = jnp.concatenate([returned_ref[i] for i in range(chips)], axis=1)
        new_state = state_ref[...] + returned_all.astype(f32)
        state_out[...] = new_state
        rounded_ref[...] = new_state.astype(bf16)
        scale = lax.rsqrt(mean_last(new_state * new_state) + norm_eps)
        for i in range(chips):
            part = slice(i * cols, (i + 1) * cols)
            inputs_ref[:, part] = (new_state[:, part] * scale + embeds_ref[i].astype(f32)).astype(bf16)

    return call(
        body,
        (1,),
        [whole()] * 3,
        [whole()] * 3,
        [struct((rows, width), f32), struct((rows, width), bf16), struct((rows, width), bf16)],
        moved=rows * width * 16,
    )(place, state, returned, embeds)


def carry_gradient(place, state_grad, state, terms):
    rows, width = state.shape
    cols = width // chips

    def body(place_ref, upper_ref, lower_ref, state_ref, *refs):
        term_refs, out_ref = refs[:-1], refs[-1]
        previous = state_ref[...]
        d_input = add(*[ref[...] for ref in term_refs])
        scale = lax.rsqrt(mean_last(previous * previous) + norm_eps)
        shared = mean_last(d_input * previous)
        total = upper_ref[0] + scale * d_input - previous * (scale * scale * scale * shared) + lower_ref[0]
        total = total.astype(bf16)
        for i in range(chips):
            out_ref[i] = total[:, i * cols : (i + 1) * cols]

    return call(
        body,
        (1,),
        [
            pl.BlockSpec((1, rows, width), lambda i, place: (1, 0, 0)),
            pl.BlockSpec((1, rows, width), lambda i, place: (0, 0, 0)),
        ]
        + [whole()] * (1 + len(terms)),
        whole(),
        struct((chips, rows, cols), bf16),
        moved=rows * width * 24,
    )(place, state_grad, state_grad, state, *terms)


def after(values, *earlier):
    return lax.optimization_barrier((values,) + earlier)[0]


def on_device(
    context, residual, out_proj, final_gain, next_ids, embed_table, head_weight, state_grad
):
    tensor_count = lax.axis_size("tensor")
    dp_count = lax.axis_size("dp")
    my_tensor = lax.axis_index("tensor")
    my_core = my_tensor % 2
    my_z, my_x_hi = my_tensor // 4, (my_tensor // 2) % 2
    my_dp = lax.axis_index("dp")
    my_y, my_x_lo = my_dp // 2, my_dp % 2
    tok_rows, model_width = residual.shape
    head_count, _, head_cols = head_weight.shape
    weight = jnp.swapaxes(head_weight, 1, 2)
    vocab_rows, table_cols = embed_table.shape
    place = jnp.stack([((my_z + dz) % 4) * 2 + (my_x_hi ^ dx) for dz, dx in steps] + [my_core])
    place = place.astype(jnp.int32)

    ids_here = next_ids.reshape(1, -1)
    id_count = ids_here.shape[1]
    group_ids = dp_count * id_count
    capacity = 2 * group_ids // tensor_count
    places_all = tensor_count * capacity
    group = lax.all_to_all(
        jnp.broadcast_to(ids_here, (dp_count, id_count)), "dp", split_axis=0, concat_axis=0, tiled=True
    )
    group = group.reshape(dp_count, head_count, tok_rows).transpose(1, 0, 2).reshape(group_ids)
    owners = group // vocab_rows
    rows_in = group - owners * vocab_rows
    before = jnp.triu(jnp.ones((group_ids, group_ids), bf16), 1)
    is_owner = owners[None, :] == jnp.arange(tensor_count, dtype=jnp.int32)[:, None]
    earlier = matmul(is_owner.astype(bf16), before)
    slots = jnp.sum(jnp.where(is_owner, earlier, 0.0), axis=0).astype(jnp.int32)
    places = owners * capacity + slots
    pick = (places[:, None] == jnp.arange(places_all, dtype=jnp.int32)[None, :]).astype(bf16)
    digits = jnp.stack([rows_in // 64, rows_in % 64]).astype(bf16)
    asked = matmul(digits, pick)
    requests = (asked[0] * 64.0 + asked[1]).astype(jnp.int32).reshape(tensor_count, capacity)

    arrived = to_sibling(project(place, context, out_proj, tok_rows, True))
    blocks = project(place, context, out_proj, tok_rows, False, arrived)
    requests, blocks = lax.optimization_barrier((requests, blocks))
    terms = scatter_chips(blocks, "tensor")

    wanted = lax.all_to_all(requests, "tensor", split_axis=0, concat_axis=0, tiled=True)
    found_rows = jnp.take(embed_table, wanted, axis=0, mode="clip")
    answers = lax.all_to_all(found_rows, "tensor", split_axis=0, concat_axis=0, tiled=True)
    answers = answers.reshape(places_all, table_cols)
    head_ids = dp_count * tok_rows

    def my_embeds(head):
        rows = matmul(pick[head * head_ids : (head + 1) * head_ids], answers).astype(bf16)
        rows = rows.reshape(dp_count, tok_rows, table_cols)
        return lax.all_to_all(rows, "dp", split_axis=0, concat_axis=0, tiled=True)

    embeds_0 = my_embeds(0)
    sibling_weight = to_sibling(weight)

    state_0, inputs_0 = first_state(place, residual, terms, final_gain, embeds_0)
    pieces_0 = gather_chips(inputs_0)
    answers = after(answers, inputs_0)
    embeds_1 = my_embeds(1)
    update_0, slope_0, gathered_0 = forward(place, pieces_0, weight, sibling_weight, 0)
    returned_0 = exchange(update_0.reshape(chips, tok_rows, 2 * head_cols))
    state_1, inputs_1, rounded_0 = next_state(place, state_0, returned_0, embeds_1)

    pieces_1 = gather_chips(inputs_1)
    upper = state_grad[1].astype(bf16).reshape(tok_rows, chips, 2 * head_cols).transpose(1, 0, 2)
    down_1 = exchange(after(upper, inputs_0))
    update_1, slope_1, gathered_1 = forward(place, pieces_1, weight, sibling_weight, 1)
    mine_1, theirs_1 = slope_product(place, down_1, slope_1)
    d_blocks = backward(place, mine_1, theirs_1, weight, sibling_weight, 1)
    d_terms = scatter_chips(d_blocks, "tensor")

    cols = model_width // dp_count
    sibling_gathered_1 = to_sibling(gathered_1)
    sibling_theirs_1 = to_sibling(theirs_1)
    products = []
    for dy in (2, 1, 3, 0):
        target = ((my_y + dy) % 4).astype(jnp.int32)
        products.append(
            grad_block(target, gathered_1, sibling_gathered_1, mine_1, sibling_theirs_1, 2 * cols, bf16)
        )
    tied = lax.optimization_barrier((d_terms[3], *products))
    d_terms[3], products = tied[0], tied[1:]
    y_terms = [send(part, "dp", dy, 0) for dy, part in zip((2, 1, 3), products)] + [products[3]]
    y_total = add(*y_terms)
    keep = jnp.where(my_x_lo == 0, y_total[:, :cols], y_total[:, cols:])
    give = jnp.where(my_x_lo == 0, y_total[:, cols:], y_total[:, :cols]).astype(bf16)
    grad_1 = keep + send(give, "dp", 0, 1).astype(f32)

    lower = carry_gradient(place, state_grad, state_1, d_terms)
    down_0 = exchange(lower)
    mine_0, theirs_0 = slope_product(place, down_0, slope_0)
    sibling_gathered_0 = to_sibling(gathered_0)
    sibling_theirs_0 = to_sibling(theirs_0)
    grad_blocks = {}
    for step in [(2, 1), (1, 1), (3, 1), (1, 0), (3, 0), (2, 0), (0, 1), (0, 0)]:
        target = (((my_y + step[0]) % 4) * 2 + (my_x_lo ^ step[1])).astype(jnp.int32)
        grad_blocks[step] = grad_block(
            target, gathered_0, sibling_gathered_0, mine_0, sibling_theirs_0, cols, bf16
        )
    grad_0 = add(*scatter_chips([grad_blocks[step] for step in steps], "dp"))

    update_1 = after(update_1, grad_blocks[(0, 0)])
    returned_1 = exchange(update_1.reshape(chips, tok_rows, 2 * head_cols))
    returned_1 = returned_1.transpose(1, 0, 2).reshape(tok_rows, model_width)
    rounded_1 = (state_1 + returned_1.astype(f32)).astype(bf16)
    head_grad = jnp.swapaxes(jnp.stack([grad_0, grad_1]), 1, 2)
    return (jnp.stack([rounded_0, rounded_1]), head_grad)


def solution(mesh):
    in_specs = (
        P("dp", "tensor"),
        P(("dp", "tensor"), None),
        P("tensor", None),
        P(),
        P(None, ("dp", "tensor")),
        P("tensor", "dp"),
        P(None, None, "tensor"),
        P(None, ("dp", "tensor"), None),
    )
    out_specs = (P(None, ("dp", "tensor"), None), P(None, "dp", "tensor"))
    return jax.shard_map(
        on_device, mesh=mesh, in_specs=in_specs, out_specs=out_specs, check_vma=False
    )
```

time: 407 us -> 350 us (0.86)
  waiting for transfers between devices: 173 us -> 81.3 us
  Pallas kernels: 0 us -> 60.4 us
  matrix products: 49 us -> 4.98 us
  local copies, waits for them, and re-layouts: 19.1 us -> 53.3 us
  starting transfers between devices: 69.3 us -> 94.7 us
  blocking collectives: 58.5 us -> 36.4 us
  other arithmetic: 33 us -> 15.3 us
    all_to_all x9 -> x5, waiting for transfers between devices: 84.7 us -> 9.8 us  [the longest x2 8.4 us: my_embeds(): return lax.all_to_all(rows, 'dp', split_axis=0, concat_axis=0, tiled=True)]
    pallas_call x0 -> x22, Pallas kernels: none -> 60.4 us  [the longest x12 21.8 us: grad_block(): call(body, (1,), [whole()] * 4, whole(), struct((out_rows, cols), dtype),...]
    ppermute x4 -> x39, starting transfers between devices: 7.59 us -> 60 us  [send(): return lax.ppermute(values, axis, chip_moves(axis, dz, dx))]
    dot_general x13 -> x4, matrix products: 49 us -> 4.98 us  [matmul(): lax.dot_general(left, right, (((left_dim,), (right_dim,)), ((), ())), pre...]
    unnamed x29 -> x135, local copies, waits for them, and re-layouts: 1.01 us -> 40.8 us
    all_to_all x9 -> x5, starting transfers between devices: 53.6 us -> 26.9 us  [the longest x2 13.5 us: exchange(): lax.all_to_all(values, 'tensor', split_axis=0, concat_axis=0, tiled=True,...]
    all_to_all x3, blocking collectives: 58.5 us -> 36.4 us  [the longest x2 25.3 us: exchange(): lax.all_to_all(values, 'tensor', split_axis=0, concat_axis=0, tiled=True,...]
    select_n x4 -> x0, other arithmetic: 16.7 us -> none  [the longest x1 15.4 us: on_device(): jnp.where(first_core, jnp.concatenate([head_weight, sibling_weight], axis...]
  transfers between devices with their start and end apart: 20 -> 51, of which waited for: 12 -> 17; matrix products, arithmetic and copies ran while one was open for 21% -> 9% of each run, Pallas kernels for 0% -> 13%
where the time goes in v2:
time: 350 us; the launch traced here: 348 us
  starting transfers between devices  94.7 us (27%)
  waiting for transfers between devices  81.3 us (23%)
  Pallas kernels  60.4 us (17%)
  local copies, waits for them, and re-layouts  53.3 us (15%)
  blocking collectives  36.4 us (10%)
  other arithmetic  15.3 us (4%)
  matrix products  4.98 us (1%)
    ppermute x39, starting transfers between devices, send(): return lax.ppermute(values, axis, chip_moves(axis, dz, dx))  60 us
    ppermute x39, waiting for transfers between devices, send(): return lax.ppermute(values, axis, chip_moves(axis, dz, dx))  59.8 us
    unnamed x135, local copies, waits for them, and re-layouts  40.8 us
    all_to_all x2, blocking collectives, exchange(): lax.all_to_all(values, 'tensor', split_axis=0, concat_axis=0, tiled=True,...  25.3 us
    pallas_call x12, Pallas kernels, grad_block(): call(body, (1,), [whole()] * 4, whole(), struct((out_rows, cols), dtype),...  21.8 us
    pallas_call x2, Pallas kernels, forward(): call(body, (count,), [whole()] * chips + [weight_spec] * 2, [whole()] * 3...  16.1 us
    all_to_all x2, starting transfers between devices, exchange(): lax.all_to_all(values, 'tensor', split_axis=0, concat_axis=0, tiled=True,...  13.5 us
    all_to_all x1, blocking collectives, on_device(): lax.all_to_all(jnp.broadcast_to(ids_here, (dp_count, id_count)), 'dp', sp...  11 us
  transfers between devices with their start and end apart: 51, of which 17 were waited for; matrix products, arithmetic and copies ran while one was open for 9% of the time, Pallas kernels for 13%

profile of v2, /device:TPU:4, one launch (start us, length us, event | category | flops | bytes accessed | tf_op | source)
XLA Modules:
  0.0 347.9 jit_solution(16222944713728992164)
XLA Ops:
  4.4 4.8 %shard_map.95 = bf16[256,5120]{1,0:T(8,128)(2,1)} custom-call(s32[9]{0:T(128)S(1)} %stack.63.place_ref, bf16[512,512]{1,0:T(8,128)(2,1)S(1)} %copy-done.14, bf16[512,5120]{1,0:T(8,128)(2,1)S(1)} %copy-done.6), custom_call_target="tpu_custom_call" | custom-call | flops 1342177280 | bytes 10485760 | tf_op jit(solution)/shard_map/pallas_call | solution.py:134
  9.8 11.0 %all_to_all.50 = s32[8,1,64]{2,1,0:T(1,128)S(1)} all-to-all(s32[8,1,64]{2,1,0:T(1,128)S(1)} %broadcast_in_dim.27), channel_id=1, replica_groups=mesh['dp'=8,'tensor'=16] {'dp'}, dimensions={0} | all-to-all | bytes 4096 | tf_op jit(solution)/shard_map/all_to_all | solution.py:390
  26.5 4.0 %shard_map.96 = (bf16[32,5120]{1,0:T(8,128)(2,1)S(1)}, bf16[32,5120]{1,0:T(8,128)(2,1)S(1)}, bf16[32,5120]{1,0:T(8,128)(2,1)S(1)}, bf16[32,5120]{1,0:T(8,128)(2,...) custom-call(s32[9]{0:T(128)S(1)} %stack.63.place_ref, ...), custom_call_target="tpu_custom_call" | custom-call | flops 1342177280 | bytes 10485760 | tf_op jit(solution)/shard_map/pallas_call | solution.py:137
  38.2 6.3 %all-to-all-start.1 = ((s32[16,1,64]{2,1,0:T(1,128)}), s32[16,1,64]{2,1,0:T(1,128)S(1)}, u32[]{:S(2)}, u32[]{:S(2)}) async-start(s32[16,1,64]{2,1,0:T(1,128)} %bitcast.10), calls=%async_computation.1 | async-start | bytes 16384 | tf_op jit(solution)/shard_map/all_to_all | solution.py:411
  49.9 8.8 %gather_fusion = bf16[1024,640]{1,0:T(8,128)(2,1)} fusion(bf16[4752,640]{1,0:T(8,128)(2,1)} %param.13, s32[1024]{0:T(1024)S(1)} %broadcast_clamp_fusion), kind=kCustom, calls=%fused_computation | custom fusion | bytes 2625536 | tf_op jit(solution)/shard_map/jit(_take)/gather | solution.py:412
  58.7 6.6 %all-to-all-start.2 = ((bf16[16,64,640]{2,1,0:T(8,128)(2,1)}), bf16[16,64,640]{2,1,0:T(8,128)(2,1)S(1)}, u32[]{:S(2)}, u32[]{:S(2)}) async-start(bf16[16,64,640]{2,1,0:T(8,128)(2,1)} %bitcast.11), calls=%async_computation.2 | async-start | bytes 2621440 | tf_op jit(solution)/shard_map/all_to_all | solution.py:413
  73.3 10.3 %all-to-all-done.2 = bf16[16,64,640]{2,1,0:T(8,128)(2,1)S(1)} async-done(((bf16[16,64,640]{2,1,0:T(8,128)(2,1)}), bf16[16,64,640]{2,1,0:T(8,128)(2,1)S(1)}, u32[]{:S(2)}, u32[]{:S(2)}) %all-to-all-start.2) | async-done | bytes 1310752 | tf_op jit(solution)/shard_map/all_to_all | solution.py:413
  91.1 8.4 %all-to-all-done.3.refs_6_ = bf16[8,32,640]{2,1,0:T(8,128)(2,1)S(1)} async-done(((bf16[8,32,640]{2,1,0:T(8,128)(2,1)}), bf16[8,32,640]{2,1,0:T(8,128)(2,1)S(1)}, u32[]{:S(2)}, u32[]{:S(2)}) %all-to-all-start.3) | async-done | bytes 327712 | tf_op jit(solution)/shard_map/all_to_all | solution.py:420
  103.9 5.1 %collective-permute-start.11 = (bf16[32,5120]{1,0:T(8,128)(2,1)S(1)}, bf16[32,5120]{1,0:T(8,128)(2,1)S(1)}, u32[]{:S(2)}, u32[]{:S(2)}) collective-permute-start(bf16[32,5120]{1,0:T(8,128)(2,1)S(1)} %get-tuple-element.68.refs_0_), channel_id=1, source_target_pairs={{0,8},{1,9},{2,10},{3,11},{4,12},{5,13},{6,14},{7,15},{8,0},{9,1},... | collective-permute-start | bytes 983048 | tf_op jit(solution)/shard_map/ppermute | solution.py:30
  112.3 5.3 %collective-permute-done.11.refs_4_ = bf16[32,5120]{1,0:T(8,128)(2,1)S(1)} collective-permute-done((bf16[32,5120]{1,0:T(8,128)(2,1)S(1)}, bf16[32,5120]{1,0:T(8,128)(2,1)S(1)}, u32[]{:S(2)}, u32[]{:S(2)}) %collective-permute-start.11) | collective-permute-done | bytes 327712 | tf_op jit(solution)/shard_map/ppermute | solution.py:30
  117.7 6.5 %collective-permute-done.13.refs_6_ = bf16[32,5120]{1,0:T(8,128)(2,1)S(1)} collective-permute-done((bf16[32,5120]{1,0:T(8,128)(2,1)S(1)}, bf16[32,5120]{1,0:T(8,128)(2,1)S(1)}, u32[]{:S(2)}, u32[]{:S(2)}) %collective-permute-start.13) | collective-permute-done | bytes 327712 | tf_op jit(solution)/shard_map/ppermute | solution.py:30
  129.2 3.6 %all-to-all-start.5 = ((bf16[8,32,640]{2,1,0:T(8,128)(2,1)}), bf16[8,32,640]{2,1,0:T(8,128)(2,1)S(1)}, u32[]{:S(2)}, u32[]{:S(2)}) async-start(bf16[8,32,640]{2,1,0:T(8,128)(2,1)} %bitcast.69), calls=%async_computation.5 | async-start | bytes 655360 | tf_op jit(solution)/shard_map/all_to_all | solution.py:420
  145.4 7.3 %shard_map.98 = (bf16[256,640]{1,0:T(8,128)(2,1)S(1)}, f32[256,640]{1,0:T(8,128)S(1)}, bf16[256,5120]{1,0:T(8,128)(2,1)S(1)}) custom-call(s32[9]{0:T(128)S(1)} %stack.63.place_ref, bf16[32,5120]{1,0:T(8,128)(2,1)S(1)} %copy-done.43, bf16[32,5120]{1,0:T(8,128)(2,1)S(1)} %copy-done.45, bf16[32,5120]{1,0:T(8,128)(2,1)S(1)} %copy-done.51, ...), custom_call_target="tpu_custom_call" | custom-call | flops 1677721600 | bytes 11796480 | tf_op jit(solution)/shard_map/pallas_call | solution.py:196
  153.6 12.1 %all_to_all.51.returned_ref = bf16[8,32,640]{2,1,0:T(8,128)(2,1)S(1)} all-to-all(bf16[8,32,640]{2,1,0:T(8,128)(2,1)S(1)} %bitcast.62), channel_id=1, replica_groups={{0,2,4,6,8,10,12,14},{1,3,5,7,9,11,13,15},{16,18,20,22,24,26,28,30},{17..., dimensions={0} | all-to-all | bytes 655360 | tf_op jit(solution)/shard_map/all_to_all | solution.py:38
  179.0 5.2 %collective-permute-done.19.refs_4_ = bf16[32,5120]{1,0:T(8,128)(2,1)} collective-permute-done((bf16[32,5120]{1,0:T(8,128)(2,1)S(1)}, bf16[32,5120]{1,0:T(8,128)(2,1)}, u32[]{:S(2)}, u32[]{:S(2)}) %collective-permute-start.19) | collective-permute-done | bytes 327712 | tf_op jit(solution)/shard_map/ppermute | solution.py:30
  187.4 6.7 %all-to-all-start.6 = ((bf16[8,32,640]{2,1,0:T(8,128)(2,1)}), bf16[8,32,640]{2,1,0:T(8,128)(2,1)S(1)}, u32[]{:S(2)}, u32[]{:S(2)}) async-start(bf16[8,32,640]{2,1,0:T(8,128)(2,1)} %bitcast.66), calls=%async_computation.6 | async-start | bytes 655360 | tf_op jit(solution)/shard_map/all_to_all | solution.py:38
  194.2 8.8 %shard_map.100 = (bf16[256,640]{1,0:T(8,128)(2,1)}, f32[256,640]{1,0:T(8,128)S(1)}, bf16[256,5120]{1,0:T(8,128)(2,1)S(1)}) custom-call(s32[9]{0:T(128)S(1)} %stack.63.place_ref, bf16[32,5120]{1,0:T(8,128)(2,1)S(1)} %get-tuple-element.73.refs_0_, bf16[32,5120]{1,0:T(8,128)(2,1)} %collective-permute-done.16.refs_1_, ...), custom_call_target="tpu_custom_call" | custom-call | flops 1677721600 | bytes 11796480 | tf_op jit(solution)/shard_map/pallas_call | solution.py:196
  207.3 7.6 %shard_map.102 = (bf16[32,5120]{1,0:T(8,128)(2,1)S(1)}, bf16[32,5120]{1,0:T(8,128)(2,1)S(1)}, bf16[32,5120]{1,0:T(8,128)(2,1)}, bf16[32,5120]{1,0:T(8,128)(2,1)S...) custom-call(s32[9]{0:T(128)S(1)} %stack.63.place_ref, ...), custom_call_target="tpu_custom_call" | custom-call | flops 1677721600 | bytes 9175040 | tf_op jit(solution)/shard_map/pallas_call | solution.py:251
  217.9 5.6 %collective-permute-done.26 = bf16[32,5120]{1,0:T(8,128)(2,1)S(1)} collective-permute-done((bf16[32,5120]{1,0:T(8,128)(2,1)S(1)}, bf16[32,5120]{1,0:T(8,128)(2,1)S(1)}, u32[]{:S(2)}, u32[]{:S(2)}) %collective-permute-start.26) | collective-permute-done | bytes 327712 | tf_op jit(solution)/shard_map/ppermute | solution.py:30
  250.3 13.3 %all_to_all.52 = bf16[8,32,640]{2,1,0:T(8,128)(2,1)S(1)} all-to-all(bf16[8,32,640]{2,1,0:T(8,128)(2,1)S(1)} %shard_map.107), channel_id=1, replica_groups={{0,2,4,6,8,10,12,14},{1,3,5,7,9,11,13,15},{16,18,20,22,24,26,28,30},{17..., dimensions={0} | all-to-all | bytes 655360 | tf_op jit(solution)/shard_map/all_to_all | solution.py:38
  268.8 6.7 %all-to-all-start.8 = ((bf16[8,32,640]{2,1,0:T(8,128)(2,1)}), bf16[8,32,640]{2,1,0:T(8,128)(2,1)}, u32[]{:S(2)}, u32[]{:S(2)}) async-start(bf16[8,32,640]{2,1,0:T(8,128)(2,1)} %bitcast.26), calls=%async_computation.8 | async-start | bytes 655360 | tf_op jit(solution)/shard_map/all_to_all | solution.py:38
  306.7 8.3 %collective-permute-done.42 = bf16[320,1280]{1,0:T(8,128)(2,1)} collective-permute-done((bf16[320,1280]{1,0:T(8,128)(2,1)}, bf16[320,1280]{1,0:T(8,128)(2,1)}, u32[]{:S(2)}, u32[]{:S(2)}) %collective-permute-start.42) | collective-permute-done | bytes 819232 | tf_op jit(solution)/shard_map/ppermute | solution.py:30
  321.4 11.0 %collective-permute-done.38 = bf16[320,640]{1,0:T(8,128)(2,1)S(1)} collective-permute-done((bf16[320,640]{1,0:T(8,128)(2,1)S(1)}, bf16[320,640]{1,0:T(8,128)(2,1)S(1)}, u32[]{:S(2)}, u32[]{:S(2)}) %collective-permute-start.38) | collective-permute-done | bytes 409632 | tf_op jit(solution)/shard_map/ppermute | solution.py:30
  336.5 8.8 %collective-permute-done.37 = bf16[320,640]{1,0:T(8,128)(2,1)S(1)} collective-permute-done((bf16[320,640]{1,0:T(8,128)(2,1)S(1)}, bf16[320,640]{1,0:T(8,128)(2,1)S(1)}, u32[]{:S(2)}, u32[]{:S(2)}) %collective-permute-start.37) | collective-permute-done | bytes 409632 | tf_op jit(solution)/shard_map/ppermute | solution.py:30
  (283 shorter events, 164.2 us)
Async XLA Ops:
  9.2 128.4 %collective-permute-start.15 = (bf16[2,320,5120]{2,1,0:T(8,128)(2,1)}, bf16[2,320,5120]{2,1,0:T(8,128)(2,1)}, u32[]{:S(2)}, u32[]{:S(2)}) collective-permute-start(bf16[2,320,5120]{2,1,0:T(8,128)(2,1)} %bitcast.14.refs_8_.weight_ref), channel_id=1, source_target_pairs={{0,1},{1,0},{2,3},{3,2},{4,5},{5,4},{6,7},{7,6},{8,9},{9,8},{10,11... | collective-permute-start | bytes 19660808 | tf_op jit(solution)/shard_map/ppermute | solution.py:34
  34.2 31.1 %collective-permute-start.5 = (bf16[32,5120]{1,0:T(8,128)(2,1)}, bf16[32,5120]{1,0:T(8,128)(2,1)}, u32[]{:S(2)}, u32[]{:S(2)}) collective-permute-start(bf16[32,5120]{1,0:T(8,128)(2,1)} %get-tuple-element.64), channel_id=1, source_target_pairs={{0,4},{1,5},{2,6},{3,7},{4,8},{5,9},{6,10},{7,11},{8,12},{9,13},{1... | collective-permute-start | bytes 983048 | tf_op jit(solution)/shard_map/ppermute | solution.py:30
  36.1 32.1 %collective-permute-start.6 = (bf16[32,5120]{1,0:T(8,128)(2,1)}, bf16[32,5120]{1,0:T(8,128)(2,1)}, u32[]{:S(2)}, u32[]{:S(2)}) collective-permute-start(bf16[32,5120]{1,0:T(8,128)(2,1)} %get-tuple-element.65), channel_id=1, source_target_pairs={{0,12},{1,13},{2,14},{3,15},{4,0},{5,1},{6,2},{7,3},{8,4},{9,5},{1... | collective-permute-start | bytes 983048 | tf_op jit(solution)/shard_map/ppermute | solution.py:30
  45.7 25.0 %collective-permute-start.3 = (bf16[32,5120]{1,0:T(8,128)(2,1)}, bf16[32,5120]{1,0:T(8,128)(2,1)}, u32[]{:S(2)}, u32[]{:S(2)}) collective-permute-start(bf16[32,5120]{1,0:T(8,128)(2,1)} %copy-done.61), channel_id=1, source_target_pairs={{0,2},{1,3},{2,0},{3,1},{4,6},{5,7},{6,4},{7,5},{8,10},{9,11},{10,... | collective-permute-start | bytes 983048 | tf_op jit(solution)/shard_map/ppermute | solution.py:30
  45.8 45.3 %collective-permute-start.1 = (bf16[32,5120]{1,0:T(8,128)(2,1)}, bf16[32,5120]{1,0:T(8,128)(2,1)S(1)}, u32[]{:S(2)}, u32[]{:S(2)}) collective-permute-start(bf16[32,5120]{1,0:T(8,128)(2,1)} %copy-done.60), channel_id=1, source_target_pairs={{0,4},{1,5},{2,6},{3,7},{4,8},{5,9},{6,10},{7,11},{8,12},{9,13},{1... | collective-permute-start | bytes 983048 | tf_op jit(solution)/shard_map/ppermute | solution.py:30
  58.7 24.8 %all-to-all-start.2 = ((bf16[16,64,640]{2,1,0:T(8,128)(2,1)}), bf16[16,64,640]{2,1,0:T(8,128)(2,1)S(1)}, u32[]{:S(2)}, u32[]{:S(2)}) async-start(bf16[16,64,640]{2,1,0:T(8,128)(2,1)} %bitcast.11), calls=%async_computation.2 | async-start | bytes 2621440 | tf_op jit(solution)/shard_map/all_to_all | solution.py:413
  65.3 25.7 %collective-permute-start.2 = (bf16[32,5120]{1,0:T(8,128)(2,1)S(1)}, bf16[32,5120]{1,0:T(8,128)(2,1)S(1)}, u32[]{:S(2)}, u32[]{:S(2)}) collective-permute-start(bf16[32,5120]{1,0:T(8,128)(2,1)S(1)} %copy-done.59), channel_id=1, source_target_pairs={{0,12},{1,13},{2,14},{3,15},{4,0},{5,1},{6,2},{7,3},{8,4},{9,5},{1... | collective-permute-start | bytes 983048 | tf_op jit(solution)/shard_map/ppermute | solution.py:30
  70.1 21.0 %collective-permute-start.7 = (bf16[32,5120]{1,0:T(8,128)(2,1)}, bf16[32,5120]{1,0:T(8,128)(2,1)S(1)}, u32[]{:S(2)}, u32[]{:S(2)}) collective-permute-start(bf16[32,5120]{1,0:T(8,128)(2,1)} %add_convert_fusion.5), channel_id=1, source_target_pairs={{0,2},{1,3},{2,0},{3,1},{4,6},{5,7},{6,4},{7,5},{8,10},{9,11},{10,... | collective-permute-start | bytes 983048 | tf_op jit(solution)/shard_map/ppermute | solution.py:30
  72.4 18.6 %collective-permute-start.4 = (bf16[32,5120]{1,0:T(8,128)(2,1)}, bf16[32,5120]{1,0:T(8,128)(2,1)S(1)}, u32[]{:S(2)}, u32[]{:S(2)}) collective-permute-start(bf16[32,5120]{1,0:T(8,128)(2,1)} %add_convert_fusion.6), channel_id=1, source_target_pairs={{0,8},{1,9},{2,10},{3,11},{4,12},{5,13},{6,14},{7,15},{8,0},{9,1},... | collective-permute-start | bytes 983048 | tf_op jit(solution)/shard_map/ppermute | solution.py:30
  109.0 23.8 %collective-permute-start.9 = (bf16[32,5120]{1,0:T(8,128)(2,1)S(1)}, bf16[32,5120]{1,0:T(8,128)(2,1)S(1)}, u32[]{:S(2)}, u32[]{:S(2)}) collective-permute-start(bf16[32,5120]{1,0:T(8,128)(2,1)S(1)} %get-tuple-element.68.refs_0_), channel_id=1, source_target_pairs={{0,12},{1,13},{2,14},{3,15},{4,0},{5,1},{6,2},{7,3},{8,4},{9,5},{1... | collective-permute-start | bytes 983048 | tf_op jit(solution)/shard_map/ppermute | solution.py:30
  112.3 21.3 %collective-permute-start.10 = (bf16[32,5120]{1,0:T(8,128)(2,1)S(1)}, bf16[32,5120]{1,0:T(8,128)(2,1)S(1)}, u32[]{:S(2)}, u32[]{:S(2)}) collective-permute-start(bf16[32,5120]{1,0:T(8,128)(2,1)S(1)} %collective-permute-done.8.refs_1_), channel_id=1, source_target_pairs={{0,12},{1,13},{2,14},{3,15},{4,0},{5,1},{6,2},{7,3},{8,4},{9,5},{1... | collective-permute-start | bytes 983048 | tf_op jit(solution)/shard_map/ppermute | solution.py:30
  117.7 19.2 %collective-permute-start.14 = (bf16[32,5120]{1,0:T(8,128)(2,1)S(1)}, bf16[32,5120]{1,0:T(8,128)(2,1)S(1)}, u32[]{:S(2)}, u32[]{:S(2)}) collective-permute-start(bf16[32,5120]{1,0:T(8,128)(2,1)S(1)} %collective-permute-done.8.refs_1_), channel_id=1, source_target_pairs={{0,4},{1,5},{2,6},{3,7},{4,8},{5,9},{6,10},{7,11},{8,12},{9,13},{1... | collective-permute-start | bytes 983048 | tf_op jit(solution)/shard_map/ppermute | solution.py:30
  129.2 24.4 %all-to-all-start.5 = ((bf16[8,32,640]{2,1,0:T(8,128)(2,1)}), bf16[8,32,640]{2,1,0:T(8,128)(2,1)S(1)}, u32[]{:S(2)}, u32[]{:S(2)}) async-start(bf16[8,32,640]{2,1,0:T(8,128)(2,1)} %bitcast.69), calls=%async_computation.5 | async-start | bytes 655360 | tf_op jit(solution)/shard_map/all_to_all | solution.py:420
  173.2 21.0 %collective-permute-start.17 = (bf16[32,5120]{1,0:T(8,128)(2,1)S(1)}, bf16[32,5120]{1,0:T(8,128)(2,1)}, u32[]{:S(2)}, u32[]{:S(2)}) collective-permute-start(bf16[32,5120]{1,0:T(8,128)(2,1)S(1)} %get-tuple-element.73.refs_0_), channel_id=1, source_target_pairs={{0,12},{1,13},{2,14},{3,15},{4,0},{5,1},{6,2},{7,3},{8,4},{9,5},{1... | collective-permute-start | bytes 983048 | tf_op jit(solution)/shard_map/ppermute | solution.py:30
  175.2 19.0 %collective-permute-start.21 = (bf16[32,5120]{1,0:T(8,128)(2,1)S(1)}, bf16[32,5120]{1,0:T(8,128)(2,1)}, u32[]{:S(2)}, u32[]{:S(2)}) collective-permute-start(bf16[32,5120]{1,0:T(8,128)(2,1)S(1)} %get-tuple-element.73.refs_0_), channel_id=1, source_target_pairs={{0,4},{1,5},{2,6},{3,7},{4,8},{5,9},{6,10},{7,11},{8,12},{9,13},{1... | collective-permute-start | bytes 983048 | tf_op jit(solution)/shard_map/ppermute | solution.py:30
  187.4 18.0 %all-to-all-start.6 = ((bf16[8,32,640]{2,1,0:T(8,128)(2,1)}), bf16[8,32,640]{2,1,0:T(8,128)(2,1)S(1)}, u32[]{:S(2)}, u32[]{:S(2)}) async-start(bf16[8,32,640]{2,1,0:T(8,128)(2,1)} %bitcast.66), calls=%async_computation.6 | async-start | bytes 655360 | tf_op jit(solution)/shard_map/all_to_all | solution.py:38
  217.4 18.2 %collective-permute-start.28 = (bf16[256,5120]{1,0:T(8,128)(2,1)S(1)}, bf16[256,5120]{1,0:T(8,128)(2,1)S(1)}, u32[]{:S(2)}, u32[]{:S(2)}) collective-permute-start(bf16[256,5120]{1,0:T(8,128)(2,1)S(1)} %copy-done.1), channel_id=1, source_target_pairs={{0,1},{1,0},{2,3},{3,2},{4,5},{5,4},{6,7},{7,6},{8,9},{9,8},{10,11... | collective-permute-start | bytes 7864328 | tf_op jit(solution)/shard_map/ppermute | solution.py:34
  217.4 47.0 %collective-permute-start.23 = (bf16[256,5120]{1,0:T(8,128)(2,1)S(1)}, bf16[256,5120]{1,0:T(8,128)(2,1)}, u32[]{:S(2)}, u32[]{:S(2)}) collective-permute-start(bf16[256,5120]{1,0:T(8,128)(2,1)S(1)} %get-tuple-element.75.inputs_ref), channel_id=1, source_target_pairs={{0,1},{1,0},{2,3},{3,2},{4,5},{5,4},{6,7},{7,6},{8,9},{9,8},{10,11... | collective-permute-start | bytes 7864328 | tf_op jit(solution)/shard_map/ppermute | solution.py:34
  268.8 34.3 %all-to-all-start.8 = ((bf16[8,32,640]{2,1,0:T(8,128)(2,1)}), bf16[8,32,640]{2,1,0:T(8,128)(2,1)}, u32[]{:S(2)}, u32[]{:S(2)}) async-start(bf16[8,32,640]{2,1,0:T(8,128)(2,1)} %bitcast.26), calls=%async_computation.8 | async-start | bytes 655360 | tf_op jit(solution)/shard_map/all_to_all | solution.py:38
  275.5 28.8 %collective-permute-start.41 = (bf16[320,1280]{1,0:T(8,128)(2,1)}, bf16[320,1280]{1,0:T(8,128)(2,1)}, u32[]{:S(2)}, u32[]{:S(2)}) collective-permute-start(bf16[320,1280]{1,0:T(8,128)(2,1)} %copy-done.22), channel_id=1, source_target_pairs={{0,64},{16,80},{32,96},{48,112},{64,0},{80,16},{96,32},{112,48},{1... | collective-permute-start | bytes 2457608 | tf_op jit(solution)/shard_map/ppermute | solution.py:30
  277.8 37.2 %collective-permute-start.42 = (bf16[320,1280]{1,0:T(8,128)(2,1)}, bf16[320,1280]{1,0:T(8,128)(2,1)}, u32[]{:S(2)}, u32[]{:S(2)}) collective-permute-start(bf16[320,1280]{1,0:T(8,128)(2,1)} %copy-done.21), channel_id=1, source_target_pairs={{0,32},{16,48},{32,64},{48,80},{64,96},{80,112},{96,0},{112,16},{1... | collective-permute-start | bytes 2457608 | tf_op jit(solution)/shard_map/ppermute | solution.py:30
  278.3 38.4 %collective-permute-start.43 = (bf16[320,1280]{1,0:T(8,128)(2,1)}, bf16[320,1280]{1,0:T(8,128)(2,1)}, u32[]{:S(2)}, u32[]{:S(2)}) collective-permute-start(bf16[320,1280]{1,0:T(8,128)(2,1)} %copy-done.20), channel_id=1, source_target_pairs={{0,96},{16,112},{32,0},{48,16},{64,32},{80,48},{96,64},{112,80},{1... | collective-permute-start | bytes 2457608 | tf_op jit(solution)/shard_map/ppermute | solution.py:30
  284.0 52.5 %collective-permute-start.34 = (bf16[320,640]{1,0:T(8,128)(2,1)}, bf16[320,640]{1,0:T(8,128)(2,1)}, u32[]{:S(2)}, u32[]{:S(2)}) collective-permute-start(bf16[320,640]{1,0:T(8,128)(2,1)} %shard_map.110), channel_id=1, source_target_pairs={{0,32},{16,48},{32,64},{48,80},{64,96},{80,112},{96,0},{112,16},{1... | collective-permute-start | bytes 1228808 | tf_op jit(solution)/shard_map/ppermute | solution.py:30
  287.0 49.5 %collective-permute-start.35 = (bf16[320,640]{1,0:T(8,128)(2,1)}, bf16[320,640]{1,0:T(8,128)(2,1)}, u32[]{:S(2)}, u32[]{:S(2)}) collective-permute-start(bf16[320,640]{1,0:T(8,128)(2,1)} %shard_map.111), channel_id=1, source_target_pairs={{0,96},{16,112},{32,0},{48,16},{64,32},{80,48},{96,64},{112,80},{1... | collective-permute-start | bytes 1228808 | tf_op jit(solution)/shard_map/ppermute | solution.py:30
  (94 other events, 697.8 us)

commit v3 on v2

v3 whole, which is shorter than its diff:
```python
import jax
import jax.numpy as jnp
from jax import lax
from jax.experimental import pallas as pl
from jax.experimental.pallas import tpu as pltpu
from jax.sharding import PartitionSpec as P

norm_eps = 1e-06
bf16 = jnp.bfloat16
f32 = jnp.float32
chips = 8
mib = 1024 * 1024

steps = [(dz, dx) for dz in range(4) for dx in range(2)]
core_swap = [(index, index ^ 1) for index in range(16)]
same_core = [[2 * chip + core for chip in range(chips)] for core in range(2)]


def chip_moves(axis, dz, dx):
    moves = []
    cores = 2 if axis == "tensor" else 1
    for chip in range(chips):
        target = ((chip // 2 + dz) % 4) * 2 + ((chip % 2) ^ dx)
        for core in range(cores):
            moves.append((chip * cores + core, target * cores + core))
    return moves


def after(values, *earlier):
    return lax.optimization_barrier((values,) + earlier)[0]


def send(values, axis, dz, dx):
    return lax.ppermute(values, axis, chip_moves(axis, dz, dx))


def to_sibling(values):
    return lax.ppermute(values, "tensor", core_swap)


def exchange(values):
    return lax.all_to_all(
        values, "tensor", split_axis=0, concat_axis=0, tiled=True, axis_index_groups=same_core
    )


def gather_chips(block):
    parts = {(0, 0): block}
    parts[(0, 1)] = send(block, "tensor", 0, 1)
    parts[(2, 0)] = send(block, "tensor", 2, 0)
    parts[(1, 0)] = send(block, "tensor", 3, 0)
    parts[(3, 0)] = send(block, "tensor", 1, 0)
    across = after(parts[(0, 1)], parts[(1, 0)], parts[(3, 0)])
    parts[(1, 1)] = send(across, "tensor", 3, 0)
    parts[(3, 1)] = send(across, "tensor", 1, 0)
    parts[(2, 1)] = send(parts[(2, 0)], "tensor", 0, 1)
    return [parts[step] for step in steps]


def add(*parts):
    total = parts[0].astype(f32)
    for part in parts[1:]:
        total = total + part.astype(f32)
    return total


groups = [(0,), (1,), (2, 3), (4,), (5,), (6, 7)]


def scatter_chips(blocks, axis, during=()):
    own, side, up, far, across, down = blocks
    across = send(across, axis, 0, 1)
    up = send(up, axis, 1, 0)
    down = send(down, axis, 3, 0)
    across, up, down, *during = lax.optimization_barrier((across, up, down, *during))
    far = send(add(far, across).astype(bf16), axis, 2, 0)
    side = send(add(side, up[1], down[1]).astype(bf16), axis, 0, 1)
    return [own, up, down, far, side], (across, up, down), during


def matmul(left, right, left_dim=1, right_dim=0):
    return lax.dot_general(
        left, right, (((left_dim,), (right_dim,)), ((), ())), preferred_element_type=f32
    )


def call(body, grid, in_specs, out_specs, out_shape, scratch=(), flops=0, moved=0, limit=16):
    return pl.pallas_call(
        body,
        grid_spec=pltpu.PrefetchScalarGridSpec(
            num_scalar_prefetch=1,
            grid=grid,
            in_specs=in_specs,
            out_specs=out_specs,
            scratch_shapes=list(scratch),
        ),
        out_shape=out_shape,
        compiler_params=pltpu.CompilerParams(vmem_limit_bytes=limit * mib),
        cost_estimate=pl.CostEstimate(flops=flops, bytes_accessed=moved, transcendentals=0),
    )


def whole():
    return pl.BlockSpec(memory_space=pltpu.VMEM)


def in_hbm():
    return pl.BlockSpec(memory_space=pltpu.HBM)


def columns(rows, tile):
    return pl.BlockSpec((rows, tile), lambda i, place: (0, i))


def group_columns(count, rows, tile):
    return pl.BlockSpec((count, rows, tile), lambda i, place: (0, 0, i))


def store_groups(out_refs, total, rows):
    for out_ref, group in zip(out_refs, groups):
        for position, i in enumerate(group):
            out_ref[position] = total[i * rows : (i + 1) * rows]


def struct(shape, dtype):
    return jax.ShapeDtypeStruct(shape, dtype)


def block_rows(index, rows):
    return pl.ds(pl.multiple_of(index * rows, rows), rows)


def project(place, context, out_proj, rows, far_side, arrived=None):
    depth, width = out_proj.shape
    tile = 2560
    half = chips * rows

    def left(place_ref, context_ref):
        core = place_ref[chips]
        core = 1 - core if far_side else core
        return jnp.concatenate(
            [context_ref[block_rows(place_ref[i] * 2 + core, rows), :] for i in range(chips)], axis=0
        )

    def far_body(place_ref, context_ref, weight_ref, out_ref):
        out_ref[...] = matmul(left(place_ref, context_ref), weight_ref[...]).astype(bf16)

    def near_body(place_ref, context_ref, weight_ref, arrived_ref, *out_refs):
        total = matmul(left(place_ref, context_ref), weight_ref[...]) + arrived_ref[...].astype(f32)
        total = total.astype(bf16)
        store_groups(out_refs, total, rows)

    in_specs = [whole(), columns(depth, tile)]
    costs = dict(flops=2 * half * depth * width, moved=2 * depth * width + 4 * half * width)
    if far_side:
        return call(
            far_body,
            (width // tile,),
            in_specs,
            columns(half, tile),
            struct((half, width), bf16),
            **costs,
        )(place, context, out_proj)
    return call(
        near_body,
        (width // tile,),
        in_specs + [columns(half, tile)],
        [group_columns(len(group), rows, tile) for group in groups],
        [struct((len(group), rows, width), bf16) for group in groups],
        limit=60,
        **costs,
    )(place, context, out_proj, arrived)


def forward(place, pieces, weight, sibling, head, extra=None):
    rows, width = pieces[0].shape
    cols = weight.shape[1]
    tile = 2560
    half = chips * rows
    count = width // tile

    def body(place_ref, *refs):
        piece_refs, (mine_ref, sibling_ref) = refs[:chips], refs[chips : chips + 2]
        update_ref, slope_ref, gathered_ref, mine_acc, sibling_acc = refs[-5:]
        step = pl.program_id(0)
        for i in range(chips):
            gathered_ref[block_rows(place_ref[i], rows), :] = piece_refs[i][...]
        left = gathered_ref[...]
        mine = matmul(left, mine_ref[0], 1, 1)
        theirs = matmul(left, sibling_ref[0], 1, 1)

        @pl.when(step == 0)
        def _():
            mine_acc[...] = mine
            sibling_acc[...] = theirs

        @pl.when(step > 0)
        def _():
            mine_acc[...] += mine
            sibling_acc[...] += theirs

        @pl.when(step == count - 1)
        def _():
            def results(pre_act):
                sigmoid = 1.0 / (1.0 + jnp.exp(-pre_act))
                return pre_act * sigmoid, sigmoid * (1.0 + pre_act * (1.0 - sigmoid))

            first = place_ref[chips] == 0
            update_a, slope_a = results(mine_acc[...])
            update_b, slope_b = results(sibling_acc[...])
            update = jnp.concatenate(
                [jnp.where(first, update_a, update_b), jnp.where(first, update_b, update_a)], axis=1
            ).astype(bf16)
            for i in range(chips):
                update_ref[i, :rows] = update[i * rows : (i + 1) * rows]
            if extra is not None:
                update_ref[:, rows:] = refs[chips + 2][...]
            slope_ref[...] = jnp.concatenate(
                [jnp.where(first, slope_a, slope_b), jnp.where(first, slope_b, slope_a)], axis=1
            )

    weight_spec = pl.BlockSpec((1, cols, tile), lambda i, place: (head, 0, i))
    extras = [] if extra is None else [extra]
    update_shape = struct((chips, rows * (1 + len(extras)), 2 * cols), bf16)
    return call(
        body,
        (count,),
        [columns(rows, tile)] * chips + [weight_spec] * 2 + [whole()] * len(extras),
        [whole()] * 2 + [columns(half, tile)],
        [update_shape, struct((half, 2 * cols), f32), struct((half, width), bf16)],
        [pltpu.VMEM((half, cols), f32)] * 2,
        flops=4 * half * width * cols,
        moved=4 * width * cols + 4 * half * width,
        limit=24,
    )(place, *pieces, weight, sibling, *extras)


def split_columns(place, values):
    _, rows, width = values.shape
    cols = width // chips

    def body(place_ref, values_ref, out_ref):
        for i in range(chips):
            out_ref[i] = values_ref[0, :, i * cols : (i + 1) * cols].astype(bf16)

    return call(
        body,
        (1,),
        [pl.BlockSpec((1, rows, width), lambda i, place: (1, 0, 0))],
        whole(),
        struct((chips, rows, cols), bf16),
        moved=rows * width * 6,
    )(place, values)


def slope_product(place, down, slope, start):
    half, both = slope.shape
    cols = both // 2
    rows = half // chips

    def body(place_ref, down_ref, slope_ref, mine_ref, theirs_ref, mine_t_ref, theirs_t_ref):
        d_act = jnp.concatenate([down_ref[i, start : start + rows] for i in range(chips)], axis=0)
        d_act = d_act.astype(f32) * slope_ref[...]
        first = place_ref[chips] == 0
        low, high = d_act[:, :cols], d_act[:, cols:]
        mine = jnp.where(first, low, high)
        theirs = jnp.where(first, high, low)
        mine_ref[...] = mine.astype(bf16)
        theirs_ref[...] = theirs.astype(bf16)
        mine_t_ref[...] = mine.T.astype(bf16)
        theirs_t_ref[...] = theirs.T.astype(bf16)

    return call(
        body,
        (1,),
        [whole()] * 2,
        [whole()] * 4,
        [struct((half, cols), bf16)] * 2 + [struct((cols, half), bf16)] * 2,
        moved=half * both * 8,
    )(place, down, slope)


def backward(place, mine, theirs, weight, sibling, head):
    half, cols = mine.shape
    width = weight.shape[2]
    rows = half // chips
    tile = 2560

    def body(place_ref, mine_ref, theirs_ref, weight_ref, sibling_ref, *out_refs):
        def ordered(ref):
            return jnp.concatenate([ref[block_rows(place_ref[i], rows), :] for i in range(chips)], axis=0)

        total = matmul(ordered(mine_ref), weight_ref[0])
        total = total + matmul(ordered(theirs_ref), sibling_ref[0])
        total = total.astype(bf16)
        store_groups(out_refs, total, rows)

    weight_spec = pl.BlockSpec((1, cols, tile), lambda i, place: (head, 0, i))
    return call(
        body,
        (width // tile,),
        [whole()] * 2 + [weight_spec] * 2,
        [group_columns(len(group), rows, tile) for group in groups],
        [struct((len(group), rows, width), bf16) for group in groups],
        flops=4 * half * width * cols,
        moved=4 * width * cols + 2 * half * width,
    )(place, mine, theirs, weight, sibling)


def grad_blocks(targets, inputs, sibling_inputs, mine, sibling_mine, cols, groups, limit):
    half = inputs.shape[0]
    out_rows = mine.shape[0]
    count = len(targets)

    def body(place_ref, inputs_ref, sibling_ref, mine_ref, sibling_mine_ref, *refs):
        out_refs = refs[: len(groups)]
        right_ref, out_vmem, in_sems, out_sems = refs[len(groups) :]
        homes = {i: out_ref.at[n] for out_ref, group in zip(out_refs, groups) for n, i in enumerate(group)}

        def load(i):
            part = block_rows(place_ref[i], cols)
            return [
                pltpu.make_async_copy(
                    source.at[:, part], right_ref.at[i, pl.ds(j * half, half), :], in_sems.at[i, j]
                )
                for j, source in enumerate((inputs_ref, sibling_ref))
            ]

        def store(i):
            return pltpu.make_async_copy(out_vmem.at[i], homes[i], out_sems.at[i])

        for i in range(count):
            for copy in load(i):
                copy.start()
        left = jnp.concatenate([mine_ref[...], sibling_mine_ref[...]], axis=1)
        for i in range(count):
            for copy in load(i):
                copy.wait()
            out_vmem[i] = matmul(left, right_ref[i]).astype(bf16)
            store(i).start()
        for i in range(count):
            store(i).wait()

    return call(
        body,
        (1,),
        [in_hbm()] * 2 + [whole()] * 2,
        [in_hbm()] * len(groups),
        [struct((len(group), out_rows, cols), bf16) for group in groups],
        [
            pltpu.VMEM((count, 2 * half, cols), bf16),
            pltpu.VMEM((count, out_rows, cols), bf16),
            pltpu.SemaphoreType.DMA((count, 2)),
            pltpu.SemaphoreType.DMA((count,)),
        ],
        flops=4 * half * cols * out_rows * count,
        moved=4 * half * (cols + out_rows) * count + 4 * cols * out_rows * count,
        limit=limit,
    )(jnp.stack(targets).astype(jnp.int32), inputs, sibling_inputs, mine, sibling_mine)


def mean_last(values):
    return jnp.mean(values, axis=-1, keepdims=True)


def first_state(place, residual, terms, gain, embeds):
    rows, width = residual.shape
    cols = width // chips

    def body(place_ref, residual_ref, *refs):
        term_refs, gain_ref, embeds_ref, state_ref, inputs_ref = refs[:-4], *refs[-4:]
        hidden = residual_ref[...].astype(f32) + add(*[ref[0] for ref in term_refs])
        state = hidden * lax.rsqrt(mean_last(hidden * hidden) + norm_eps) * gain_ref[...].astype(f32)
        state_ref[...] = state
        scale = lax.rsqrt(mean_last(state * state) + norm_eps)
        for i in range(chips):
            part = slice(i * cols, (i + 1) * cols)
            inputs_ref[:, part] = (state[:, part] * scale + embeds_ref[i, 0].astype(f32)).astype(bf16)

    return call(
        body,
        (1,),
        [whole()] * (3 + len(terms)),
        [whole()] * 2,
        [struct((rows, width), f32), struct((rows, width), bf16)],
        moved=rows * width * 20,
        limit=60,
    )(place, residual, *terms, gain.reshape(1, width), embeds)


def next_state(place, state, returned, embeds):
    rows, width = state.shape
    cols = width // chips

    def body(place_ref, state_ref, returned_ref, embeds_ref, state_out, inputs_ref, rounded_ref):
        returned_all = jnp.concatenate([returned_ref[i, :rows] for i in range(chips)], axis=1)
        new_state = state_ref[...] + returned_all.astype(f32)
        state_out[...] = new_state
        rounded_ref[...] = new_state.astype(bf16)
        scale = lax.rsqrt(mean_last(new_state * new_state) + norm_eps)
        for i in range(chips):
            part = slice(i * cols, (i + 1) * cols)
            inputs_ref[:, part] = (new_state[:, part] * scale + embeds_ref[i, 1].astype(f32)).astype(bf16)

    return call(
        body,
        (1,),
        [whole()] * 3,
        [whole()] * 3,
        [struct((rows, width), f32), struct((rows, width), bf16), struct((rows, width), bf16)],
        moved=rows * width * 16,
    )(place, state, returned, embeds)


def last_state(place, state, returned):
    rows, width = state.shape
    cols = width // chips

    def body(place_ref, state_ref, returned_ref, out_ref):
        for i in range(chips):
            part = slice(i * cols, (i + 1) * cols)
            out_ref[:, part] = (state_ref[:, part] + returned_ref[i, rows:].astype(f32)).astype(bf16)

    return call(
        body,
        (1,),
        [whole()] * 2,
        whole(),
        struct((rows, width), bf16),
        moved=rows * width * 8,
    )(place, state, returned)


def carry_gradient(place, state_grad, state, terms, extra):
    rows, width = state.shape
    cols = width // chips

    def body(place_ref, upper_ref, lower_ref, state_ref, *refs):
        term_refs, extra_ref, out_ref = refs[:-2], refs[-2], refs[-1]
        previous = state_ref[...]
        d_input = add(*[ref[0] for ref in term_refs])
        scale = lax.rsqrt(mean_last(previous * previous) + norm_eps)
        shared = mean_last(d_input * previous)
        total = upper_ref[0] + scale * d_input - previous * (scale * scale * scale * shared) + lower_ref[0]
        total = total.astype(bf16)
        for i in range(chips):
            out_ref[i, :rows] = total[:, i * cols : (i + 1) * cols]
        out_ref[:, rows:] = extra_ref[...]

    return call(
        body,
        (1,),
        [
            pl.BlockSpec((1, rows, width), lambda i, place: (1, 0, 0)),
            pl.BlockSpec((1, rows, width), lambda i, place: (0, 0, 0)),
        ]
        + [whole()] * (2 + len(terms)),
        whole(),
        struct((chips, 2 * rows, cols), bf16),
        moved=rows * width * 24,
    )(place, state_grad, state_grad, state, *terms, extra)


def on_device(
    context, residual, out_proj, final_gain, next_ids, embed_table, head_weight, state_grad
):
    tensor_count = lax.axis_size("tensor")
    dp_count = lax.axis_size("dp")
    my_tensor = lax.axis_index("tensor")
    my_core = my_tensor % 2
    my_z, my_x_hi = my_tensor // 4, (my_tensor // 2) % 2
    my_dp = lax.axis_index("dp")
    my_y, my_x_lo = my_dp // 2, my_dp % 2
    tok_rows, model_width = residual.shape
    head_count, _, head_cols = head_weight.shape
    weight = jnp.swapaxes(head_weight, 1, 2)
    vocab_rows, table_cols = embed_table.shape
    place = jnp.stack([((my_z + dz) % 4) * 2 + (my_x_hi ^ dx) for dz, dx in steps] + [my_core])
    place = place.astype(jnp.int32)

    ids_here = next_ids.reshape(1, -1)
    id_count = ids_here.shape[1]
    group_ids = dp_count * id_count
    capacity = 2 * group_ids // tensor_count
    places_all = tensor_count * capacity
    group = lax.all_to_all(
        jnp.broadcast_to(ids_here, (dp_count, id_count)), "dp", split_axis=0, concat_axis=0, tiled=True
    )
    group = group.reshape(group_ids)
    owners = group // vocab_rows
    rows_in = group - owners * vocab_rows
    before = jnp.triu(jnp.ones((group_ids, group_ids), bf16), 1)
    is_owner = owners[None, :] == jnp.arange(tensor_count, dtype=jnp.int32)[:, None]
    earlier = matmul(is_owner.astype(bf16), before)
    slots = jnp.sum(jnp.where(is_owner, earlier, 0.0), axis=0).astype(jnp.int32)
    places = owners * capacity + slots
    pick = (places[:, None] == jnp.arange(places_all, dtype=jnp.int32)[None, :]).astype(bf16)
    digits = jnp.stack([rows_in // 64, rows_in % 64]).astype(bf16)
    asked = matmul(digits, pick)
    requests = (asked[0] * 64.0 + asked[1]).astype(jnp.int32).reshape(tensor_count, capacity)

    context = after(context, group)
    arrived = to_sibling(project(place, context, out_proj, tok_rows, True))

    wanted = lax.all_to_all(requests, "tensor", split_axis=0, concat_axis=0, tiled=True)
    found_rows = jnp.take(embed_table, wanted, axis=0, mode="clip")
    arrived = after(arrived, found_rows)
    blocks = project(place, context, out_proj, tok_rows, False, arrived)
    terms, _, _ = scatter_chips(blocks, "tensor")
    answers = lax.all_to_all(found_rows, "tensor", split_axis=0, concat_axis=0, tiled=True)
    answers = answers.reshape(places_all, table_cols)
    my_rows = matmul(pick, answers).astype(bf16)
    my_rows = my_rows.reshape(dp_count, head_count, tok_rows, table_cols)

    embeds = lax.all_to_all(my_rows, "dp", split_axis=0, concat_axis=0, tiled=True)
    sibling_weight = to_sibling(weight)

    state_0, inputs_0 = first_state(place, residual, terms, final_gain, embeds)
    pieces_0 = gather_chips(inputs_0)
    upper = split_columns(place, after(state_grad, inputs_0))
    update_0, slope_0, gathered_0 = forward(place, pieces_0, weight, sibling_weight, 0, upper)
    returned_0 = exchange(update_0)
    state_1, inputs_1, rounded_0 = next_state(place, state_0, returned_0, embeds)

    pieces_1 = gather_chips(inputs_1)
    update_1, slope_1, gathered_1 = forward(place, pieces_1, weight, sibling_weight, 1)
    mine_1, theirs_1, mine_1_t, theirs_1_t = slope_product(place, returned_0, slope_1, tok_rows)
    d_blocks = backward(place, mine_1, theirs_1, weight, sibling_weight, 1)

    cols = model_width // dp_count
    y_targets = [(my_y + dy) % 4 for dy in (2, 1, 3, 0)]
    products = grad_blocks(
        y_targets,
        gathered_1,
        to_sibling(gathered_1),
        mine_1_t,
        to_sibling(theirs_1_t),
        2 * cols,
        [(0,), (1,), (2,), (3,)],
        16,
    )
    d_terms, _, _ = scatter_chips(d_blocks, "tensor", products)
    y_terms = [send(part, "dp", dy, 0) for dy, part in zip((2, 1, 3), products)] + [products[3]]

    lower = carry_gradient(place, state_grad, state_1, d_terms, update_1)
    returned_1 = exchange(lower)
    _, _, mine_0_t, theirs_0_t = slope_product(place, returned_1, slope_0, 0)
    sibling_gathered_0, sibling_0_t = to_sibling(gathered_0), to_sibling(theirs_0_t)

    def made(chosen, mine_t):
        targets = [
            ((my_y + steps[i][0]) % 4) * 2 + (my_x_lo ^ steps[i][1]) for group in chosen for i in group
        ]
        order = iter(range(len(targets)))
        places_of = [tuple(next(order) for _ in group) for group in chosen]
        return grad_blocks(
            targets, gathered_0, sibling_gathered_0, mine_t, sibling_0_t, cols, places_of, 60
        )

    mine_0_t, *y_terms = lax.optimization_barrier((mine_0_t, *y_terms))
    across, up, down = made([(5,), (2, 3), (6, 7)], mine_0_t)
    own, side, far = made([(0,), (1,), (4,)], after(mine_0_t, across))
    y_terms = lax.optimization_barrier((*y_terms, across))[:4]
    y_total = add(*[term[0] for term in y_terms])
    keep = jnp.where(my_x_lo == 0, y_total[:, :cols], y_total[:, cols:])
    give = jnp.where(my_x_lo == 0, y_total[:, cols:], y_total[:, :cols]).astype(bf16)
    given = send(give, "dp", 0, 1)
    grad_terms, first_arrived, (own, side, far, given) = scatter_chips(
        (own, side, up, far, across, down), "dp", (own, side, far, given)
    )
    grad_0 = add(*[term[0] for term in grad_terms])
    grad_1 = keep + given.astype(f32)

    rounded_1 = last_state(place, state_1, after(returned_1, *first_arrived))
    head_grad = jnp.swapaxes(jnp.stack([grad_0, grad_1]), 1, 2)
    return (jnp.stack([rounded_0, rounded_1]), head_grad)


def solution(mesh):
    in_specs = (
        P("dp", "tensor"),
        P(("dp", "tensor"), None),
        P("tensor", None),
        P(),
        P(None, ("dp", "tensor")),
        P("tensor", "dp"),
        P(None, None, "tensor"),
        P(None, ("dp", "tensor"), None),
    )
    out_specs = (P(None, ("dp", "tensor"), None), P(None, "dp", "tensor"))
    return jax.shard_map(
        on_device, mesh=mesh, in_specs=in_specs, out_specs=out_specs, check_vma=False
    )
```

time: 350 us -> 304 us (0.87)
  local copies, waits for them, and re-layouts: 53.3 us -> 22 us
  starting transfers between devices: 94.7 us -> 69.8 us
  waiting for transfers between devices: 81.3 us -> 94.7 us
  blocking collectives: 36.4 us -> 42.9 us
  Pallas kernels: 60.4 us -> 56.6 us
  other arithmetic: 15.3 us -> 11.7 us
    unnamed x135 -> x72, local copies, waits for them, and re-layouts: 40.8 us -> 9.7 us
    ppermute x39 -> x33, waiting for transfers between devices: 59.8 us -> 79.2 us  [send(): return lax.ppermute(values, axis, chip_moves(axis, dz, dx))]
    all_to_all x5 -> x2, starting transfers between devices: 26.9 us -> 11 us  [the longest x1 5.88 us: on_device(): lax.all_to_all(my_rows, 'dp', split_axis=0, concat_axis=0, tiled=True)]
    ppermute x39 -> x33, starting transfers between devices: 60 us -> 51 us  [send(): return lax.ppermute(values, axis, chip_moves(axis, dz, dx))]
    pallas_call x19 -> x12, Pallas kernels: 56 us -> 50.5 us  [the longest x3 16.8 us: grad_blocks(): call(body, (1,), [in_hbm()] * 2 + [whole()] * 2, [in_hbm()] * len(groups)...]
    all_to_all x5 -> x2, waiting for transfers between devices: 9.8 us -> 4.97 us  [the longest x1 4.97 us: on_device(): lax.all_to_all(my_rows, 'dp', split_axis=0, concat_axis=0, tiled=True)]
    all_to_all x2, blocking collectives: 25.3 us -> 30.2 us  [exchange(): lax.all_to_all(values, 'tensor', split_axis=0, concat_axis=0, tiled=True,...]
  transfers between devices with their start and end apart: 51 -> 42, of which waited for: 17 -> 29; matrix products, arithmetic and copies ran while one was open for 9% -> 7% of each run, Pallas kernels for 13% -> 12%
where the time goes in v3:
time: 304 us; the launch traced here: 303 us
  waiting for transfers between devices  94.7 us (31%)
  starting transfers between devices  69.8 us (23%)
  Pallas kernels  56.6 us (19%)
  blocking collectives  42.9 us (14%)
  local copies, waits for them, and re-layouts  22 us (7%)
  other arithmetic  11.7 us (4%)
  matrix products  4.04 us (1%)
    ppermute x33, waiting for transfers between devices, send(): return lax.ppermute(values, axis, chip_moves(axis, dz, dx))  79.2 us
    ppermute x33, starting transfers between devices, send(): return lax.ppermute(values, axis, chip_moves(axis, dz, dx))  51 us
    all_to_all x2, blocking collectives, exchange(): lax.all_to_all(values, 'tensor', split_axis=0, concat_axis=0, tiled=True,...  30.2 us
    pallas_call x3, Pallas kernels, grad_blocks(): call(body, (1,), [in_hbm()] * 2 + [whole()] * 2, [in_hbm()] * len(groups)...  16.8 us
    pallas_call x2, Pallas kernels, forward(): call(body, (count,), [columns(rows, tile)] * chips + [weight_spec] * 2 +...  14 us
    all_to_all x1, blocking collectives, on_device(): lax.all_to_all(requests, 'tensor', split_axis=0, concat_axis=0, tiled=True)  12.8 us
    unnamed x72, local copies, waits for them, and re-layouts  9.7 us
    all_to_all x1, waiting for transfers between devices, on_device(): lax.all_to_all(found_rows, 'tensor', split_axis=0, concat_axis=0, tiled=T...  8.94 us
  transfers between devices with their start and end apart: 42, of which 29 were waited for; matrix products, arithmetic and copies ran while one was open for 7% of the time, Pallas kernels for 12%

profile of v3, /device:TPU:4, one launch (start us, length us, event | category | flops | bytes accessed | tf_op | source)
XLA Modules:
  0.0 303.0 jit_solution(6477180330665761460)
XLA Ops:
  2.0 5.1 %all-to-all-start = ((s32[8,1,64]{2,1,0:T(1,128)}), s32[8,1,64]{2,1,0:T(1,128)S(1)}, u32[]{:S(2)}, u32[]{:S(2)}) async-start(s32[8,1,64]{2,1,0:T(1,128)} %broadcast_in_dim.19), calls=%async_computation | async-start | bytes 8192 | tf_op jit(solution)/shard_map/all_to_all | solution.py:486
  16.5 12.8 %all_to_all.32 = s32[16,1,64]{2,1,0:T(1,128)S(1)} all-to-all(s32[16,1,64]{2,1,0:T(1,128)S(1)} %bitcast.47), channel_id=1, replica_groups=mesh['dp'=8,'tensor'=16] {'tensor'}, dimensions={0} | all-to-all | bytes 8192 | tf_op jit(solution)/shard_map/all_to_all | solution.py:505
  30.0 8.8 %gather_fusion = bf16[1024,640]{1,0:T(8,128)(2,1)} fusion(bf16[4752,640]{1,0:T(8,128)(2,1)} %param.13, s32[1024]{0:T(1024)S(1)} %broadcast_clamp_fusion), kind=kCustom, calls=%fused_computation | custom fusion | bytes 2625536 | tf_op jit(solution)/shard_map/jit(_take)/gather | solution.py:506
  38.8 7.1 %all-to-all-start.2 = ((bf16[16,64,640]{2,1,0:T(8,128)(2,1)}), bf16[16,64,640]{2,1,0:T(8,128)(2,1)}, u32[]{:S(2)}, u32[]{:S(2)}) async-start(bf16[16,64,640]{2,1,0:T(8,128)(2,1)} %bitcast.44), calls=%async_computation.2 | async-start | bytes 2621440 | tf_op jit(solution)/shard_map/all_to_all | solution.py:510
  45.9 5.9 %shard_map.96 = (bf16[1,32,5120]{2,1,0:T(8,128)(2,1)}, bf16[1,32,5120]{2,1,0:T(8,128)(2,1)}, bf16[2,32,5120]{2,1,0:T(8,128)(2,1)}, bf16[1,32,5120]{2,1,0:T(8,128...) custom-call(s32[9]{0:T(128)} %copy-done.23, bf16[512,512]{1,0:T(8,128)(2,1)} %context_ref.1, ...), custom_call_target="tpu_custom_call" | custom-call | flops 1342177280 | bytes 10485760 | tf_op jit(solution)/shard_map/pallas_call | solution.py:164
  55.4 8.9 %all-to-all-done.2 = bf16[16,64,640]{2,1,0:T(8,128)(2,1)} async-done(((bf16[16,64,640]{2,1,0:T(8,128)(2,1)}), bf16[16,64,640]{2,1,0:T(8,128)(2,1)}, u32[]{:S(2)}, u32[]{:S(2)}) %all-to-all-start.2) | async-done | bytes 1310752 | tf_op jit(solution)/shard_map/all_to_all | solution.py:510
  67.6 5.9 %all-to-all-start.3 = ((bf16[8,2,32,640]{3,2,1,0:T(8,128)(2,1)}), bf16[8,2,32,640]{3,2,1,0:T(8,128)(2,1)S(1)}, u32[]{:S(2)}, u32[]{:S(2)}) async-start(bf16[8,2,32,640]{3,2,1,0:T(8,128)(2,1)} %bitcast.15), calls=%async_computation.3 | async-start | bytes 1310720 | tf_op jit(solution)/shard_map/all_to_all | solution.py:515
  73.5 4.4 %collective-permute-done.2.refs_1_ = bf16[2,32,5120]{2,1,0:T(8,128)(2,1)S(1)} collective-permute-done((bf16[2,32,5120]{2,1,0:T(8,128)(2,1)}, bf16[2,32,5120]{2,1,0:T(8,128)(2,1)S(1)}, u32[]{:S(2)}, u32[]{:S(2)}) %collective-permute-start.2) | collective-permute-done | bytes 655392 | tf_op jit(solution)/shard_map/ppermute | solution.py:34
  81.0 5.0 %all-to-all-done.3.refs_6_.embeds_ref = bf16[8,2,32,640]{3,2,1,0:T(8,128)(2,1)S(1)} async-done(((bf16[8,2,32,640]{3,2,1,0:T(8,128)(2,1)}), bf16[8,2,32,640]{3,2,1,0:T(8,128)(2,1)S(1)}, u32[]{:S(2)}, u32[]{:S(2)}) %all-to-all-start.3) | async-done | bytes 655392 | tf_op jit(solution)/shard_map/all_to_all | solution.py:515
  91.0 4.1 %shard_map.97 = (f32[32,5120]{1,0:T(8,128)}, bf16[32,5120]{1,0:T(8,128)(2,1)}) custom-call(s32[9]{0:T(128)} %copy-done.23, bf16[32,5120]{1,0:T(8,128)(2,1)} %residual_ref.1, bf16[1,32,5120]{2,1,0:T(8,128)(2,1)} %get-tuple-element.67.refs_0_, bf16[2,32,5120]{2,1,0:T(8,128)(2,1)} %copy-done.27, bf16[2,32,5120]{2,1,0:T(8,128)(2,1)} %copy-done.28, ...), custom_call_target="tpu_custom_call" | custom-call | bytes 3276800 | tf_op jit(solution)/shard_map/pallas_call | solution.py:380
  100.4 5.0 %collective-permute-done.6.refs_1_ = bf16[32,5120]{1,0:T(8,128)(2,1)S(1)} collective-permute-done((bf16[32,5120]{1,0:T(8,128)(2,1)}, bf16[32,5120]{1,0:T(8,128)(2,1)S(1)}, u32[]{:S(2)}, u32[]{:S(2)}) %collective-permute-start.6) | collective-permute-done | bytes 327712 | tf_op jit(solution)/shard_map/ppermute | solution.py:34
  124.6 6.5 %shard_map.99 = (bf16[8,64,640]{2,1,0:T(8,128)(2,1)S(1)}, f32[256,640]{1,0:T(8,128)S(1)}, bf16[256,5120]{1,0:T(8,128)(2,1)S(1)}) custom-call(s32[9]{0:T(128)S(1)} %copy-done.24, bf16[32,5120]{1,0:T(8,128)(2,1)S(1)} %copy-done.22, bf16[32,5120]{1,0:T(8,128)(2,1)S(1)} %collective-permute-done.6.refs_1_, bf16[32,5120]{1,0:T(8,128)(2,1)S(1)} %collective-permute-done.7.refs_2_, ...), custom_call_target="tpu_custom_call" | custom-call | flops 1677721600 | bytes 11796480 | tf_op jit(solution)/shard_map/pallas_call | solution.py:225
  131.2 14.3 %all_to_all.33.returned_ref.down_ref = bf16[8,64,640]{2,1,0:T(8,128)(2,1)S(1)} all-to-all(bf16[8,64,640]{2,1,0:T(8,128)(2,1)S(1)} %get-tuple-element.80), channel_id=1, replica_groups={{0,2,4,6,8,10,12,14},{1,3,5,7,9,11,13,15},{16,18,20,22,24,26,28,30},{17..., dimensions={0} | all-to-all | bytes 1310720 | tf_op jit(solution)/shard_map/all_to_all | solution.py:42
  156.9 4.4 %collective-permute-done.16.refs_6_ = bf16[32,5120]{1,0:T(8,128)(2,1)S(1)} collective-permute-done((bf16[32,5120]{1,0:T(8,128)(2,1)S(1)}, bf16[32,5120]{1,0:T(8,128)(2,1)S(1)}, u32[]{:S(2)}, u32[]{:S(2)}) %collective-permute-start.16) | collective-permute-done | bytes 327712 | tf_op jit(solution)/shard_map/ppermute | solution.py:34
  168.3 5.1 %collective-permute-done.19.refs_5_ = bf16[32,5120]{1,0:T(8,128)(2,1)S(1)} collective-permute-done((bf16[32,5120]{1,0:T(8,128)(2,1)S(1)}, bf16[32,5120]{1,0:T(8,128)(2,1)S(1)}, u32[]{:S(2)}, u32[]{:S(2)}) %collective-permute-start.19) | collective-permute-done | bytes 327712 | tf_op jit(solution)/shard_map/ppermute | solution.py:34
  173.4 7.4 %shard_map.101 = (bf16[8,32,640]{2,1,0:T(8,128)(2,1)S(1)}, f32[256,640]{1,0:T(8,128)S(1)}, bf16[256,5120]{1,0:T(8,128)(2,1)}) custom-call(s32[9]{0:T(128)S(1)} %copy-done.24, bf16[32,5120]{1,0:T(8,128)(2,1)S(1)} %get-tuple-element.83.refs_0_, bf16[32,5120]{1,0:T(8,128)(2,1)S(1)} %collective-permute-done.14.refs_1_, ...), custom_call_target="tpu_custom_call" | custom-call | flops 1677721600 | bytes 11796480 | tf_op jit(solution)/shard_map/pallas_call | solution.py:225
  182.5 6.6 %shard_map.103 = (bf16[1,32,5120]{2,1,0:T(8,128)(2,1)S(1)}, bf16[1,32,5120]{2,1,0:T(8,128)(2,1)S(1)}, bf16[2,32,5120]{2,1,0:T(8,128)(2,1)}, bf16[1,32,5120]{2,1,...) custom-call(s32[9]{0:T(128)S(1)} %copy-done.24, ...), custom_call_target="tpu_custom_call" | custom-call | flops 1677721600 | bytes 9175040 | tf_op jit(solution)/shard_map/pallas_call | solution.py:299
  199.6 5.8 %shard_map.104 = (bf16[1,320,1280]{2,1,0:T(8,128)(2,1)}, bf16[1,320,1280]{2,1,0:T(8,128)(2,1)}, bf16[1,320,1280]{2,1,0:T(8,128)(2,1)}, bf16[1,320,1280]{2,1,0:T(8,128)(2,1)S(1)}) custom-call(s32[4]{0:T(128)S(1)} %pad_add_fusion.place_ref, bf16[256,5120]{1,0:T(8,128)(2,1)} %get-tuple-element.92.inputs_ref, ...), custom_call_target="tpu_custom_call" | custom-call | flops 1677721600 | bytes 13107200 | tf_op jit(solution)/shard_map/pallas_call | solution.py:344
  226.3 15.9 %all_to_all.34.down_ref.returned_ref = bf16[8,64,640]{2,1,0:T(8,128)(2,1)S(1)} all-to-all(bf16[8,64,640]{2,1,0:T(8,128)(2,1)S(1)} %shard_map.105), channel_id=1, replica_groups={{0,2,4,6,8,10,12,14},{1,3,5,7,9,11,13,15},{16,18,20,22,24,26,28,30},{17..., dimensions={0} | all-to-all | bytes 1310720 | tf_op jit(solution)/shard_map/all_to_all | solution.py:42
  245.0 9.8 %collective-permute-done.30 = bf16[1,320,1280]{2,1,0:T(8,128)(2,1)} collective-permute-done((bf16[1,320,1280]{2,1,0:T(8,128)(2,1)}, bf16[1,320,1280]{2,1,0:T(8,128)(2,1)}, u32[]{:S(2)}, u32[]{:S(2)}) %collective-permute-start.30) | collective-permute-done | bytes 819232 | tf_op jit(solution)/shard_map/ppermute | solution.py:34
  255.9 6.1 %shard_map.107 = (bf16[1,320,640]{2,1,0:T(8,128)(2,1)}, bf16[2,320,640]{2,1,0:T(8,128)(2,1)}, bf16[2,320,640]{2,1,0:T(8,128)(2,1)}) custom-call(s32[5]{0:T(128)} %stack.119.place_ref, bf16[256,5120]{1,0:T(8,128)(2,1)} %copy-done.2, bf16[256,5120]{1,0:T(8,128)(2,1)} %collective-permute-done.28.sibling_ref, bf16[320,256]{1,0:T(8,128)(2,1)} %copy-done.8, ...), custom_call_target="tpu_custom_call" | custom-call | flops 1048576000 | bytes 9011200 | tf_op jit(solution)/shard_map/pallas_call | solution.py:344
  271.2 5.0 %shard_map.108 = (bf16[1,320,640]{2,1,0:T(8,128)(2,1)}, bf16[1,320,640]{2,1,0:T(8,128)(2,1)}, bf16[1,320,640]{2,1,0:T(8,128)(2,1)}) custom-call(s32[3]{0:T(128)} %pad_add_fusion.1.place_ref, bf16[256,5120]{1,0:T(8,128)(2,1)} %copy-done.2, bf16[256,5120]{1,0:T(8,128)(2,1)} %collective-permute-done.28.sibling_ref, bf16[320,256]{1,0:T(8,128)(2,1)} %copy-done.8, ...), custom_call_target="tpu_custom_call" | custom-call | flops 629145600 | bytes 5406720 | tf_op jit(solution)/shard_map/pallas_call | solution.py:344
  276.2 6.2 %collective-permute-done.36 = bf16[320,640]{1,0:T(8,128)(2,1)S(1)} collective-permute-done((bf16[320,640]{1,0:T(8,128)(2,1)S(1)}, bf16[320,640]{1,0:T(8,128)(2,1)S(1)}, u32[]{:S(2)}, u32[]{:S(2)}) %collective-permute-start.36) | collective-permute-done | bytes 409632 | tf_op jit(solution)/shard_map/ppermute | solution.py:34
  292.4 6.1 %collective-permute-done.38 = bf16[1,320,640]{2,1,0:T(8,128)(2,1)S(1)} collective-permute-done((bf16[1,320,640]{2,1,0:T(8,128)(2,1)S(1)}, bf16[1,320,640]{2,1,0:T(8,128)(2,1)S(1)}, u32[]{:S(2)}, u32[]{:S(2)}) %collective-permute-start.38) | collective-permute-done | bytes 409632 | tf_op jit(solution)/shard_map/ppermute | solution.py:34
  (189 shorter events, 129.9 us)
Async XLA Ops:
  2.0 12.1 %all-to-all-start = ((s32[8,1,64]{2,1,0:T(1,128)}), s32[8,1,64]{2,1,0:T(1,128)S(1)}, u32[]{:S(2)}, u32[]{:S(2)}) async-start(s32[8,1,64]{2,1,0:T(1,128)} %broadcast_in_dim.19), calls=%async_computation | async-start | bytes 8192 | tf_op jit(solution)/shard_map/all_to_all | solution.py:486
  13.5 32.4 %collective-permute-start = (bf16[256,5120]{1,0:T(8,128)(2,1)S(1)}, bf16[256,5120]{1,0:T(8,128)(2,1)}, u32[]{:S(2)}, u32[]{:S(2)}) collective-permute-start(bf16[256,5120]{1,0:T(8,128)(2,1)S(1)} %shard_map.95), channel_id=1, source_target_pairs={{0,1},{1,0},{2,3},{3,2},{4,5},{5,4},{6,7},{7,6},{8,9},{9,8},{10,11... | collective-permute-start | bytes 7864328 | tf_op jit(solution)/shard_map/ppermute | solution.py:38
  13.6 110.9 %collective-permute-start.13 = (bf16[2,320,5120]{2,1,0:T(8,128)(2,1)}, bf16[2,320,5120]{2,1,0:T(8,128)(2,1)}, u32[]{:S(2)}, u32[]{:S(2)}) collective-permute-start(bf16[2,320,5120]{2,1,0:T(8,128)(2,1)} %bitcast.16.refs_8_.weight_ref), channel_id=1, source_target_pairs={{0,1},{1,0},{2,3},{3,2},{4,5},{5,4},{6,7},{7,6},{8,9},{9,8},{10,11... | collective-permute-start | bytes 19660808 | tf_op jit(solution)/shard_map/ppermute | solution.py:38
  38.8 25.5 %all-to-all-start.2 = ((bf16[16,64,640]{2,1,0:T(8,128)(2,1)}), bf16[16,64,640]{2,1,0:T(8,128)(2,1)}, u32[]{:S(2)}, u32[]{:S(2)}) async-start(bf16[16,64,640]{2,1,0:T(8,128)(2,1)} %bitcast.44), calls=%async_computation.2 | async-start | bytes 2621440 | tf_op jit(solution)/shard_map/all_to_all | solution.py:510
  51.8 26.1 %collective-permute-start.2 = (bf16[2,32,5120]{2,1,0:T(8,128)(2,1)}, bf16[2,32,5120]{2,1,0:T(8,128)(2,1)S(1)}, u32[]{:S(2)}, u32[]{:S(2)}) collective-permute-start(bf16[2,32,5120]{2,1,0:T(8,128)(2,1)} %get-tuple-element.69), channel_id=1, source_target_pairs={{0,4},{1,5},{2,6},{3,7},{4,8},{5,9},{6,10},{7,11},{8,12},{9,13},{1... | collective-permute-start | bytes 1966088 | tf_op jit(solution)/shard_map/ppermute | solution.py:34
  53.3 24.6 %collective-permute-start.3 = (bf16[2,32,5120]{2,1,0:T(8,128)(2,1)}, bf16[2,32,5120]{2,1,0:T(8,128)(2,1)S(1)}, u32[]{:S(2)}, u32[]{:S(2)}) collective-permute-start(bf16[2,32,5120]{2,1,0:T(8,128)(2,1)} %get-tuple-element.70), channel_id=1, source_target_pairs={{0,12},{1,13},{2,14},{3,15},{4,0},{5,1},{6,2},{7,3},{8,4},{9,5},{1... | collective-permute-start | bytes 1966088 | tf_op jit(solution)/shard_map/ppermute | solution.py:34
  55.1 18.4 %collective-permute-start.1 = (bf16[1,32,5120]{2,1,0:T(8,128)(2,1)}, bf16[1,32,5120]{2,1,0:T(8,128)(2,1)S(1)}, u32[]{:S(2)}, u32[]{:S(2)}) collective-permute-start(bf16[1,32,5120]{2,1,0:T(8,128)(2,1)} %get-tuple-element.68), channel_id=1, source_target_pairs={{0,2},{1,3},{2,0},{3,1},{4,6},{5,7},{6,4},{7,5},{8,10},{9,11},{10,... | collective-permute-start | bytes 983048 | tf_op jit(solution)/shard_map/ppermute | solution.py:34
  67.6 18.3 %all-to-all-start.3 = ((bf16[8,2,32,640]{3,2,1,0:T(8,128)(2,1)}), bf16[8,2,32,640]{3,2,1,0:T(8,128)(2,1)S(1)}, u32[]{:S(2)}, u32[]{:S(2)}) async-start(bf16[8,2,32,640]{3,2,1,0:T(8,128)(2,1)} %bitcast.15), calls=%async_computation.3 | async-start | bytes 1310720 | tf_op jit(solution)/shard_map/all_to_all | solution.py:515
  97.4 11.8 %collective-permute-start.8 = (bf16[32,5120]{1,0:T(8,128)(2,1)}, bf16[32,5120]{1,0:T(8,128)(2,1)S(1)}, u32[]{:S(2)}, u32[]{:S(2)}) collective-permute-start(bf16[32,5120]{1,0:T(8,128)(2,1)} %get-tuple-element.77.refs_0_), channel_id=1, source_target_pairs={{0,4},{1,5},{2,6},{3,7},{4,8},{5,9},{6,10},{7,11},{8,12},{9,13},{1... | collective-permute-start | bytes 983048 | tf_op jit(solution)/shard_map/ppermute | solution.py:34
  98.8 15.0 %collective-permute-start.10 = (bf16[32,5120]{1,0:T(8,128)(2,1)}, bf16[32,5120]{1,0:T(8,128)(2,1)S(1)}, u32[]{:S(2)}, u32[]{:S(2)}) collective-permute-start(bf16[32,5120]{1,0:T(8,128)(2,1)} %get-tuple-element.77.refs_0_), channel_id=1, source_target_pairs={{0,8},{1,9},{2,10},{3,11},{4,12},{5,13},{6,14},{7,15},{8,0},{9,1},... | collective-permute-start | bytes 983048 | tf_op jit(solution)/shard_map/ppermute | solution.py:34
  151.8 13.0 %collective-permute-start.18 = (bf16[32,5120]{1,0:T(8,128)(2,1)S(1)}, bf16[32,5120]{1,0:T(8,128)(2,1)S(1)}, u32[]{:S(2)}, u32[]{:S(2)}) collective-permute-start(bf16[32,5120]{1,0:T(8,128)(2,1)S(1)} %get-tuple-element.83.refs_0_), channel_id=1, source_target_pairs={{0,8},{1,9},{2,10},{3,11},{4,12},{5,13},{6,14},{7,15},{8,0},{9,1},... | collective-permute-start | bytes 983048 | tf_op jit(solution)/shard_map/ppermute | solution.py:34
  180.8 18.7 %collective-permute-start.24 = (bf16[256,5120]{1,0:T(8,128)(2,1)}, bf16[256,5120]{1,0:T(8,128)(2,1)}, u32[]{:S(2)}, u32[]{:S(2)}) collective-permute-start(bf16[256,5120]{1,0:T(8,128)(2,1)} %get-tuple-element.92.inputs_ref), channel_id=1, source_target_pairs={{0,1},{1,0},{2,3},{3,2},{4,5},{5,4},{6,7},{7,6},{8,9},{9,8},{10,11... | collective-permute-start | bytes 7864328 | tf_op jit(solution)/shard_map/ppermute | solution.py:38
  191.3 18.5 %collective-permute-start.22 = (bf16[2,32,5120]{2,1,0:T(8,128)(2,1)}, bf16[2,32,5120]{2,1,0:T(8,128)(2,1)S(1)}, u32[]{:S(2)}, u32[]{:S(2)}) collective-permute-start(bf16[2,32,5120]{2,1,0:T(8,128)(2,1)} %get-tuple-element.90), channel_id=1, source_target_pairs={{0,4},{1,5},{2,6},{3,7},{4,8},{5,9},{6,10},{7,11},{8,12},{9,13},{1... | collective-permute-start | bytes 1966088 | tf_op jit(solution)/shard_map/ppermute | solution.py:34
  191.3 18.5 %collective-permute-start.23 = (bf16[2,32,5120]{2,1,0:T(8,128)(2,1)}, bf16[2,32,5120]{2,1,0:T(8,128)(2,1)S(1)}, u32[]{:S(2)}, u32[]{:S(2)}) collective-permute-start(bf16[2,32,5120]{2,1,0:T(8,128)(2,1)} %get-tuple-element.91), channel_id=1, source_target_pairs={{0,12},{1,13},{2,14},{3,15},{4,0},{5,1},{6,2},{7,3},{8,4},{9,5},{1... | collective-permute-start | bytes 1966088 | tf_op jit(solution)/shard_map/ppermute | solution.py:34
  199.4 55.7 %collective-permute-start.28 = (bf16[256,5120]{1,0:T(8,128)(2,1)}, bf16[256,5120]{1,0:T(8,128)(2,1)}, u32[]{:S(2)}, u32[]{:S(2)}) collective-permute-start(bf16[256,5120]{1,0:T(8,128)(2,1)} %copy-done.2), channel_id=1, source_target_pairs={{0,1},{1,0},{2,3},{3,2},{4,5},{5,4},{6,7},{7,6},{8,9},{9,8},{10,11... | collective-permute-start | bytes 7864328 | tf_op jit(solution)/shard_map/ppermute | solution.py:38
  212.6 12.5 %collective-permute-start.27 = (bf16[1,32,5120]{2,1,0:T(8,128)(2,1)S(1)}, bf16[1,32,5120]{2,1,0:T(8,128)(2,1)S(1)}, u32[]{:S(2)}, u32[]{:S(2)}) collective-permute-start(bf16[1,32,5120]{2,1,0:T(8,128)(2,1)S(1)} %add_convert_fusion.2), channel_id=1, source_target_pairs={{0,2},{1,3},{2,0},{3,1},{4,6},{5,7},{6,4},{7,5},{8,10},{9,11},{10,... | collective-permute-start | bytes 983048 | tf_op jit(solution)/shard_map/ppermute | solution.py:34
  215.9 29.1 %collective-permute-start.29 = (bf16[1,320,1280]{2,1,0:T(8,128)(2,1)}, bf16[1,320,1280]{2,1,0:T(8,128)(2,1)}, u32[]{:S(2)}, u32[]{:S(2)}) collective-permute-start(bf16[1,320,1280]{2,1,0:T(8,128)(2,1)} %get-tuple-element.95), channel_id=1, source_target_pairs={{0,64},{16,80},{32,96},{48,112},{64,0},{80,16},{96,32},{112,48},{1... | collective-permute-start | bytes 2457608 | tf_op jit(solution)/shard_map/ppermute | solution.py:34
  219.4 35.4 %collective-permute-start.30 = (bf16[1,320,1280]{2,1,0:T(8,128)(2,1)}, bf16[1,320,1280]{2,1,0:T(8,128)(2,1)}, u32[]{:S(2)}, u32[]{:S(2)}) collective-permute-start(bf16[1,320,1280]{2,1,0:T(8,128)(2,1)} %get-tuple-element.96), channel_id=1, source_target_pairs={{0,32},{16,48},{32,64},{48,80},{64,96},{80,112},{96,0},{112,16},{1... | collective-permute-start | bytes 2457608 | tf_op jit(solution)/shard_map/ppermute | solution.py:34
  221.8 33.4 %collective-permute-start.31 = (bf16[1,320,1280]{2,1,0:T(8,128)(2,1)}, bf16[1,320,1280]{2,1,0:T(8,128)(2,1)}, u32[]{:S(2)}, u32[]{:S(2)}) collective-permute-start(bf16[1,320,1280]{2,1,0:T(8,128)(2,1)} %get-tuple-element.97), channel_id=1, source_target_pairs={{0,96},{16,112},{32,0},{48,16},{64,32},{80,48},{96,64},{112,80},{1... | collective-permute-start | bytes 2457608 | tf_op jit(solution)/shard_map/ppermute | solution.py:34
  261.9 14.3 %collective-permute-start.33 = (bf16[1,320,640]{2,1,0:T(8,128)(2,1)}, bf16[1,320,640]{2,1,0:T(8,128)(2,1)S(1)}, u32[]{:S(2)}, u32[]{:S(2)}) collective-permute-start(bf16[1,320,640]{2,1,0:T(8,128)(2,1)} %get-tuple-element.110), channel_id=1, source_target_pairs={{0,16},{16,0},{32,48},{48,32},{64,80},{80,64},{96,112},{112,96},{1... | collective-permute-start | bytes 1228808 | tf_op jit(solution)/shard_map/ppermute | solution.py:34
  263.9 21.3 %collective-permute-start.34 = (bf16[2,320,640]{2,1,0:T(8,128)(2,1)}, bf16[2,320,640]{2,1,0:T(8,128)(2,1)S(1)}, u32[]{:S(2)}, u32[]{:S(2)}) collective-permute-start(bf16[2,320,640]{2,1,0:T(8,128)(2,1)} %get-tuple-element.111), channel_id=1, source_target_pairs={{0,32},{16,48},{32,64},{48,80},{64,96},{80,112},{96,0},{112,16},{1... | collective-permute-start | bytes 2457608 | tf_op jit(solution)/shard_map/ppermute | solution.py:34
  265.3 19.9 %collective-permute-start.35 = (bf16[2,320,640]{2,1,0:T(8,128)(2,1)}, bf16[2,320,640]{2,1,0:T(8,128)(2,1)}, u32[]{:S(2)}, u32[]{:S(2)}) collective-permute-start(bf16[2,320,640]{2,1,0:T(8,128)(2,1)} %get-tuple-element.112), channel_id=1, source_target_pairs={{0,96},{16,112},{32,0},{48,16},{64,32},{80,48},{96,64},{112,80},{1... | collective-permute-start | bytes 2457608 | tf_op jit(solution)/shard_map/ppermute | solution.py:34
  270.4 12.1 %collective-permute-start.36 = (bf16[320,640]{1,0:T(8,128)(2,1)S(1)}, bf16[320,640]{1,0:T(8,128)(2,1)S(1)}, u32[]{:S(2)}, u32[]{:S(2)}) collective-permute-start(bf16[320,640]{1,0:T(8,128)(2,1)S(1)} %select_convert_fusion), channel_id=1, source_target_pairs={{0,16},{16,0},{32,48},{48,32},{64,80},{80,64},{96,112},{112,96},{1... | collective-permute-start | bytes 1228808 | tf_op jit(solution)/shard_map/ppermute | solution.py:34
  288.8 11.5 %collective-permute-start.37 = (bf16[1,320,640]{2,1,0:T(8,128)(2,1)S(1)}, bf16[1,320,640]{2,1,0:T(8,128)(2,1)S(1)}, u32[]{:S(2)}, u32[]{:S(2)}) collective-permute-start(bf16[1,320,640]{2,1,0:T(8,128)(2,1)S(1)} %add_convert_fusion.1), channel_id=1, source_target_pairs={{0,64},{16,80},{32,96},{48,112},{64,0},{80,16},{96,32},{112,48},{1... | collective-permute-start | bytes 1228808 | tf_op jit(solution)/shard_map/ppermute | solution.py:34
  (54 other events, 528.9 us)

commit v4 on v3

--- a/solution.py
+++ b/solution.py
@@ -172,7 +172,7 @@
     )(place, context, out_proj, arrived)
 
 
-def forward(place, pieces, weight, sibling, head, extra=None):
+def forward(place, pieces, weight, sibling, head, extra):
     rows, width = pieces[0].shape
     cols = weight.shape[1]
     tile = 2560
@@ -213,26 +213,121 @@
             ).astype(bf16)
             for i in range(chips):
                 update_ref[i, :rows] = update[i * rows : (i + 1) * rows]
-            if extra is not None:
-                update_ref[:, rows:] = refs[chips + 2][...]
+            update_ref[:, rows:] = refs[chips + 2][...]
             slope_ref[...] = jnp.concatenate(
                 [jnp.where(first, slope_a, slope_b), jnp.where(first, slope_b, slope_a)], axis=1
             )
 
     weight_spec = pl.BlockSpec((1, cols, tile), lambda i, place: (head, 0, i))
-    extras = [] if extra is None else [extra]
-    update_shape = struct((chips, rows * (1 + len(extras)), 2 * cols), bf16)
+    update_shape = struct((chips, 2 * rows, 2 * cols), bf16)
     return call(
         body,
         (count,),
-        [columns(rows, tile)] * chips + [weight_spec] * 2 + [whole()] * len(extras),
+        [columns(rows, tile)] * chips + [weight_spec] * 2 + [whole()],
         [whole()] * 2 + [columns(half, tile)],
         [update_shape, struct((half, 2 * cols), f32), struct((half, width), bf16)],
         [pltpu.VMEM((half, cols), f32)] * 2,
         flops=4 * half * width * cols,
         moved=4 * width * cols + 4 * half * width,
         limit=24,
-    )(place, *pieces, weight, sibling, *extras)
+    )(place, *pieces, weight, sibling, extra)
+
+
+def forward_backward(place, pieces, weight, sibling, head, down):
+    rows, width = pieces[0].shape
+    cols = weight.shape[1]
+    tile = 2560
+    half = chips * rows
+    count = width // tile
+
+    def body(place_ref, *refs):
+        piece_refs, (mine_ref, sibling_ref, down_ref) = refs[:chips], refs[chips : chips + 3]
+        update_ref, mine_t_ref, theirs_t_ref, gathered_ref = refs[chips + 3 : chips + 7]
+        out_refs = refs[chips + 7 : -2]
+        mine_acc, sibling_acc = refs[-2:]
+        step = pl.program_id(0)
+
+        @pl.when(step < count)
+        def _():
+            for i in range(chips):
+                gathered_ref[block_rows(place_ref[i], rows), :] = piece_refs[i][...]
+            left = gathered_ref[...]
+            mine = matmul(left, mine_ref[0], 1, 1)
+            theirs = matmul(left, sibling_ref[0], 1, 1)
+
+            @pl.when(step == 0)
+            def _():
+                mine_acc[...] = mine
+                sibling_acc[...] = theirs
+
+            @pl.when(step > 0)
+            def _():
+                mine_acc[...] += mine
+                sibling_acc[...] += theirs
+
+        @pl.when(step == count - 1)
+        def _():
+            first = place_ref[chips] == 0
+            down_all = jnp.concatenate([down_ref[i, rows:] for i in range(chips)], axis=0).astype(f32)
+            low, high = down_all[:, :cols], down_all[:, cols:]
+
+            def results(acc, down_cols, out_t_ref):
+                pre_act = acc[...]
+                sigmoid = 1.0 / (1.0 + jnp.exp(-pre_act))
+                d_act = down_cols * (sigmoid * (1.0 + pre_act * (1.0 - sigmoid)))
+                acc[...] = d_act
+                out_t_ref[...] = d_act.T.astype(bf16)
+                return pre_act * sigmoid
+
+            update_a = results(mine_acc, jnp.where(first, low, high), mine_t_ref)
+            update_b = results(sibling_acc, jnp.where(first, high, low), theirs_t_ref)
+            update = jnp.concatenate(
+                [jnp.where(first, update_a, update_b), jnp.where(first, update_b, update_a)], axis=1
+            ).astype(bf16)
+            for i in range(chips):
+                update_ref[i] = update[i * rows : (i + 1) * rows]
+
+        @pl.when(step >= count)
+        def _():
+            def ordered(ref):
+                parts = [ref[block_rows(place_ref[i], rows), :] for i in range(chips)]
+                return jnp.concatenate(parts, axis=0).astype(bf16)
+
+            total = matmul(ordered(mine_acc), mine_ref[0])
+            total = total + matmul(ordered(sibling_acc), sibling_ref[0])
+            store_groups(out_refs, total.astype(bf16), rows)
+
+    def there(i):
+        return jnp.minimum(i, count - 1)
+
+    def back(i):
+        return jnp.where(i < count, count - 1, 2 * count - 1 - i)
+
+    def both_ways(i):
+        return jnp.where(i < count, i, 2 * count - 1 - i)
+
+    weight_spec = pl.BlockSpec((1, cols, tile), lambda i, place: (head, 0, both_ways(i)))
+    return call(
+        body,
+        (2 * count,),
+        [pl.BlockSpec((rows, tile), lambda i, place: (0, there(i)))] * chips
+        + [weight_spec] * 2
+        + [whole()],
+        [whole()] * 3
+        + [pl.BlockSpec((half, tile), lambda i, place: (0, there(i)))]
+        + [pl.BlockSpec((len(g), rows, tile), lambda i, place: (0, 0, back(i))) for g in groups],
+        [
+            struct((chips, rows, 2 * cols), bf16),
+            struct((cols, half), bf16),
+            struct((cols, half), bf16),
+            struct((half, width), bf16),
+        ]
+        + [struct((len(g), rows, width), bf16) for g in groups],
+        [pltpu.VMEM((half, cols), f32)] * 2,
+        flops=8 * half * width * cols,
+        moved=6 * width * cols + 6 * half * width,
+        limit=36,
+    )(place, *pieces, weight, sibling, down)
 
 
 def split_columns(place, values):
@@ -253,61 +348,30 @@
     )(place, values)
 
 
-def slope_product(place, down, slope, start):
+def slope_product(place, down, slope):
     half, both = slope.shape
     cols = both // 2
     rows = half // chips
 
-    def body(place_ref, down_ref, slope_ref, mine_ref, theirs_ref, mine_t_ref, theirs_t_ref):
-        d_act = jnp.concatenate([down_ref[i, start : start + rows] for i in range(chips)], axis=0)
+    def body(place_ref, down_ref, slope_ref, mine_ref, theirs_ref):
+        d_act = jnp.concatenate([down_ref[i, :rows] for i in range(chips)], axis=0)
         d_act = d_act.astype(f32) * slope_ref[...]
         first = place_ref[chips] == 0
         low, high = d_act[:, :cols], d_act[:, cols:]
-        mine = jnp.where(first, low, high)
-        theirs = jnp.where(first, high, low)
-        mine_ref[...] = mine.astype(bf16)
-        theirs_ref[...] = theirs.astype(bf16)
-        mine_t_ref[...] = mine.T.astype(bf16)
-        theirs_t_ref[...] = theirs.T.astype(bf16)
+        mine_ref[...] = jnp.where(first, low, high).T.astype(bf16)
+        theirs_ref[...] = jnp.where(first, high, low).T.astype(bf16)
 
     return call(
         body,
         (1,),
         [whole()] * 2,
-        [whole()] * 4,
-        [struct((half, cols), bf16)] * 2 + [struct((cols, half), bf16)] * 2,
+        [whole()] * 2,
+        [struct((cols, half), bf16)] * 2,
         moved=half * both * 8,
     )(place, down, slope)
 
 
-def backward(place, mine, theirs, weight, sibling, head):
-    half, cols = mine.shape
-    width = weight.shape[2]
-    rows = half // chips
-    tile = 2560
-
-    def body(place_ref, mine_ref, theirs_ref, weight_ref, sibling_ref, *out_refs):
-        def ordered(ref):
-            return jnp.concatenate([ref[block_rows(place_ref[i], rows), :] for i in range(chips)], axis=0)
-
-        total = matmul(ordered(mine_ref), weight_ref[0])
-        total = total + matmul(ordered(theirs_ref), sibling_ref[0])
-        total = total.astype(bf16)
-        store_groups(out_refs, total, rows)
-
-    weight_spec = pl.BlockSpec((1, cols, tile), lambda i, place: (head, 0, i))
-    return call(
-        body,
-        (width // tile,),
-        [whole()] * 2 + [weight_spec] * 2,
-        [group_columns(len(group), rows, tile) for group in groups],
-        [struct((len(group), rows, width), bf16) for group in groups],
-        flops=4 * half * width * cols,
-        moved=4 * width * cols + 2 * half * width,
-    )(place, mine, theirs, weight, sibling)
-
-
-def grad_blocks(targets, inputs, sibling_inputs, mine, sibling_mine, cols, groups, limit):
+def grad_blocks(place, targets, inputs, sibling_inputs, mine, sibling_mine, cols, groups, limit):
     half = inputs.shape[0]
     out_rows = mine.shape[0]
     count = len(targets)
@@ -318,7 +382,7 @@
         homes = {i: out_ref.at[n] for out_ref, group in zip(out_refs, groups) for n, i in enumerate(group)}
 
         def load(i):
-            part = block_rows(place_ref[i], cols)
+            part = block_rows(place_ref[targets[i]], cols)
             return [
                 pltpu.make_async_copy(
                     source.at[:, part], right_ref.at[i, pl.ds(j * half, half), :], in_sems.at[i, j]
@@ -356,7 +420,7 @@
         flops=4 * half * cols * out_rows * count,
         moved=4 * half * (cols + out_rows) * count + 4 * cols * out_rows * count,
         limit=limit,
-    )(jnp.stack(targets).astype(jnp.int32), inputs, sibling_inputs, mine, sibling_mine)
+    )(place, inputs, sibling_inputs, mine, sibling_mine)
 
 
 def mean_last(values):
@@ -380,7 +444,9 @@
     return call(
         body,
         (1,),
-        [whole()] * (3 + len(terms)),
+        [whole()]
+        + [pl.BlockSpec((1, rows, width), lambda i, place: (0, 0, 0))] * len(terms)
+        + [whole(), pl.BlockSpec((chips, 1, rows, cols), lambda i, place: (0, 0, 0, 0))],
         [whole()] * 2,
         [struct((rows, width), f32), struct((rows, width), bf16)],
         moved=rows * width * 20,
@@ -412,23 +478,24 @@
     )(place, state, returned, embeds)
 
 
-def last_state(place, state, returned):
+def both_states(place, rounded, state, returned):
     rows, width = state.shape
     cols = width // chips
 
-    def body(place_ref, state_ref, returned_ref, out_ref):
+    def body(place_ref, rounded_ref, state_ref, returned_ref, out_ref):
+        out_ref[0] = rounded_ref[...]
         for i in range(chips):
             part = slice(i * cols, (i + 1) * cols)
-            out_ref[:, part] = (state_ref[:, part] + returned_ref[i, rows:].astype(f32)).astype(bf16)
+            out_ref[1, :, part] = (state_ref[:, part] + returned_ref[i, rows:].astype(f32)).astype(bf16)
 
     return call(
         body,
         (1,),
-        [whole()] * 2,
+        [whole()] * 3,
         whole(),
-        struct((rows, width), bf16),
-        moved=rows * width * 8,
-    )(place, state, returned)
+        struct((2, rows, width), bf16),
+        moved=rows * width * 12,
+    )(place, rounded, state, returned)
 
 
 def carry_gradient(place, state_grad, state, terms, extra):
@@ -475,7 +542,12 @@
     head_count, _, head_cols = head_weight.shape
     weight = jnp.swapaxes(head_weight, 1, 2)
     vocab_rows, table_cols = embed_table.shape
-    place = jnp.stack([((my_z + dz) % 4) * 2 + (my_x_hi ^ dx) for dz, dx in steps] + [my_core])
+    place = jnp.stack(
+        [((my_z + dz) % 4) * 2 + (my_x_hi ^ dx) for dz, dx in steps]
+        + [my_core]
+        + [((my_y + dy) % 4) * 2 + (my_x_lo ^ dx) for dy, dx in steps]
+        + [(my_y + dy) % 4 for dy in range(4)]
+    )
     place = place.astype(jnp.int32)
 
     ids_here = next_ids.reshape(1, -1)
@@ -523,13 +595,14 @@
     state_1, inputs_1, rounded_0 = next_state(place, state_0, returned_0, embeds)
 
     pieces_1 = gather_chips(inputs_1)
-    update_1, slope_1, gathered_1 = forward(place, pieces_1, weight, sibling_weight, 1)
-    mine_1, theirs_1, mine_1_t, theirs_1_t = slope_product(place, returned_0, slope_1, tok_rows)
-    d_blocks = backward(place, mine_1, theirs_1, weight, sibling_weight, 1)
+    update_1, mine_1_t, theirs_1_t, gathered_1, *d_blocks = forward_backward(
+        place, pieces_1, weight, sibling_weight, 1, returned_0
+    )
 
     cols = model_width // dp_count
-    y_targets = [(my_y + dy) % 4 for dy in (2, 1, 3, 0)]
+    y_targets = [2 * chips + 1 + dy for dy in (2, 1, 3, 0)]
     products = grad_blocks(
+        place,
         y_targets,
         gathered_1,
         to_sibling(gathered_1),
@@ -544,20 +617,18 @@
 
     lower = carry_gradient(place, state_grad, state_1, d_terms, update_1)
     returned_1 = exchange(lower)
-    _, _, mine_0_t, theirs_0_t = slope_product(place, returned_1, slope_0, 0)
+    mine_0_t, theirs_0_t = slope_product(place, returned_1, slope_0)
     sibling_gathered_0, sibling_0_t = to_sibling(gathered_0), to_sibling(theirs_0_t)
 
     def made(chosen, mine_t):
-        targets = [
-            ((my_y + steps[i][0]) % 4) * 2 + (my_x_lo ^ steps[i][1]) for group in chosen for i in group
-        ]
+        targets = [chips + 1 + i for group in chosen for i in group]
         order = iter(range(len(targets)))
         places_of = [tuple(next(order) for _ in group) for group in chosen]
         return grad_blocks(
-            targets, gathered_0, sibling_gathered_0, mine_t, sibling_0_t, cols, places_of, 60
+            place, targets, gathered_0, sibling_gathered_0, mine_t, sibling_0_t, cols, places_of, 60
         )
 
-    mine_0_t, *y_terms = lax.optimization_barrier((mine_0_t, *y_terms))
+    mine_0_t, y_terms[1], y_terms[2] = lax.optimization_barrier((mine_0_t, y_terms[1], y_terms[2]))
     across, up, down = made([(5,), (2, 3), (6, 7)], mine_0_t)
     own, side, far = made([(0,), (1,), (4,)], after(mine_0_t, across))
     y_terms = lax.optimization_barrier((*y_terms, across))[:4]
@@ -565,15 +636,15 @@
     keep = jnp.where(my_x_lo == 0, y_total[:, :cols], y_total[:, cols:])
     give = jnp.where(my_x_lo == 0, y_total[:, cols:], y_total[:, :cols]).astype(bf16)
     given = send(give, "dp", 0, 1)
-    grad_terms, first_arrived, (own, side, far, given) = scatter_chips(
-        (own, side, up, far, across, down), "dp", (own, side, far, given)
+    states = both_states(place, rounded_0, state_1, returned_1)
+    grad_terms, _, (own, side, far, given, states) = scatter_chips(
+        (own, side, up, far, across, down), "dp", (own, side, far, given, states)
     )
     grad_0 = add(*[term[0] for term in grad_terms])
     grad_1 = keep + given.astype(f32)
 
-    rounded_1 = last_state(place, state_1, after(returned_1, *first_arrived))
     head_grad = jnp.swapaxes(jnp.stack([grad_0, grad_1]), 1, 2)
-    return (jnp.stack([rounded_0, rounded_1]), head_grad)
+    return (states, head_grad)
 
 
 def solution(mesh):

time: 304 us -> 289 us (0.951)
  blocking collectives: 42.9 us -> 29.1 us
  starting transfers between devices: 69.8 us -> 81.3 us
  Pallas kernels: 56.6 us -> 49.6 us
    all_to_all x2 -> x1, blocking collectives: 30.2 us -> 16.3 us  [exchange(): lax.all_to_all(values, 'tensor', split_axis=0, concat_axis=0, tiled=True,...]
    ppermute x33, waiting for transfers between devices: 79.2 us -> 70.8 us  [send(): return lax.ppermute(values, axis, chip_moves(axis, dz, dx))]
    pallas_call x2 -> x1, Pallas kernels: 14 us -> 6.54 us  [forward(): call(body, (count,), [columns(rows, tile)] * chips + [weight_spec] * 2 +...]
    all_to_all x0 -> x1, starting transfers between devices: none -> 6.89 us  [exchange(): lax.all_to_all(values, 'tensor', split_axis=0, concat_axis=0, tiled=True,...]
    all_to_all x0 -> x1, waiting for transfers between devices: none -> 5.29 us  [exchange(): lax.all_to_all(values, 'tensor', split_axis=0, concat_axis=0, tiled=True,...]
    ppermute x33, starting transfers between devices: 51 us -> 55.6 us  [send(): return lax.ppermute(values, axis, chip_moves(axis, dz, dx))]
    pallas_call x5 -> x4, Pallas kernels: 14.5 us -> 16.6 us  [the longest x1 10.5 us: forward_backward(): call(body, (2 * count,), [pl.BlockSpec((rows, tile), lambda i, place: (0,...]
    unnamed x72 -> x60, local copies, waits for them, and re-layouts: 9.7 us -> 8.5 us
  transfers between devices with their start and end apart: 42 -> 43, of which waited for: 29 -> 25; matrix products, arithmetic and copies ran while one was open for 7% -> 6% of each run, Pallas kernels for 12% -> 11%
where the time goes in v4:
time: 289 us; the launch traced here: 288 us
  waiting for transfers between devices  93.3 us (32%)
  starting transfers between devices  81.3 us (28%)
  Pallas kernels  49.6 us (17%)
  blocking collectives  29.1 us (10%)
  local copies, waits for them, and re-layouts  20.2 us (7%)
  other arithmetic  9.21 us (3%)
  matrix products  4.03 us (1%)
    ppermute x33, waiting for transfers between devices, send(): return lax.ppermute(values, axis, chip_moves(axis, dz, dx))  70.8 us
    ppermute x33, starting transfers between devices, send(): return lax.ppermute(values, axis, chip_moves(axis, dz, dx))  55.6 us
    all_to_all x1, blocking collectives, exchange(): lax.all_to_all(values, 'tensor', split_axis=0, concat_axis=0, tiled=True,...  16.3 us
    pallas_call x3, Pallas kernels, grad_blocks(): call(body, (1,), [in_hbm()] * 2 + [whole()] * 2, [in_hbm()] * len(groups)...  15.2 us
    all_to_all x1, blocking collectives, on_device(): lax.all_to_all(requests, 'tensor', split_axis=0, concat_axis=0, tiled=True)  12.8 us
    pallas_call x1, Pallas kernels, forward_backward(): call(body, (2 * count,), [pl.BlockSpec((rows, tile), lambda i, place: (0,...  10.5 us
    all_to_all x1, waiting for transfers between devices, on_device(): lax.all_to_all(found_rows, 'tensor', split_axis=0, concat_axis=0, tiled=T...  8.94 us
    gather x1, local copies, waits for them, and re-layouts, on_device(): found_rows = jnp.take(embed_table, wanted, axis=0, mode='clip')  8.8 us
  transfers between devices with their start and end apart: 43, of which 25 were waited for; matrix products, arithmetic and copies ran while one was open for 6% of the time, Pallas kernels for 11%

profile of v4, /device:TPU:4, one launch (start us, length us, event | category | flops | bytes accessed | tf_op | source)
XLA Modules:
  0.0 287.8 jit_solution(934463595495370502)
XLA Ops:
  2.0 5.1 %all-to-all-start = ((s32[8,1,64]{2,1,0:T(1,128)}), s32[8,1,64]{2,1,0:T(1,128)S(1)}, u32[]{:S(2)}, u32[]{:S(2)}) async-start(s32[8,1,64]{2,1,0:T(1,128)} %broadcast_in_dim.19), calls=%async_computation | async-start | bytes 8192 | tf_op jit(solution)/shard_map/all_to_all | solution.py:558
  16.4 12.8 %all_to_all.32 = s32[16,1,64]{2,1,0:T(1,128)S(1)} all-to-all(s32[16,1,64]{2,1,0:T(1,128)S(1)} %bitcast.43), channel_id=1, replica_groups=mesh['dp'=8,'tensor'=16] {'tensor'}, dimensions={0} | all-to-all | bytes 8192 | tf_op jit(solution)/shard_map/all_to_all | solution.py:577
  30.0 8.8 %gather_fusion = bf16[1024,640]{1,0:T(8,128)(2,1)} fusion(bf16[4752,640]{1,0:T(8,128)(2,1)} %param.13, s32[1024]{0:T(1024)S(1)} %broadcast_clamp_fusion), kind=kCustom, calls=%fused_computation | custom fusion | bytes 2625536 | tf_op jit(solution)/shard_map/jit(_take)/gather | solution.py:578
  38.8 7.1 %all-to-all-start.2 = ((bf16[16,64,640]{2,1,0:T(8,128)(2,1)}), bf16[16,64,640]{2,1,0:T(8,128)(2,1)}, u32[]{:S(2)}, u32[]{:S(2)}) async-start(bf16[16,64,640]{2,1,0:T(8,128)(2,1)} %bitcast.40), calls=%async_computation.2 | async-start | bytes 2621440 | tf_op jit(solution)/shard_map/all_to_all | solution.py:582
  45.9 5.9 %shard_map.96 = (bf16[1,32,5120]{2,1,0:T(8,128)(2,1)}, bf16[1,32,5120]{2,1,0:T(8,128)(2,1)}, bf16[2,32,5120]{2,1,0:T(8,128)(2,1)}, bf16[1,32,5120]{2,1,0:T(8,128...) custom-call(s32[21]{0:T(128)} %copy-done.18, bf16[512,512]{1,0:T(8,128)(2,1)} %context_ref.1, ...), custom_call_target="tpu_custom_call" | custom-call | flops 1342177280 | bytes 10485760 | tf_op jit(solution)/shard_map/pallas_call | solution.py:164
  55.3 8.9 %all-to-all-done.2 = bf16[16,64,640]{2,1,0:T(8,128)(2,1)} async-done(((bf16[16,64,640]{2,1,0:T(8,128)(2,1)}), bf16[16,64,640]{2,1,0:T(8,128)(2,1)}, u32[]{:S(2)}, u32[]{:S(2)}) %all-to-all-start.2) | async-done | bytes 1310752 | tf_op jit(solution)/shard_map/all_to_all | solution.py:582
  67.6 5.9 %all-to-all-start.3 = ((bf16[8,2,32,640]{3,2,1,0:T(8,128)(2,1)}), bf16[8,2,32,640]{3,2,1,0:T(8,128)(2,1)S(1)}, u32[]{:S(2)}, u32[]{:S(2)}) async-start(bf16[8,2,32,640]{3,2,1,0:T(8,128)(2,1)} %bitcast.27), calls=%async_computation.3 | async-start | bytes 1310720 | tf_op jit(solution)/shard_map/all_to_all | solution.py:587
  73.5 4.4 %collective-permute-done.2.refs_1_ = bf16[2,32,5120]{2,1,0:T(8,128)(2,1)S(1)} collective-permute-done((bf16[2,32,5120]{2,1,0:T(8,128)(2,1)}, bf16[2,32,5120]{2,1,0:T(8,128)(2,1)S(1)}, u32[]{:S(2)}, u32[]{:S(2)}) %collective-permute-start.2) | collective-permute-done | bytes 655392 | tf_op jit(solution)/shard_map/ppermute | solution.py:34
  80.9 5.4 %all-to-all-done.3.refs_6_.embeds_ref = bf16[8,2,32,640]{3,2,1,0:T(8,128)(2,1)S(1)} async-done(((bf16[8,2,32,640]{3,2,1,0:T(8,128)(2,1)}), bf16[8,2,32,640]{3,2,1,0:T(8,128)(2,1)S(1)}, u32[]{:S(2)}, u32[]{:S(2)}) %all-to-all-start.3) | async-done | bytes 655392 | tf_op jit(solution)/shard_map/all_to_all | solution.py:587
  100.4 11.7 %collective-permute-done.8.refs_6_ = bf16[32,5120]{1,0:T(8,128)(2,1)S(1)} collective-permute-done((bf16[32,5120]{1,0:T(8,128)(2,1)}, bf16[32,5120]{1,0:T(8,128)(2,1)S(1)}, u32[]{:S(2)}, u32[]{:S(2)}) %collective-permute-start.8) | collective-permute-done | bytes 327712 | tf_op jit(solution)/shard_map/ppermute | solution.py:34
  122.7 6.5 %shard_map.99 = (bf16[8,64,640]{2,1,0:T(8,128)(2,1)S(1)}, f32[256,640]{1,0:T(8,128)S(1)}, bf16[256,5120]{1,0:T(8,128)(2,1)S(1)}) custom-call(s32[21]{0:T(128)S(1)} %copy-done.19, bf16[32,5120]{1,0:T(8,128)(2,1)S(1)} %copy-done.17, bf16[32,5120]{1,0:T(8,128)(2,1)S(1)} %collective-permute-done.6.refs_1_, bf16[32,5120]{1,0:T(8,128)(2,1)S(1)} %collective-permute-done.7.refs_2_, ...), custom_call_target="tpu_custom_call" | custom-call | flops 1677721600 | bytes 11796480 | tf_op jit(solution)/shard_map/pallas_call | solution.py:223
  130.1 16.3 %all_to_all.33.returned_ref.refs_10_ = bf16[8,64,640]{2,1,0:T(8,128)(2,1)S(1)} all-to-all(bf16[8,64,640]{2,1,0:T(8,128)(2,1)S(1)} %get-tuple-element.76), channel_id=1, replica_groups={{0,2,4,6,8,10,12,14},{1,3,5,7,9,11,13,15},{16,18,20,22,24,26,28,30},{17..., dimensions={0} | all-to-all | bytes 1310720 | tf_op jit(solution)/shard_map/all_to_all | solution.py:42
  153.4 5.2 %collective-permute-done.17.refs_6_ = bf16[32,5120]{1,0:T(8,128)(2,1)S(1)} collective-permute-done((bf16[32,5120]{1,0:T(8,128)(2,1)S(1)}, bf16[32,5120]{1,0:T(8,128)(2,1)S(1)}, u32[]{:S(2)}, u32[]{:S(2)}) %collective-permute-start.17) | collective-permute-done | bytes 327712 | tf_op jit(solution)/shard_map/ppermute | solution.py:34
  159.8 4.5 %collective-permute-done.19.refs_4_ = bf16[32,5120]{1,0:T(8,128)(2,1)S(1)} collective-permute-done((bf16[32,5120]{1,0:T(8,128)(2,1)S(1)}, bf16[32,5120]{1,0:T(8,128)(2,1)S(1)}, u32[]{:S(2)}, u32[]{:S(2)}) %collective-permute-start.19) | collective-permute-done | bytes 327712 | tf_op jit(solution)/shard_map/ppermute | solution.py:34
  168.5 4.3 %collective-permute-done.20.refs_5_ = bf16[32,5120]{1,0:T(8,128)(2,1)S(1)} collective-permute-done((bf16[32,5120]{1,0:T(8,128)(2,1)S(1)}, bf16[32,5120]{1,0:T(8,128)(2,1)S(1)}, u32[]{:S(2)}, u32[]{:S(2)}) %collective-permute-start.20) | collective-permute-done | bytes 327712 | tf_op jit(solution)/shard_map/ppermute | solution.py:34
  173.6 10.5 %shard_map.101 = (bf16[8,32,640]{2,1,0:T(8,128)(2,1)S(1)}, bf16[320,256]{1,0:T(8,128)(2,1)S(1)}, bf16[320,256]{1,0:T(8,128)(2,1)S(1)}, bf16[256,5120]{1,0:T(8,12...) custom-call(s32[21]{0:T(128)S(1)} %copy-done.19, ...), custom_call_target="tpu_custom_call" | custom-call | flops 3355443200 | bytes 17694720 | tf_op jit(solution)/shard_map/pallas_call | solution.py:310
  191.5 4.1 %shard_map.102 = (bf16[1,320,1280]{2,1,0:T(8,128)(2,1)S(1)}, bf16[1,320,1280]{2,1,0:T(8,128)(2,1)}, bf16[1,320,1280]{2,1,0:T(8,128)(2,1)}, bf16[1,320,1280]{2,1,0:T(8,128)(2,1)S(1)}) custom-call(s32[21]{0:T(128)S(1)} %copy-done.19, bf16[256,5120]{1,0:T(8,128)(2,1)S(1)} %get-tuple-element.84.inputs_ref, ...), custom_call_target="tpu_custom_call" | custom-call | flops 1677721600 | bytes 13107200 | tf_op jit(solution)/shard_map/pallas_call | solution.py:408
  218.3 6.9 %all-to-all-start.5 = ((bf16[8,64,640]{2,1,0:T(8,128)(2,1)}), bf16[8,64,640]{2,1,0:T(8,128)(2,1)S(1)}, u32[]{:S(2)}, u32[]{:S(2)}) async-start(bf16[8,64,640]{2,1,0:T(8,128)(2,1)} %copy-done.7), calls=%async_computation.5 | async-start | bytes 1310720 | tf_op jit(solution)/shard_map/all_to_all | solution.py:42
  228.7 5.3 %all-to-all-done.5.down_ref.returned_ref = bf16[8,64,640]{2,1,0:T(8,128)(2,1)S(1)} async-done(((bf16[8,64,640]{2,1,0:T(8,128)(2,1)}), bf16[8,64,640]{2,1,0:T(8,128)(2,1)S(1)}, u32[]{:S(2)}, u32[]{:S(2)}) %all-to-all-start.5) | async-done | bytes 655392 | tf_op jit(solution)/shard_map/all_to_all | solution.py:42
  238.2 6.0 %shard_map.105 = (bf16[1,320,640]{2,1,0:T(8,128)(2,1)}, bf16[2,320,640]{2,1,0:T(8,128)(2,1)}, bf16[2,320,640]{2,1,0:T(8,128)(2,1)}) custom-call(s32[21]{0:T(128)} %copy-done.18, bf16[256,5120]{1,0:T(8,128)(2,1)} %copy-done.2, bf16[256,5120]{1,0:T(8,128)(2,1)} %collective-permute-done.14.sibling_ref, bf16[320,256]{1,0:T(8,128)(2,1)} %copy-done.11, ...), custom_call_target="tpu_custom_call" | custom-call | flops 1048576000 | bytes 9011200 | tf_op jit(solution)/shard_map/pallas_call | solution.py:408
  253.5 5.8 %collective-permute-start.36 = (bf16[320,640]{1,0:T(8,128)(2,1)S(1)}, bf16[320,640]{1,0:T(8,128)(2,1)S(1)}, u32[]{:S(2)}, u32[]{:S(2)}) collective-permute-start(bf16[320,640]{1,0:T(8,128)(2,1)S(1)} %select_convert_fusion), channel_id=1, source_target_pairs={{0,16},{16,0},{32,48},{48,32},{64,80},{80,64},{96,112},{112,96},{1... | collective-permute-start | bytes 1228808 | tf_op jit(solution)/shard_map/ppermute | solution.py:34
  260.8 5.0 %shard_map.106 = (bf16[1,320,640]{2,1,0:T(8,128)(2,1)}, bf16[1,320,640]{2,1,0:T(8,128)(2,1)}, bf16[1,320,640]{2,1,0:T(8,128)(2,1)}) custom-call(s32[21]{0:T(128)} %copy-done.18, bf16[256,5120]{1,0:T(8,128)(2,1)} %copy-done.2, bf16[256,5120]{1,0:T(8,128)(2,1)} %collective-permute-done.14.sibling_ref, bf16[320,256]{1,0:T(8,128)(2,1)} %copy-done.11, ...), custom_call_target="tpu_custom_call" | custom-call | flops 629145600 | bytes 5406720 | tf_op jit(solution)/shard_map/pallas_call | solution.py:408
  266.6 5.6 %collective-permute-done.32 = bf16[1,320,640]{2,1,0:T(8,128)(2,1)S(1)} collective-permute-done((bf16[1,320,640]{2,1,0:T(8,128)(2,1)S(1)}, bf16[1,320,640]{2,1,0:T(8,128)(2,1)S(1)}, u32[]{:S(2)}, u32[]{:S(2)}) %collective-permute-start.32) | collective-permute-done | bytes 409632 | tf_op jit(solution)/shard_map/ppermute | solution.py:34
  276.2 6.6 %collective-permute-done.38 = bf16[1,320,640]{2,1,0:T(8,128)(2,1)S(1)} collective-permute-done((bf16[1,320,640]{2,1,0:T(8,128)(2,1)S(1)}, bf16[1,320,640]{2,1,0:T(8,128)(2,1)S(1)}, u32[]{:S(2)}, u32[]{:S(2)}) %collective-permute-start.38) | collective-permute-done | bytes 409632 | tf_op jit(solution)/shard_map/ppermute | solution.py:34
  (172 shorter events, 118.3 us)
Async XLA Ops:
  2.0 12.1 %all-to-all-start = ((s32[8,1,64]{2,1,0:T(1,128)}), s32[8,1,64]{2,1,0:T(1,128)S(1)}, u32[]{:S(2)}, u32[]{:S(2)}) async-start(s32[8,1,64]{2,1,0:T(1,128)} %broadcast_in_dim.19), calls=%async_computation | async-start | bytes 8192 | tf_op jit(solution)/shard_map/all_to_all | solution.py:558
  13.5 32.3 %collective-permute-start = (bf16[256,5120]{1,0:T(8,128)(2,1)S(1)}, bf16[256,5120]{1,0:T(8,128)(2,1)}, u32[]{:S(2)}, u32[]{:S(2)}) collective-permute-start(bf16[256,5120]{1,0:T(8,128)(2,1)S(1)} %shard_map.95), channel_id=1, source_target_pairs={{0,1},{1,0},{2,3},{3,2},{4,5},{5,4},{6,7},{7,6},{8,9},{9,8},{10,11... | collective-permute-start | bytes 7864328 | tf_op jit(solution)/shard_map/ppermute | solution.py:38
  13.6 109.0 %collective-permute-start.13 = (bf16[2,320,5120]{2,1,0:T(8,128)(2,1)}, bf16[2,320,5120]{2,1,0:T(8,128)(2,1)}, u32[]{:S(2)}, u32[]{:S(2)}) collective-permute-start(bf16[2,320,5120]{2,1,0:T(8,128)(2,1)} %bitcast.28.refs_8_), channel_id=1, source_target_pairs={{0,1},{1,0},{2,3},{3,2},{4,5},{5,4},{6,7},{7,6},{8,9},{9,8},{10,11... | collective-permute-start | bytes 19660808 | tf_op jit(solution)/shard_map/ppermute | solution.py:38
  38.8 25.5 %all-to-all-start.2 = ((bf16[16,64,640]{2,1,0:T(8,128)(2,1)}), bf16[16,64,640]{2,1,0:T(8,128)(2,1)}, u32[]{:S(2)}, u32[]{:S(2)}) async-start(bf16[16,64,640]{2,1,0:T(8,128)(2,1)} %bitcast.40), calls=%async_computation.2 | async-start | bytes 2621440 | tf_op jit(solution)/shard_map/all_to_all | solution.py:582
  51.8 26.1 %collective-permute-start.2 = (bf16[2,32,5120]{2,1,0:T(8,128)(2,1)}, bf16[2,32,5120]{2,1,0:T(8,128)(2,1)S(1)}, u32[]{:S(2)}, u32[]{:S(2)}) collective-permute-start(bf16[2,32,5120]{2,1,0:T(8,128)(2,1)} %get-tuple-element.64), channel_id=1, source_target_pairs={{0,4},{1,5},{2,6},{3,7},{4,8},{5,9},{6,10},{7,11},{8,12},{9,13},{1... | collective-permute-start | bytes 1966088 | tf_op jit(solution)/shard_map/ppermute | solution.py:34
  53.3 24.6 %collective-permute-start.3 = (bf16[2,32,5120]{2,1,0:T(8,128)(2,1)}, bf16[2,32,5120]{2,1,0:T(8,128)(2,1)S(1)}, u32[]{:S(2)}, u32[]{:S(2)}) collective-permute-start(bf16[2,32,5120]{2,1,0:T(8,128)(2,1)} %get-tuple-element.65), channel_id=1, source_target_pairs={{0,12},{1,13},{2,14},{3,15},{4,0},{5,1},{6,2},{7,3},{8,4},{9,5},{1... | collective-permute-start | bytes 1966088 | tf_op jit(solution)/shard_map/ppermute | solution.py:34
  55.0 18.4 %collective-permute-start.1 = (bf16[1,32,5120]{2,1,0:T(8,128)(2,1)}, bf16[1,32,5120]{2,1,0:T(8,128)(2,1)S(1)}, u32[]{:S(2)}, u32[]{:S(2)}) collective-permute-start(bf16[1,32,5120]{2,1,0:T(8,128)(2,1)} %get-tuple-element.63), channel_id=1, source_target_pairs={{0,2},{1,3},{2,0},{3,1},{4,6},{5,7},{6,4},{7,5},{8,10},{9,11},{10,... | collective-permute-start | bytes 983048 | tf_op jit(solution)/shard_map/ppermute | solution.py:34
  67.6 18.8 %all-to-all-start.3 = ((bf16[8,2,32,640]{3,2,1,0:T(8,128)(2,1)}), bf16[8,2,32,640]{3,2,1,0:T(8,128)(2,1)S(1)}, u32[]{:S(2)}, u32[]{:S(2)}) async-start(bf16[8,2,32,640]{3,2,1,0:T(8,128)(2,1)} %bitcast.27), calls=%async_computation.3 | async-start | bytes 1310720 | tf_op jit(solution)/shard_map/all_to_all | solution.py:587
  78.0 12.1 %collective-permute-start.5 = (bf16[1,32,5120]{2,1,0:T(8,128)(2,1)S(1)}, bf16[1,32,5120]{2,1,0:T(8,128)(2,1)}, u32[]{:S(2)}, u32[]{:S(2)}) collective-permute-start(bf16[1,32,5120]{2,1,0:T(8,128)(2,1)S(1)} %add_convert_fusion.4), channel_id=1, source_target_pairs={{0,2},{1,3},{2,0},{3,1},{4,6},{5,7},{6,4},{7,5},{8,10},{9,11},{10,... | collective-permute-start | bytes 983048 | tf_op jit(solution)/shard_map/ppermute | solution.py:34
  94.6 17.5 %collective-permute-start.8 = (bf16[32,5120]{1,0:T(8,128)(2,1)}, bf16[32,5120]{1,0:T(8,128)(2,1)S(1)}, u32[]{:S(2)}, u32[]{:S(2)}) collective-permute-start(bf16[32,5120]{1,0:T(8,128)(2,1)} %get-tuple-element.71.refs_0_), channel_id=1, source_target_pairs={{0,4},{1,5},{2,6},{3,7},{4,8},{5,9},{6,10},{7,11},{8,12},{9,13},{1... | collective-permute-start | bytes 983048 | tf_op jit(solution)/shard_map/ppermute | solution.py:34
  94.6 17.5 %collective-permute-start.7 = (bf16[32,5120]{1,0:T(8,128)(2,1)}, bf16[32,5120]{1,0:T(8,128)(2,1)S(1)}, u32[]{:S(2)}, u32[]{:S(2)}) collective-permute-start(bf16[32,5120]{1,0:T(8,128)(2,1)} %get-tuple-element.71.refs_0_), channel_id=1, source_target_pairs={{0,12},{1,13},{2,14},{3,15},{4,0},{5,1},{6,2},{7,3},{8,4},{9,5},{1... | collective-permute-start | bytes 983048 | tf_op jit(solution)/shard_map/ppermute | solution.py:34
  97.8 14.3 %collective-permute-start.6 = (bf16[32,5120]{1,0:T(8,128)(2,1)}, bf16[32,5120]{1,0:T(8,128)(2,1)S(1)}, u32[]{:S(2)}, u32[]{:S(2)}) collective-permute-start(bf16[32,5120]{1,0:T(8,128)(2,1)} %get-tuple-element.71.refs_0_), channel_id=1, source_target_pairs={{0,2},{1,3},{2,0},{3,1},{4,6},{5,7},{6,4},{7,5},{8,10},{9,11},{10,... | collective-permute-start | bytes 983048 | tf_op jit(solution)/shard_map/ppermute | solution.py:34
  100.4 11.7 %collective-permute-start.10 = (bf16[32,5120]{1,0:T(8,128)(2,1)}, bf16[32,5120]{1,0:T(8,128)(2,1)S(1)}, u32[]{:S(2)}, u32[]{:S(2)}) collective-permute-start(bf16[32,5120]{1,0:T(8,128)(2,1)} %get-tuple-element.71.refs_0_), channel_id=1, source_target_pairs={{0,8},{1,9},{2,10},{3,11},{4,12},{5,13},{6,14},{7,15},{8,0},{9,1},... | collective-permute-start | bytes 983048 | tf_op jit(solution)/shard_map/ppermute | solution.py:34
  184.2 18.6 %collective-permute-start.23 = (bf16[2,32,5120]{2,1,0:T(8,128)(2,1)S(1)}, bf16[2,32,5120]{2,1,0:T(8,128)(2,1)S(1)}, u32[]{:S(2)}, u32[]{:S(2)}) collective-permute-start(bf16[2,32,5120]{2,1,0:T(8,128)(2,1)S(1)} %get-tuple-element.82), channel_id=1, source_target_pairs={{0,4},{1,5},{2,6},{3,7},{4,8},{5,9},{6,10},{7,11},{8,12},{9,13},{1... | collective-permute-start | bytes 1966088 | tf_op jit(solution)/shard_map/ppermute | solution.py:34
  184.2 18.6 %collective-permute-start.24 = (bf16[2,32,5120]{2,1,0:T(8,128)(2,1)S(1)}, bf16[2,32,5120]{2,1,0:T(8,128)(2,1)S(1)}, u32[]{:S(2)}, u32[]{:S(2)}) collective-permute-start(bf16[2,32,5120]{2,1,0:T(8,128)(2,1)S(1)} %get-tuple-element.83), channel_id=1, source_target_pairs={{0,12},{1,13},{2,14},{3,15},{4,0},{5,1},{6,2},{7,3},{8,4},{9,5},{1... | collective-permute-start | bytes 1966088 | tf_op jit(solution)/shard_map/ppermute | solution.py:34
  191.4 45.3 %collective-permute-start.14 = (bf16[256,5120]{1,0:T(8,128)(2,1)S(1)}, bf16[256,5120]{1,0:T(8,128)(2,1)}, u32[]{:S(2)}, u32[]{:S(2)}) collective-permute-start(bf16[256,5120]{1,0:T(8,128)(2,1)S(1)} %get-tuple-element.74.inputs_ref), channel_id=1, source_target_pairs={{0,1},{1,0},{2,3},{3,2},{4,5},{5,4},{6,7},{7,6},{8,9},{9,8},{10,11... | collective-permute-start | bytes 7864328 | tf_op jit(solution)/shard_map/ppermute | solution.py:38
  208.5 28.2 %collective-permute-start.29 = (bf16[1,320,1280]{2,1,0:T(8,128)(2,1)}, bf16[1,320,1280]{2,1,0:T(8,128)(2,1)}, u32[]{:S(2)}, u32[]{:S(2)}) collective-permute-start(bf16[1,320,1280]{2,1,0:T(8,128)(2,1)} %get-tuple-element.88), channel_id=1, source_target_pairs={{0,32},{16,48},{32,64},{48,80},{64,96},{80,112},{96,0},{112,16},{1... | collective-permute-start | bytes 2457608 | tf_op jit(solution)/shard_map/ppermute | solution.py:34
  210.7 26.0 %collective-permute-start.30 = (bf16[1,320,1280]{2,1,0:T(8,128)(2,1)}, bf16[1,320,1280]{2,1,0:T(8,128)(2,1)}, u32[]{:S(2)}, u32[]{:S(2)}) collective-permute-start(bf16[1,320,1280]{2,1,0:T(8,128)(2,1)} %get-tuple-element.89), channel_id=1, source_target_pairs={{0,96},{16,112},{32,0},{48,16},{64,32},{80,48},{96,64},{112,80},{1... | collective-permute-start | bytes 2457608 | tf_op jit(solution)/shard_map/ppermute | solution.py:34
  218.3 15.7 %all-to-all-start.5 = ((bf16[8,64,640]{2,1,0:T(8,128)(2,1)}), bf16[8,64,640]{2,1,0:T(8,128)(2,1)S(1)}, u32[]{:S(2)}, u32[]{:S(2)}) async-start(bf16[8,64,640]{2,1,0:T(8,128)(2,1)} %copy-done.7), calls=%async_computation.5 | async-start | bytes 1310720 | tf_op jit(solution)/shard_map/all_to_all | solution.py:42
  225.2 22.9 %collective-permute-start.35 = (bf16[1,320,1280]{2,1,0:T(8,128)(2,1)}, bf16[1,320,1280]{2,1,0:T(8,128)(2,1)}, u32[]{:S(2)}, u32[]{:S(2)}) collective-permute-start(bf16[1,320,1280]{2,1,0:T(8,128)(2,1)} %copy-done.21), channel_id=1, source_target_pairs={{0,64},{16,80},{32,96},{48,112},{64,0},{80,16},{96,32},{112,48},{1... | collective-permute-start | bytes 2457608 | tf_op jit(solution)/shard_map/ppermute | solution.py:34
  248.1 24.0 %collective-permute-start.33 = (bf16[2,320,640]{2,1,0:T(8,128)(2,1)}, bf16[2,320,640]{2,1,0:T(8,128)(2,1)}, u32[]{:S(2)}, u32[]{:S(2)}) collective-permute-start(bf16[2,320,640]{2,1,0:T(8,128)(2,1)} %get-tuple-element.102), channel_id=1, source_target_pairs={{0,32},{16,48},{32,64},{48,80},{64,96},{80,112},{96,0},{112,16},{1... | collective-permute-start | bytes 2457608 | tf_op jit(solution)/shard_map/ppermute | solution.py:34
  249.3 22.9 %collective-permute-start.34 = (bf16[2,320,640]{2,1,0:T(8,128)(2,1)}, bf16[2,320,640]{2,1,0:T(8,128)(2,1)}, u32[]{:S(2)}, u32[]{:S(2)}) collective-permute-start(bf16[2,320,640]{2,1,0:T(8,128)(2,1)} %get-tuple-element.103), channel_id=1, source_target_pairs={{0,96},{16,112},{32,0},{48,16},{64,32},{80,48},{96,64},{112,80},{1... | collective-permute-start | bytes 2457608 | tf_op jit(solution)/shard_map/ppermute | solution.py:34
  253.5 13.1 %collective-permute-start.36 = (bf16[320,640]{1,0:T(8,128)(2,1)S(1)}, bf16[320,640]{1,0:T(8,128)(2,1)S(1)}, u32[]{:S(2)}, u32[]{:S(2)}) collective-permute-start(bf16[320,640]{1,0:T(8,128)(2,1)S(1)} %select_convert_fusion), channel_id=1, source_target_pairs={{0,16},{16,0},{32,48},{48,32},{64,80},{80,64},{96,112},{112,96},{1... | collective-permute-start | bytes 1228808 | tf_op jit(solution)/shard_map/ppermute | solution.py:34
  259.3 12.9 %collective-permute-start.32 = (bf16[1,320,640]{2,1,0:T(8,128)(2,1)S(1)}, bf16[1,320,640]{2,1,0:T(8,128)(2,1)S(1)}, u32[]{:S(2)}, u32[]{:S(2)}) collective-permute-start(bf16[1,320,640]{2,1,0:T(8,128)(2,1)S(1)} %copy-done.29), channel_id=1, source_target_pairs={{0,16},{16,0},{32,48},{48,32},{64,80},{80,64},{96,112},{112,96},{1... | collective-permute-start | bytes 1228808 | tf_op jit(solution)/shard_map/ppermute | solution.py:34
  (49 other events, 575.8 us)

commit v5 on v4

--- a/solution.py
+++ b/solution.py
@@ -528,6 +528,14 @@
     )(place, state_grad, state_grad, state, *terms, extra)
 
 
+def swap_ids(ids, axis):
+    count, width = ids.shape
+    tiles = jnp.pad(ids, ((0, 0), (0, 128 - width)))
+    tiles = jnp.broadcast_to(tiles[:, None, :], (count, 8, 128))
+    tiles = lax.all_to_all(tiles, axis, split_axis=0, concat_axis=0, tiled=True)
+    return tiles[:, 0, :width]
+
+
 def on_device(
     context, residual, out_proj, final_gain, next_ids, embed_table, head_weight, state_grad
 ):
@@ -555,9 +563,7 @@
     group_ids = dp_count * id_count
     capacity = 2 * group_ids // tensor_count
     places_all = tensor_count * capacity
-    group = lax.all_to_all(
-        jnp.broadcast_to(ids_here, (dp_count, id_count)), "dp", split_axis=0, concat_axis=0, tiled=True
-    )
+    group = swap_ids(jnp.broadcast_to(ids_here, (dp_count, id_count)), "dp")
     group = group.reshape(group_ids)
     owners = group // vocab_rows
     rows_in = group - owners * vocab_rows
@@ -574,7 +580,7 @@
     context = after(context, group)
     arrived = to_sibling(project(place, context, out_proj, tok_rows, True))
 
-    wanted = lax.all_to_all(requests, "tensor", split_axis=0, concat_axis=0, tiled=True)
+    wanted = swap_ids(requests, "tensor")
     found_rows = jnp.take(embed_table, wanted, axis=0, mode="clip")
     arrived = after(arrived, found_rows)
     blocks = project(place, context, out_proj, tok_rows, False, arrived)

time: 289 us -> 288 us (level)
  no operation moved by 1% of the time
where the time goes in v5:
time: 288 us; the launch traced here: 287 us
  waiting for transfers between devices  93.4 us (32%)
  starting transfers between devices  81.9 us (28%)
  Pallas kernels  49.6 us (17%)
  blocking collectives  29.2 us (10%)
  local copies, waits for them, and re-layouts  19.8 us (7%)
  other arithmetic  7.89 us (3%)
  matrix products  4.04 us (1%)
    ppermute x33, waiting for transfers between devices, send(): return lax.ppermute(values, axis, chip_moves(axis, dz, dx))  70.8 us
    ppermute x33, starting transfers between devices, send(): return lax.ppermute(values, axis, chip_moves(axis, dz, dx))  55.3 us
    all_to_all x1, blocking collectives, exchange(): lax.all_to_all(values, 'tensor', split_axis=0, concat_axis=0, tiled=True,...  16.3 us
    pallas_call x3, Pallas kernels, grad_blocks(): call(body, (1,), [in_hbm()] * 2 + [whole()] * 2, [in_hbm()] * len(groups)...  15.2 us
    all_to_all x1, blocking collectives, swap_ids(): tiles = lax.all_to_all(tiles, axis, split_axis=0, concat_axis=0, tiled=True)  13 us
    pallas_call x1, Pallas kernels, forward_backward(): call(body, (2 * count,), [pl.BlockSpec((rows, tile), lambda i, place: (0,...  10.5 us
    all_to_all x1, waiting for transfers between devices, on_device(): lax.all_to_all(found_rows, 'tensor', split_axis=0, concat_axis=0, tiled=T...  9.01 us
    gather x1, local copies, waits for them, and re-layouts, on_device(): found_rows = jnp.take(embed_table, wanted, axis=0, mode='clip')  8.8 us
  transfers between devices with their start and end apart: 43, of which 25 were waited for; matrix products, arithmetic and copies ran while one was open for 6% of the time, Pallas kernels for 11%

profile of v5, /device:TPU:4, one launch (start us, length us, event | category | flops | bytes accessed | tf_op | source)
XLA Modules:
  0.0 287.0 jit_solution(1157928436540058509)
XLA Ops:
  2.0 5.1 %all-to-all-start = ((s32[8,8,128]{2,1,0:T(8,128)}), s32[8,8,128]{2,1,0:T(8,128)S(1)}, u32[]{:S(2)}, u32[]{:S(2)}) async-start(s32[8,8,128]{2,1,0:T(8,128)} %broadcast_in_dim.20), calls=%async_computation | async-start | bytes 65536 | tf_op jit(solution)/shard_map/all_to_all | solution.py:535
  15.3 13.0 %all_to_all.30 = s32[16,8,128]{2,1,0:T(8,128)S(1)} all-to-all(s32[16,8,128]{2,1,0:T(8,128)S(1)} %broadcast_in_dim.25), channel_id=1, replica_groups=mesh['dp'=8,'tensor'=16] {'tensor'}, dimensions={0} | all-to-all | bytes 131072 | tf_op jit(solution)/shard_map/all_to_all | solution.py:535
  28.4 8.8 %gather_fusion = bf16[1024,640]{1,0:T(8,128)(2,1)} fusion(bf16[4752,640]{1,0:T(8,128)(2,1)} %param.13, s32[1024]{0:T(1024)S(1)} %broadcast_clamp_fusion), kind=kCustom, calls=%fused_computation | custom fusion | bytes 2625536 | tf_op jit(solution)/shard_map/jit(_take)/gather | solution.py:584
  37.2 7.9 %all-to-all-start.2 = ((bf16[16,64,640]{2,1,0:T(8,128)(2,1)}), bf16[16,64,640]{2,1,0:T(8,128)(2,1)}, u32[]{:S(2)}, u32[]{:S(2)}) async-start(bf16[16,64,640]{2,1,0:T(8,128)(2,1)} %bitcast.39), calls=%async_computation.2 | async-start | bytes 2621440 | tf_op jit(solution)/shard_map/all_to_all | solution.py:588
  45.1 6.0 %shard_map.96 = (bf16[1,32,5120]{2,1,0:T(8,128)(2,1)}, bf16[1,32,5120]{2,1,0:T(8,128)(2,1)}, bf16[2,32,5120]{2,1,0:T(8,128)(2,1)}, bf16[1,32,5120]{2,1,0:T(8,128...) custom-call(s32[21]{0:T(128)} %copy-done.18, bf16[512,512]{1,0:T(8,128)(2,1)} %context_ref.1, ...), custom_call_target="tpu_custom_call" | custom-call | flops 1342177280 | bytes 10485760 | tf_op jit(solution)/shard_map/pallas_call | solution.py:164
  54.5 9.0 %all-to-all-done.2 = bf16[16,64,640]{2,1,0:T(8,128)(2,1)} async-done(((bf16[16,64,640]{2,1,0:T(8,128)(2,1)}), bf16[16,64,640]{2,1,0:T(8,128)(2,1)}, u32[]{:S(2)}, u32[]{:S(2)}) %all-to-all-start.2) | async-done | bytes 1310752 | tf_op jit(solution)/shard_map/all_to_all | solution.py:588
  66.8 5.9 %all-to-all-start.3 = ((bf16[8,2,32,640]{3,2,1,0:T(8,128)(2,1)}), bf16[8,2,32,640]{3,2,1,0:T(8,128)(2,1)S(1)}, u32[]{:S(2)}, u32[]{:S(2)}) async-start(bf16[8,2,32,640]{3,2,1,0:T(8,128)(2,1)} %bitcast.23), calls=%async_computation.3 | async-start | bytes 1310720 | tf_op jit(solution)/shard_map/all_to_all | solution.py:593
  72.7 4.4 %collective-permute-done.2.refs_1_ = bf16[2,32,5120]{2,1,0:T(8,128)(2,1)S(1)} collective-permute-done((bf16[2,32,5120]{2,1,0:T(8,128)(2,1)}, bf16[2,32,5120]{2,1,0:T(8,128)(2,1)S(1)}, u32[]{:S(2)}, u32[]{:S(2)}) %collective-permute-start.2) | collective-permute-done | bytes 655392 | tf_op jit(solution)/shard_map/ppermute | solution.py:34
  80.2 5.5 %all-to-all-done.3.refs_6_.embeds_ref = bf16[8,2,32,640]{3,2,1,0:T(8,128)(2,1)S(1)} async-done(((bf16[8,2,32,640]{3,2,1,0:T(8,128)(2,1)}), bf16[8,2,32,640]{3,2,1,0:T(8,128)(2,1)S(1)}, u32[]{:S(2)}, u32[]{:S(2)}) %all-to-all-start.3) | async-done | bytes 655392 | tf_op jit(solution)/shard_map/all_to_all | solution.py:593
  99.6 11.7 %collective-permute-done.8.refs_6_ = bf16[32,5120]{1,0:T(8,128)(2,1)S(1)} collective-permute-done((bf16[32,5120]{1,0:T(8,128)(2,1)}, bf16[32,5120]{1,0:T(8,128)(2,1)S(1)}, u32[]{:S(2)}, u32[]{:S(2)}) %collective-permute-start.8) | collective-permute-done | bytes 327712 | tf_op jit(solution)/shard_map/ppermute | solution.py:34
  121.9 6.5 %shard_map.99 = (bf16[8,64,640]{2,1,0:T(8,128)(2,1)S(1)}, f32[256,640]{1,0:T(8,128)S(1)}, bf16[256,5120]{1,0:T(8,128)(2,1)S(1)}) custom-call(s32[21]{0:T(128)S(1)} %copy-done.19, bf16[32,5120]{1,0:T(8,128)(2,1)S(1)} %copy-done.17, bf16[32,5120]{1,0:T(8,128)(2,1)S(1)} %collective-permute-done.6.refs_1_, bf16[32,5120]{1,0:T(8,128)(2,1)S(1)} %collective-permute-done.7.refs_2_, ...), custom_call_target="tpu_custom_call" | custom-call | flops 1677721600 | bytes 11796480 | tf_op jit(solution)/shard_map/pallas_call | solution.py:223
  129.3 16.3 %all_to_all.31.returned_ref.refs_10_ = bf16[8,64,640]{2,1,0:T(8,128)(2,1)S(1)} all-to-all(bf16[8,64,640]{2,1,0:T(8,128)(2,1)S(1)} %get-tuple-element.76), channel_id=1, replica_groups={{0,2,4,6,8,10,12,14},{1,3,5,7,9,11,13,15},{16,18,20,22,24,26,28,30},{17..., dimensions={0} | all-to-all | bytes 1310720 | tf_op jit(solution)/shard_map/all_to_all | solution.py:42
  152.7 5.1 %collective-permute-done.17.refs_6_ = bf16[32,5120]{1,0:T(8,128)(2,1)S(1)} collective-permute-done((bf16[32,5120]{1,0:T(8,128)(2,1)S(1)}, bf16[32,5120]{1,0:T(8,128)(2,1)S(1)}, u32[]{:S(2)}, u32[]{:S(2)}) %collective-permute-start.17) | collective-permute-done | bytes 327712 | tf_op jit(solution)/shard_map/ppermute | solution.py:34
  159.0 4.4 %collective-permute-done.19.refs_4_ = bf16[32,5120]{1,0:T(8,128)(2,1)S(1)} collective-permute-done((bf16[32,5120]{1,0:T(8,128)(2,1)S(1)}, bf16[32,5120]{1,0:T(8,128)(2,1)S(1)}, u32[]{:S(2)}, u32[]{:S(2)}) %collective-permute-start.19) | collective-permute-done | bytes 327712 | tf_op jit(solution)/shard_map/ppermute | solution.py:34
  167.8 4.2 %collective-permute-done.20.refs_5_ = bf16[32,5120]{1,0:T(8,128)(2,1)S(1)} collective-permute-done((bf16[32,5120]{1,0:T(8,128)(2,1)S(1)}, bf16[32,5120]{1,0:T(8,128)(2,1)S(1)}, u32[]{:S(2)}, u32[]{:S(2)}) %collective-permute-start.20) | collective-permute-done | bytes 327712 | tf_op jit(solution)/shard_map/ppermute | solution.py:34
  172.9 10.5 %shard_map.101 = (bf16[8,32,640]{2,1,0:T(8,128)(2,1)S(1)}, bf16[320,256]{1,0:T(8,128)(2,1)S(1)}, bf16[320,256]{1,0:T(8,128)(2,1)S(1)}, bf16[256,5120]{1,0:T(8,12...) custom-call(s32[21]{0:T(128)S(1)} %copy-done.19, ...), custom_call_target="tpu_custom_call" | custom-call | flops 3355443200 | bytes 17694720 | tf_op jit(solution)/shard_map/pallas_call | solution.py:310
  190.7 4.2 %shard_map.102 = (bf16[1,320,1280]{2,1,0:T(8,128)(2,1)S(1)}, bf16[1,320,1280]{2,1,0:T(8,128)(2,1)}, bf16[1,320,1280]{2,1,0:T(8,128)(2,1)}, bf16[1,320,1280]{2,1,0:T(8,128)(2,1)S(1)}) custom-call(s32[21]{0:T(128)S(1)} %copy-done.19, bf16[256,5120]{1,0:T(8,128)(2,1)S(1)} %get-tuple-element.84.inputs_ref, ...), custom_call_target="tpu_custom_call" | custom-call | flops 1677721600 | bytes 13107200 | tf_op jit(solution)/shard_map/pallas_call | solution.py:408
  217.5 6.9 %all-to-all-start.5 = ((bf16[8,64,640]{2,1,0:T(8,128)(2,1)}), bf16[8,64,640]{2,1,0:T(8,128)(2,1)S(1)}, u32[]{:S(2)}, u32[]{:S(2)}) async-start(bf16[8,64,640]{2,1,0:T(8,128)(2,1)} %copy-done.7), calls=%async_computation.5 | async-start | bytes 1310720 | tf_op jit(solution)/shard_map/all_to_all | solution.py:42
  228.0 5.3 %all-to-all-done.5.down_ref.returned_ref = bf16[8,64,640]{2,1,0:T(8,128)(2,1)S(1)} async-done(((bf16[8,64,640]{2,1,0:T(8,128)(2,1)}), bf16[8,64,640]{2,1,0:T(8,128)(2,1)S(1)}, u32[]{:S(2)}, u32[]{:S(2)}) %all-to-all-start.5) | async-done | bytes 655392 | tf_op jit(solution)/shard_map/all_to_all | solution.py:42
  237.4 6.0 %shard_map.105 = (bf16[1,320,640]{2,1,0:T(8,128)(2,1)}, bf16[2,320,640]{2,1,0:T(8,128)(2,1)}, bf16[2,320,640]{2,1,0:T(8,128)(2,1)}) custom-call(s32[21]{0:T(128)} %copy-done.18, bf16[256,5120]{1,0:T(8,128)(2,1)} %copy-done.2, bf16[256,5120]{1,0:T(8,128)(2,1)} %collective-permute-done.14.sibling_ref, bf16[320,256]{1,0:T(8,128)(2,1)} %copy-done.11, ...), custom_call_target="tpu_custom_call" | custom-call | flops 1048576000 | bytes 9011200 | tf_op jit(solution)/shard_map/pallas_call | solution.py:408
  252.7 5.7 %collective-permute-start.36 = (bf16[320,640]{1,0:T(8,128)(2,1)S(1)}, bf16[320,640]{1,0:T(8,128)(2,1)S(1)}, u32[]{:S(2)}, u32[]{:S(2)}) collective-permute-start(bf16[320,640]{1,0:T(8,128)(2,1)S(1)} %select_convert_fusion), channel_id=1, source_target_pairs={{0,16},{16,0},{32,48},{48,32},{64,80},{80,64},{96,112},{112,96},{1... | collective-permute-start | bytes 1228808 | tf_op jit(solution)/shard_map/ppermute | solution.py:34
  260.0 5.0 %shard_map.106 = (bf16[1,320,640]{2,1,0:T(8,128)(2,1)}, bf16[1,320,640]{2,1,0:T(8,128)(2,1)}, bf16[1,320,640]{2,1,0:T(8,128)(2,1)}) custom-call(s32[21]{0:T(128)} %copy-done.18, bf16[256,5120]{1,0:T(8,128)(2,1)} %copy-done.2, bf16[256,5120]{1,0:T(8,128)(2,1)} %collective-permute-done.14.sibling_ref, bf16[320,256]{1,0:T(8,128)(2,1)} %copy-done.11, ...), custom_call_target="tpu_custom_call" | custom-call | flops 629145600 | bytes 5406720 | tf_op jit(solution)/shard_map/pallas_call | solution.py:408
  265.9 5.6 %collective-permute-done.32 = bf16[1,320,640]{2,1,0:T(8,128)(2,1)S(1)} collective-permute-done((bf16[1,320,640]{2,1,0:T(8,128)(2,1)S(1)}, bf16[1,320,640]{2,1,0:T(8,128)(2,1)S(1)}, u32[]{:S(2)}, u32[]{:S(2)}) %collective-permute-start.32) | collective-permute-done | bytes 409632 | tf_op jit(solution)/shard_map/ppermute | solution.py:34
  275.3 6.6 %collective-permute-done.38 = bf16[1,320,640]{2,1,0:T(8,128)(2,1)S(1)} collective-permute-done((bf16[1,320,640]{2,1,0:T(8,128)(2,1)S(1)}, bf16[1,320,640]{2,1,0:T(8,128)(2,1)S(1)}, u32[]{:S(2)}, u32[]{:S(2)}) %collective-permute-start.38) | collective-permute-done | bytes 409632 | tf_op jit(solution)/shard_map/ppermute | solution.py:34
  (174 shorter events, 116.5 us)
Async XLA Ops:
  2.0 12.1 %all-to-all-start = ((s32[8,8,128]{2,1,0:T(8,128)}), s32[8,8,128]{2,1,0:T(8,128)S(1)}, u32[]{:S(2)}, u32[]{:S(2)}) async-start(s32[8,8,128]{2,1,0:T(8,128)} %broadcast_in_dim.20), calls=%async_computation | async-start | bytes 65536 | tf_op jit(solution)/shard_map/all_to_all | solution.py:535
  13.5 31.6 %collective-permute-start = (bf16[256,5120]{1,0:T(8,128)(2,1)S(1)}, bf16[256,5120]{1,0:T(8,128)(2,1)}, u32[]{:S(2)}, u32[]{:S(2)}) collective-permute-start(bf16[256,5120]{1,0:T(8,128)(2,1)S(1)} %shard_map.95), channel_id=1, source_target_pairs={{0,1},{1,0},{2,3},{3,2},{4,5},{5,4},{6,7},{7,6},{8,9},{9,8},{10,11... | collective-permute-start | bytes 7864328 | tf_op jit(solution)/shard_map/ppermute | solution.py:38
  13.6 108.2 %collective-permute-start.13 = (bf16[2,320,5120]{2,1,0:T(8,128)(2,1)}, bf16[2,320,5120]{2,1,0:T(8,128)(2,1)}, u32[]{:S(2)}, u32[]{:S(2)}) collective-permute-start(bf16[2,320,5120]{2,1,0:T(8,128)(2,1)} %bitcast.24.refs_8_), channel_id=1, source_target_pairs={{0,1},{1,0},{2,3},{3,2},{4,5},{5,4},{6,7},{7,6},{8,9},{9,8},{10,11... | collective-permute-start | bytes 19660808 | tf_op jit(solution)/shard_map/ppermute | solution.py:38
  37.2 26.3 %all-to-all-start.2 = ((bf16[16,64,640]{2,1,0:T(8,128)(2,1)}), bf16[16,64,640]{2,1,0:T(8,128)(2,1)}, u32[]{:S(2)}, u32[]{:S(2)}) async-start(bf16[16,64,640]{2,1,0:T(8,128)(2,1)} %bitcast.39), calls=%async_computation.2 | async-start | bytes 2621440 | tf_op jit(solution)/shard_map/all_to_all | solution.py:588
  51.1 26.0 %collective-permute-start.2 = (bf16[2,32,5120]{2,1,0:T(8,128)(2,1)}, bf16[2,32,5120]{2,1,0:T(8,128)(2,1)S(1)}, u32[]{:S(2)}, u32[]{:S(2)}) collective-permute-start(bf16[2,32,5120]{2,1,0:T(8,128)(2,1)} %get-tuple-element.64), channel_id=1, source_target_pairs={{0,4},{1,5},{2,6},{3,7},{4,8},{5,9},{6,10},{7,11},{8,12},{9,13},{1... | collective-permute-start | bytes 1966088 | tf_op jit(solution)/shard_map/ppermute | solution.py:34
  52.5 24.5 %collective-permute-start.3 = (bf16[2,32,5120]{2,1,0:T(8,128)(2,1)}, bf16[2,32,5120]{2,1,0:T(8,128)(2,1)S(1)}, u32[]{:S(2)}, u32[]{:S(2)}) collective-permute-start(bf16[2,32,5120]{2,1,0:T(8,128)(2,1)} %get-tuple-element.65), channel_id=1, source_target_pairs={{0,12},{1,13},{2,14},{3,15},{4,0},{5,1},{6,2},{7,3},{8,4},{9,5},{1... | collective-permute-start | bytes 1966088 | tf_op jit(solution)/shard_map/ppermute | solution.py:34
  54.3 18.4 %collective-permute-start.1 = (bf16[1,32,5120]{2,1,0:T(8,128)(2,1)}, bf16[1,32,5120]{2,1,0:T(8,128)(2,1)S(1)}, u32[]{:S(2)}, u32[]{:S(2)}) collective-permute-start(bf16[1,32,5120]{2,1,0:T(8,128)(2,1)} %get-tuple-element.63), channel_id=1, source_target_pairs={{0,2},{1,3},{2,0},{3,1},{4,6},{5,7},{6,4},{7,5},{8,10},{9,11},{10,... | collective-permute-start | bytes 983048 | tf_op jit(solution)/shard_map/ppermute | solution.py:34
  66.8 18.8 %all-to-all-start.3 = ((bf16[8,2,32,640]{3,2,1,0:T(8,128)(2,1)}), bf16[8,2,32,640]{3,2,1,0:T(8,128)(2,1)S(1)}, u32[]{:S(2)}, u32[]{:S(2)}) async-start(bf16[8,2,32,640]{3,2,1,0:T(8,128)(2,1)} %bitcast.23), calls=%async_computation.3 | async-start | bytes 1310720 | tf_op jit(solution)/shard_map/all_to_all | solution.py:593
  77.2 12.1 %collective-permute-start.5 = (bf16[1,32,5120]{2,1,0:T(8,128)(2,1)S(1)}, bf16[1,32,5120]{2,1,0:T(8,128)(2,1)}, u32[]{:S(2)}, u32[]{:S(2)}) collective-permute-start(bf16[1,32,5120]{2,1,0:T(8,128)(2,1)S(1)} %add_convert_fusion.4), channel_id=1, source_target_pairs={{0,2},{1,3},{2,0},{3,1},{4,6},{5,7},{6,4},{7,5},{8,10},{9,11},{10,... | collective-permute-start | bytes 983048 | tf_op jit(solution)/shard_map/ppermute | solution.py:34
  93.8 17.5 %collective-permute-start.8 = (bf16[32,5120]{1,0:T(8,128)(2,1)}, bf16[32,5120]{1,0:T(8,128)(2,1)S(1)}, u32[]{:S(2)}, u32[]{:S(2)}) collective-permute-start(bf16[32,5120]{1,0:T(8,128)(2,1)} %get-tuple-element.71.refs_0_), channel_id=1, source_target_pairs={{0,4},{1,5},{2,6},{3,7},{4,8},{5,9},{6,10},{7,11},{8,12},{9,13},{1... | collective-permute-start | bytes 983048 | tf_op jit(solution)/shard_map/ppermute | solution.py:34
  93.8 17.5 %collective-permute-start.7 = (bf16[32,5120]{1,0:T(8,128)(2,1)}, bf16[32,5120]{1,0:T(8,128)(2,1)S(1)}, u32[]{:S(2)}, u32[]{:S(2)}) collective-permute-start(bf16[32,5120]{1,0:T(8,128)(2,1)} %get-tuple-element.71.refs_0_), channel_id=1, source_target_pairs={{0,12},{1,13},{2,14},{3,15},{4,0},{5,1},{6,2},{7,3},{8,4},{9,5},{1... | collective-permute-start | bytes 983048 | tf_op jit(solution)/shard_map/ppermute | solution.py:34
  97.0 14.3 %collective-permute-start.6 = (bf16[32,5120]{1,0:T(8,128)(2,1)}, bf16[32,5120]{1,0:T(8,128)(2,1)S(1)}, u32[]{:S(2)}, u32[]{:S(2)}) collective-permute-start(bf16[32,5120]{1,0:T(8,128)(2,1)} %get-tuple-element.71.refs_0_), channel_id=1, source_target_pairs={{0,2},{1,3},{2,0},{3,1},{4,6},{5,7},{6,4},{7,5},{8,10},{9,11},{10,... | collective-permute-start | bytes 983048 | tf_op jit(solution)/shard_map/ppermute | solution.py:34
  99.6 11.7 %collective-permute-start.10 = (bf16[32,5120]{1,0:T(8,128)(2,1)}, bf16[32,5120]{1,0:T(8,128)(2,1)S(1)}, u32[]{:S(2)}, u32[]{:S(2)}) collective-permute-start(bf16[32,5120]{1,0:T(8,128)(2,1)} %get-tuple-element.71.refs_0_), channel_id=1, source_target_pairs={{0,8},{1,9},{2,10},{3,11},{4,12},{5,13},{6,14},{7,15},{8,0},{9,1},... | collective-permute-start | bytes 983048 | tf_op jit(solution)/shard_map/ppermute | solution.py:34
  183.5 18.6 %collective-permute-start.23 = (bf16[2,32,5120]{2,1,0:T(8,128)(2,1)S(1)}, bf16[2,32,5120]{2,1,0:T(8,128)(2,1)S(1)}, u32[]{:S(2)}, u32[]{:S(2)}) collective-permute-start(bf16[2,32,5120]{2,1,0:T(8,128)(2,1)S(1)} %get-tuple-element.82), channel_id=1, source_target_pairs={{0,4},{1,5},{2,6},{3,7},{4,8},{5,9},{6,10},{7,11},{8,12},{9,13},{1... | collective-permute-start | bytes 1966088 | tf_op jit(solution)/shard_map/ppermute | solution.py:34
  183.5 18.5 %collective-permute-start.24 = (bf16[2,32,5120]{2,1,0:T(8,128)(2,1)S(1)}, bf16[2,32,5120]{2,1,0:T(8,128)(2,1)S(1)}, u32[]{:S(2)}, u32[]{:S(2)}) collective-permute-start(bf16[2,32,5120]{2,1,0:T(8,128)(2,1)S(1)} %get-tuple-element.83), channel_id=1, source_target_pairs={{0,12},{1,13},{2,14},{3,15},{4,0},{5,1},{6,2},{7,3},{8,4},{9,5},{1... | collective-permute-start | bytes 1966088 | tf_op jit(solution)/shard_map/ppermute | solution.py:34
  190.6 45.3 %collective-permute-start.14 = (bf16[256,5120]{1,0:T(8,128)(2,1)S(1)}, bf16[256,5120]{1,0:T(8,128)(2,1)}, u32[]{:S(2)}, u32[]{:S(2)}) collective-permute-start(bf16[256,5120]{1,0:T(8,128)(2,1)S(1)} %get-tuple-element.74.inputs_ref), channel_id=1, source_target_pairs={{0,1},{1,0},{2,3},{3,2},{4,5},{5,4},{6,7},{7,6},{8,9},{9,8},{10,11... | collective-permute-start | bytes 7864328 | tf_op jit(solution)/shard_map/ppermute | solution.py:38
  207.7 28.2 %collective-permute-start.29 = (bf16[1,320,1280]{2,1,0:T(8,128)(2,1)}, bf16[1,320,1280]{2,1,0:T(8,128)(2,1)}, u32[]{:S(2)}, u32[]{:S(2)}) collective-permute-start(bf16[1,320,1280]{2,1,0:T(8,128)(2,1)} %get-tuple-element.88), channel_id=1, source_target_pairs={{0,32},{16,48},{32,64},{48,80},{64,96},{80,112},{96,0},{112,16},{1... | collective-permute-start | bytes 2457608 | tf_op jit(solution)/shard_map/ppermute | solution.py:34
  209.9 26.0 %collective-permute-start.30 = (bf16[1,320,1280]{2,1,0:T(8,128)(2,1)}, bf16[1,320,1280]{2,1,0:T(8,128)(2,1)}, u32[]{:S(2)}, u32[]{:S(2)}) collective-permute-start(bf16[1,320,1280]{2,1,0:T(8,128)(2,1)} %get-tuple-element.89), channel_id=1, source_target_pairs={{0,96},{16,112},{32,0},{48,16},{64,32},{80,48},{96,64},{112,80},{1... | collective-permute-start | bytes 2457608 | tf_op jit(solution)/shard_map/ppermute | solution.py:34
  217.5 15.7 %all-to-all-start.5 = ((bf16[8,64,640]{2,1,0:T(8,128)(2,1)}), bf16[8,64,640]{2,1,0:T(8,128)(2,1)S(1)}, u32[]{:S(2)}, u32[]{:S(2)}) async-start(bf16[8,64,640]{2,1,0:T(8,128)(2,1)} %copy-done.7), calls=%async_computation.5 | async-start | bytes 1310720 | tf_op jit(solution)/shard_map/all_to_all | solution.py:42
  224.4 23.0 %collective-permute-start.35 = (bf16[1,320,1280]{2,1,0:T(8,128)(2,1)}, bf16[1,320,1280]{2,1,0:T(8,128)(2,1)}, u32[]{:S(2)}, u32[]{:S(2)}) collective-permute-start(bf16[1,320,1280]{2,1,0:T(8,128)(2,1)} %copy-done.21), channel_id=1, source_target_pairs={{0,64},{16,80},{32,96},{48,112},{64,0},{80,16},{96,32},{112,48},{1... | collective-permute-start | bytes 2457608 | tf_op jit(solution)/shard_map/ppermute | solution.py:34
  247.4 24.0 %collective-permute-start.33 = (bf16[2,320,640]{2,1,0:T(8,128)(2,1)}, bf16[2,320,640]{2,1,0:T(8,128)(2,1)}, u32[]{:S(2)}, u32[]{:S(2)}) collective-permute-start(bf16[2,320,640]{2,1,0:T(8,128)(2,1)} %get-tuple-element.102), channel_id=1, source_target_pairs={{0,32},{16,48},{32,64},{48,80},{64,96},{80,112},{96,0},{112,16},{1... | collective-permute-start | bytes 2457608 | tf_op jit(solution)/shard_map/ppermute | solution.py:34
  248.5 22.9 %collective-permute-start.34 = (bf16[2,320,640]{2,1,0:T(8,128)(2,1)}, bf16[2,320,640]{2,1,0:T(8,128)(2,1)}, u32[]{:S(2)}, u32[]{:S(2)}) collective-permute-start(bf16[2,320,640]{2,1,0:T(8,128)(2,1)} %get-tuple-element.103), channel_id=1, source_target_pairs={{0,96},{16,112},{32,0},{48,16},{64,32},{80,48},{96,64},{112,80},{1... | collective-permute-start | bytes 2457608 | tf_op jit(solution)/shard_map/ppermute | solution.py:34
  252.7 13.1 %collective-permute-start.36 = (bf16[320,640]{1,0:T(8,128)(2,1)S(1)}, bf16[320,640]{1,0:T(8,128)(2,1)S(1)}, u32[]{:S(2)}, u32[]{:S(2)}) collective-permute-start(bf16[320,640]{1,0:T(8,128)(2,1)S(1)} %select_convert_fusion), channel_id=1, source_target_pairs={{0,16},{16,0},{32,48},{48,32},{64,80},{80,64},{96,112},{112,96},{1... | collective-permute-start | bytes 1228808 | tf_op jit(solution)/shard_map/ppermute | solution.py:34
  258.5 12.9 %collective-permute-start.32 = (bf16[1,320,640]{2,1,0:T(8,128)(2,1)S(1)}, bf16[1,320,640]{2,1,0:T(8,128)(2,1)S(1)}, u32[]{:S(2)}, u32[]{:S(2)}) collective-permute-start(bf16[1,320,640]{2,1,0:T(8,128)(2,1)S(1)} %copy-done.29), channel_id=1, source_target_pairs={{0,16},{16,0},{32,48},{48,32},{64,80},{80,64},{96,112},{112,96},{1... | collective-permute-start | bytes 1228808 | tf_op jit(solution)/shard_map/ppermute | solution.py:34
  (49 other events, 575.3 us)
